TPU v7x, 32 devices: a whole 2x2x4 slice. The times are simulated.
32 devices in a mesh: rng: 4 (over y, x), azi: 8 (over z, core).
Axes of the slice: x: 2, y: 2, z: 4, core: 2. Of those that a mesh axis runs over, the one named last changes fastest.
Arguments:
- observed: float32 [512, 2048], P('rng', 'azi'), may hold values from -6 to 6
- psf_tiles: float32 [4, 16, 121], P('rng', 'azi'), may hold values from 0.002 to 0.02
Outputs:
- estimate: float32 [512, 2048], P('rng', 'azi')
- residual: float32 [512, 2048], P('rng', 'azi')
All inputs are finite; a program needn't handle non-finite values.
Results may differ from a plain program's by a relative error of at most 0.00035.
Values sent between devices are 32-bit elements; how exact they have to be, the bound alone decides.
No kernel may reach another device: no remote copies, remote signals or barrier semaphores. Data moves between devices by JAX's collectives and lax.ppermute only.
A program may use at most 64 MiB of HBM per device.

v0:
```python
import jax
import jax.numpy as jnp
from jax import lax
from jax.sharding import PartitionSpec as P

TILE = 128
KSIZE = 11
ITERS = 2


def passed_along(block, axis, distance):
    devices = range(lax.axis_size(axis))
    route = [(i - distance, i) for i in devices if i - distance in devices]
    return lax.ppermute(block, axis, route)


def padded(block, sides, width):
    for axis, dim in sides:
        count = lax.axis_size(axis)
        forward = [(i, i + 1) for i in range(count - 1)]
        backward = [(target, source) for source, target in forward]
        low = lax.ppermute(
            lax.slice_in_dim(block, block.shape[dim] - width, None, axis=dim), axis, forward
        )
        high = lax.ppermute(lax.slice_in_dim(block, 0, width, axis=dim), axis, backward)
        block = jnp.concatenate([low, block, high], axis=dim)
    return block


def band_matrices(psf_tiles):
    tiles_r, tiles_c = (psf_tiles.shape[0], psf_tiles.shape[1])
    kernels = psf_tiles.reshape(tiles_r, tiles_c, KSIZE, KSIZE)
    span_cols = TILE + KSIZE - 1
    col_idx = lax.broadcasted_iota(jnp.int32, (KSIZE, span_cols, TILE), 1)
    out_idx = lax.broadcasted_iota(jnp.int32, (KSIZE, span_cols, TILE), 2)
    tap_idx = lax.broadcasted_iota(jnp.int32, (KSIZE, span_cols, TILE), 0)
    selector = (col_idx - out_idx == tap_idx).astype(jnp.float32)
    return jnp.einsum("abuv,vcj->uabcj", kernels, selector, precision=lax.Precision.HIGHEST)


def blur_local(field_ext, band_mats):
    radius = (KSIZE - 1) // 2
    tiles_r, tiles_c = (band_mats.shape[1], band_mats.shape[2])
    span_cols = band_mats.shape[3]
    row_count = field_ext.shape[0] - 2 * radius
    windows = jnp.stack(
        [
            field_ext[:, column_tile * TILE : column_tile * TILE + span_cols]
            for column_tile in range(tiles_c)
        ]
    )
    summed = jnp.zeros((tiles_r, TILE, tiles_c, TILE), jnp.float32)
    for offset in range(KSIZE):
        window_rows = windows[:, offset : offset + row_count, :].reshape(
            tiles_c, tiles_r, TILE, span_cols
        )
        summed = summed + jnp.einsum(
            "barc,abcj->arbj", window_rows, band_mats[offset], precision=lax.Precision.HIGHEST
        )
    return summed.reshape(row_count, tiles_c * TILE)


def adjoint_local(field, band_mats):
    radius = (KSIZE - 1) // 2
    tiles_r, tiles_c = (band_mats.shape[1], band_mats.shape[2])
    span_cols = band_mats.shape[3]
    row_count, col_count = field.shape
    shaped = field.reshape(tiles_r, TILE, tiles_c, TILE)
    extended = jnp.zeros((row_count + 2 * radius, col_count + 2 * radius), jnp.float32)
    for offset in range(KSIZE):
        spread = jnp.einsum(
            "arbj,abcj->arbc", shaped, band_mats[offset], precision=lax.Precision.HIGHEST
        )
        for column_tile in range(tiles_c):
            piece = spread[:, :, column_tile, :].reshape(row_count, span_cols)
            extended = extended.at[
                offset : offset + row_count, column_tile * TILE : column_tile * TILE + span_cols
            ].add(piece)
    return extended


def fold_rims(extended):
    radius = (KSIZE - 1) // 2
    top_strip = extended[:radius]
    low_strip = extended[-radius:]
    from_below = passed_along(top_strip, "rng", -1)
    from_above = passed_along(low_strip, "rng", 1)
    inner = extended[radius:-radius]
    inner = inner.at[-radius:].add(from_below).at[:radius].add(from_above)
    left_strip = inner[:, :radius]
    right_strip = inner[:, -radius:]
    from_right = passed_along(left_strip, "azi", -1)
    from_left = passed_along(right_strip, "azi", 1)
    inner = (
        inner.at[:, -2 * radius : -radius].add(from_right).at[:, radius : 2 * radius].add(from_left)
    )
    return inner[:, radius:-radius]


def with_rims(field):
    radius = (KSIZE - 1) // 2
    return padded(field, (("rng", 0), ("azi", 1)), radius)


def gradient_pair(residual, band_mats):
    block = fold_rims(adjoint_local(residual, band_mats))
    return (block, block)


def rimmed(block):
    return with_rims(block)


def grad_norm(gradient):
    return lax.psum(jnp.sum(gradient * gradient), ("rng", "azi"))


def body(observed, psf_tiles):
    band_mats = band_matrices(psf_tiles)
    estimate = jnp.zeros_like(observed)
    residual = observed
    direction = jnp.zeros_like(observed)
    image = jnp.zeros_like(observed)
    gamma = jnp.float32(1.0)
    delta = jnp.float32(0.0)
    for step in range(ITERS):
        gradient, gradient_wide = gradient_pair(residual, band_mats)
        gamma_new = grad_norm(gradient)
        factor = gamma_new / gamma
        direction = gradient + factor * direction
        gamma = gamma_new
        image = blur_local(rimmed(direction), band_mats)
        delta = lax.psum(jnp.sum(image * image), ("rng", "azi"))
        alpha = gamma / delta
        estimate = estimate + alpha * direction
        residual = residual - alpha * image
    return (estimate, residual)


def solution(mesh):
    return jax.shard_map(
        body,
        mesh=mesh,
        in_specs=(P("rng", "azi"), P("rng", "azi", None)),
        out_specs=(P("rng", "azi"), P("rng", "azi")),
        check_vma=False,
    )
```

profile of v0, /device:TPU:0, one launch (start us, length us, event | category | flops | bytes accessed | tf_op | source)
XLA Modules:
  0.0 369.9 jit_solution(5952918168385531505)
XLA Ops:
  7.6 3.0 scatter-add.175
  10.7 2.1 scatter-add.176
  15.1 2.1 scatter-add.180
  19.4 2.1 scatter-add.184
  23.8 2.1 scatter-add.186
  28.1 2.1 scatter-add.190
  32.5 2.1 scatter-add.194
  36.9 2.1 scatter-add.196
  41.2 2.1 scatter-add.200
  55.4 5.5 %collective-permute-start.1 = (f32[5,266]{0,1:T(8,128)S(1)}, f32[5,266]{0,1:T(8,128)S(1)}, u32[]{:S(2)}, u32[]{:S(2)}) collective-permute-start(f32[5,266]{0,1:T(8,128)S(1)} %get-tuple-element.651), channel_id=1, source_target_pairs={{0,8},{8,16},{16,24},{1,9},{9,17},{17,25},{2,10},{10,18},{18,26},{... | collective-permute-start | bytes 15968 | tf_op jit(solution)/shard_map/ppermute | solution.py:14
  67.2 3.0 collective-permute-start.3
  72.5 44.4 %psum.28 = f32[]{:T(128)} all-reduce(f32[]{:T(128)} %multiply_reduce_fusion.3), channel_id=1, replica_groups=mesh['rng'=4,'azi'=8] {'rng','azi'}, use_global_device_ids=true, to_apply=%region_4.0 | all-reduce | flops 1 | bytes 8 | tf_op jit(solution)/shard_map/psum | solution.py:115
  117.7 4.2 %collective-permute-start.4 = (f32[5,256]{0,1:T(8,128)S(1)}, f32[5,256]{0,1:T(8,128)S(1)}, u32[]{:S(2)}, u32[]{:S(2)}) collective-permute-start(f32[5,256]{0,1:T(8,128)S(1)} %get-tuple-element.659), channel_id=1, source_target_pairs={{0,8},{8,16},{16,24},{1,9},{9,17},{17,25},{2,10},{10,18},{18,26},{... | collective-permute-start | bytes 15368 | tf_op jit(solution)/shard_map/ppermute | solution.py:22
  124.4 4.9 %collective-permute-done.5 = f32[5,256]{0,1:T(8,128)S(1)} collective-permute-done((f32[5,256]{0,1:T(8,128)S(1)}, f32[5,256]{0,1:T(8,128)S(1)}, u32[]{:S(2)}, u32[]{:S(2)}) %collective-permute-start.5) | collective-permute-done | bytes 5152 | tf_op jit(solution)/shard_map/ppermute | solution.py:25
  132.0 3.5 collective-permute-done.7
  144.1 42.0 %psum.29 = f32[]{:T(128)} all-reduce(f32[]{:T(128)} %get-tuple-element.663), channel_id=1, replica_groups=mesh['rng'=4,'azi'=8] {'rng','azi'}, use_global_device_ids=true, to_apply=%region_6.0 | all-reduce | flops 1 | bytes 8 | tf_op jit(solution)/shard_map/psum | solution.py:133
  194.6 2.5 scatter-add.219
  240.2 4.8 %collective-permute-start.9 = (f32[5,266]{0,1:T(8,128)S(1)}, f32[5,266]{0,1:T(8,128)S(1)}, u32[]{:S(2)}, u32[]{:S(2)}) collective-permute-start(f32[5,266]{0,1:T(8,128)S(1)} %get-tuple-element.649), channel_id=1, source_target_pairs={{0,8},{8,16},{16,24},{1,9},{9,17},{17,25},{2,10},{10,18},{18,26},{... | collective-permute-start | bytes 15968 | tf_op jit(solution)/shard_map/ppermute | solution.py:14
  249.6 3.0 collective-permute-start.11
  254.9 43.0 %psum.30 = f32[]{:T(128)} all-reduce(f32[]{:T(128)} %multiply_reduce_fusion.2), channel_id=1, replica_groups=mesh['rng'=4,'azi'=8] {'rng','azi'}, use_global_device_ids=true, to_apply=%region_8.0 | all-reduce | flops 1 | bytes 8 | tf_op jit(solution)/shard_map/psum | solution.py:115
  299.4 4.2 %collective-permute-start.12 = (f32[5,256]{0,1:T(8,128)S(1)}, f32[5,256]{0,1:T(8,128)S(1)}, u32[]{:S(2)}, u32[]{:S(2)}) collective-permute-start(f32[5,256]{0,1:T(8,128)S(1)} %get-tuple-element.657), channel_id=1, source_target_pairs={{0,8},{8,16},{16,24},{1,9},{9,17},{17,25},{2,10},{10,18},{18,26},{... | collective-permute-start | bytes 15368 | tf_op jit(solution)/shard_map/ppermute | solution.py:22
  306.2 4.8 %collective-permute-done.13 = f32[5,256]{0,1:T(8,128)S(1)} collective-permute-done((f32[5,256]{0,1:T(8,128)S(1)}, f32[5,256]{0,1:T(8,128)S(1)}, u32[]{:S(2)}, u32[]{:S(2)}) %collective-permute-start.13) | collective-permute-done | bytes 5152 | tf_op jit(solution)/shard_map/ppermute | solution.py:25
  313.7 2.7 collective-permute-done.15
  324.8 41.7 %psum.31 = f32[]{:T(128)} all-reduce(f32[]{:T(128)} %get-tuple-element.665), channel_id=1, replica_groups=mesh['rng'=4,'azi'=8] {'rng','azi'}, use_global_device_ids=true, to_apply=%region_10.0 | all-reduce | flops 1 | bytes 8 | tf_op jit(solution)/shard_map/psum | solution.py:133
  (196 shorter events, 128.8 us)
Async XLA Ops:
  2.4 1.1 copy-start
  2.4 2.1 copy-start.1
  54.1 8.5 %collective-permute-start = (f32[5,266]{0,1:T(8,128)S(1)}, f32[5,266]{0,1:T(8,128)S(1)}, u32[]{:S(2)}, u32[]{:S(2)}) collective-permute-start(f32[5,266]{0,1:T(8,128)S(1)} %get-tuple-element.652), channel_id=1, source_target_pairs={{8,0},{16,8},{24,16},{9,1},{17,9},{25,17},{10,2},{18,10},{26,18},{... | collective-permute-start | bytes 15968 | tf_op jit(solution)/shard_map/ppermute | solution.py:14
  55.4 8.4 %collective-permute-start.1 = (f32[5,266]{0,1:T(8,128)S(1)}, f32[5,266]{0,1:T(8,128)S(1)}, u32[]{:S(2)}, u32[]{:S(2)}) collective-permute-start(f32[5,266]{0,1:T(8,128)S(1)} %get-tuple-element.651), channel_id=1, source_target_pairs={{0,8},{8,16},{16,24},{1,9},{9,17},{17,25},{2,10},{10,18},{18,26},{... | collective-permute-start | bytes 15968 | tf_op jit(solution)/shard_map/ppermute | solution.py:14
  64.5 5.7 %collective-permute-start.2 = (f32[128,5]{0,1:T(8,128)S(1)}, f32[128,5]{0,1:T(8,128)S(1)}, u32[]{:S(2)}, u32[]{:S(2)}) collective-permute-start(f32[128,5]{0,1:T(8,128)S(1)} %get-tuple-element.656), channel_id=1, source_target_pairs={{1,0},{2,1},{3,2},{4,3},{5,4},{6,5},{7,6},{9,8},{10,9},{11,10},{12... | collective-permute-start | bytes 7688 | tf_op jit(solution)/shard_map/ppermute | solution.py:14
  67.2 3.9 %collective-permute-start.3 = (f32[128,5]{0,1:T(8,128)S(1)}, f32[128,5]{0,1:T(8,128)S(1)}, u32[]{:S(2)}, u32[]{:S(2)}) collective-permute-start(f32[128,5]{0,1:T(8,128)S(1)} %get-tuple-element.655), channel_id=1, source_target_pairs={{0,1},{1,2},{2,3},{3,4},{4,5},{5,6},{6,7},{8,9},{9,10},{10,11},{11... | collective-permute-start | bytes 7688 | tf_op jit(solution)/shard_map/ppermute | solution.py:14
  117.7 6.7 %collective-permute-start.4 = (f32[5,256]{0,1:T(8,128)S(1)}, f32[5,256]{0,1:T(8,128)S(1)}, u32[]{:S(2)}, u32[]{:S(2)}) collective-permute-start(f32[5,256]{0,1:T(8,128)S(1)} %get-tuple-element.659), channel_id=1, source_target_pairs={{0,8},{8,16},{16,24},{1,9},{9,17},{17,25},{2,10},{10,18},{18,26},{... | collective-permute-start | bytes 15368 | tf_op jit(solution)/shard_map/ppermute | solution.py:22
  121.9 7.4 %collective-permute-start.5 = (f32[5,256]{0,1:T(8,128)S(1)}, f32[5,256]{0,1:T(8,128)S(1)}, u32[]{:S(2)}, u32[]{:S(2)}) collective-permute-start(f32[5,256]{0,1:T(8,128)S(1)} %get-tuple-element.660), channel_id=1, source_target_pairs={{8,0},{16,8},{24,16},{9,1},{17,9},{25,17},{10,2},{18,10},{26,18},{... | collective-permute-start | bytes 15368 | tf_op jit(solution)/shard_map/ppermute | solution.py:25
  129.4 2.6 collective-permute-start.6
  130.7 4.8 %collective-permute-start.7 = (f32[138,5]{0,1:T(8,128)S(1)}, f32[138,5]{0,1:T(8,128)S(1)}, u32[]{:S(2)}, u32[]{:S(2)}) collective-permute-start(f32[138,5]{0,1:T(8,128)S(1)} %get-tuple-element.647), channel_id=1, source_target_pairs={{1,0},{2,1},{3,2},{4,3},{5,4},{6,5},{7,6},{9,8},{10,9},{11,10},{12... | collective-permute-start | bytes 8288 | tf_op jit(solution)/shard_map/ppermute | solution.py:25
  238.8 7.2 %collective-permute-start.8 = (f32[5,266]{0,1:T(8,128)S(1)}, f32[5,266]{0,1:T(8,128)S(1)}, u32[]{:S(2)}, u32[]{:S(2)}) collective-permute-start(f32[5,266]{0,1:T(8,128)S(1)} %get-tuple-element.650), channel_id=1, source_target_pairs={{8,0},{16,8},{24,16},{9,1},{17,9},{25,17},{10,2},{18,10},{26,18},{... | collective-permute-start | bytes 15968 | tf_op jit(solution)/shard_map/ppermute | solution.py:14
  240.2 7.4 %collective-permute-start.9 = (f32[5,266]{0,1:T(8,128)S(1)}, f32[5,266]{0,1:T(8,128)S(1)}, u32[]{:S(2)}, u32[]{:S(2)}) collective-permute-start(f32[5,266]{0,1:T(8,128)S(1)} %get-tuple-element.649), channel_id=1, source_target_pairs={{0,8},{8,16},{16,24},{1,9},{9,17},{17,25},{2,10},{10,18},{18,26},{... | collective-permute-start | bytes 15968 | tf_op jit(solution)/shard_map/ppermute | solution.py:14
  248.3 4.3 %collective-permute-start.10 = (f32[128,5]{0,1:T(8,128)S(1)}, f32[128,5]{0,1:T(8,128)S(1)}, u32[]{:S(2)}, u32[]{:S(2)}) collective-permute-start(f32[128,5]{0,1:T(8,128)S(1)} %get-tuple-element.654), channel_id=1, source_target_pairs={{1,0},{2,1},{3,2},{4,3},{5,4},{6,5},{7,6},{9,8},{10,9},{11,10},{12... | collective-permute-start | bytes 7688 | tf_op jit(solution)/shard_map/ppermute | solution.py:14
  249.6 3.9 %collective-permute-start.11 = (f32[128,5]{0,1:T(8,128)S(1)}, f32[128,5]{0,1:T(8,128)S(1)}, u32[]{:S(2)}, u32[]{:S(2)}) collective-permute-start(f32[128,5]{0,1:T(8,128)S(1)} %get-tuple-element.653), channel_id=1, source_target_pairs={{0,1},{1,2},{2,3},{3,4},{4,5},{5,6},{6,7},{8,9},{9,10},{10,11},{11... | collective-permute-start | bytes 7688 | tf_op jit(solution)/shard_map/ppermute | solution.py:14
  299.4 6.8 %collective-permute-start.12 = (f32[5,256]{0,1:T(8,128)S(1)}, f32[5,256]{0,1:T(8,128)S(1)}, u32[]{:S(2)}, u32[]{:S(2)}) collective-permute-start(f32[5,256]{0,1:T(8,128)S(1)} %get-tuple-element.657), channel_id=1, source_target_pairs={{0,8},{8,16},{16,24},{1,9},{9,17},{17,25},{2,10},{10,18},{18,26},{... | collective-permute-start | bytes 15368 | tf_op jit(solution)/shard_map/ppermute | solution.py:22
  303.6 7.4 %collective-permute-start.13 = (f32[5,256]{0,1:T(8,128)S(1)}, f32[5,256]{0,1:T(8,128)S(1)}, u32[]{:S(2)}, u32[]{:S(2)}) collective-permute-start(f32[5,256]{0,1:T(8,128)S(1)} %get-tuple-element.658), channel_id=1, source_target_pairs={{8,0},{16,8},{24,16},{9,1},{17,9},{25,17},{10,2},{18,10},{26,18},{... | collective-permute-start | bytes 15368 | tf_op jit(solution)/shard_map/ppermute | solution.py:25
  311.1 2.6 collective-permute-start.14
  312.3 4.0 %collective-permute-start.15 = (f32[138,5]{0,1:T(8,128)S(1)}, f32[138,5]{0,1:T(8,128)S(1)}, u32[]{:S(2)}, u32[]{:S(2)}) collective-permute-start(f32[138,5]{0,1:T(8,128)S(1)} %get-tuple-element.643), channel_id=1, source_target_pairs={{1,0},{2,1},{3,2},{4,3},{5,4},{6,5},{7,6},{9,8},{10,9},{11,10},{12... | collective-permute-start | bytes 8288 | tf_op jit(solution)/shard_map/ppermute | solution.py:25
where the time goes:
time: 374 us; the launch traced here: 370 us
  blocking collectives  171 us (46%)
  local copies, waits for them, and re-layouts  88.8 us (24%)
  starting transfers between devices  37.6 us (10%)
  matrix products  27.1 us (7%)
  waiting for transfers between devices  21.8 us (6%)
  other arithmetic  16.6 us (4%)
  between operations  6.8 us (2%)
    psum x2, blocking collectives, grad_norm(): return lax.psum(jnp.sum(gradient * gradient), ('rng', 'azi'))  87.4 us
    psum x2, blocking collectives, body(): delta = lax.psum(jnp.sum(image * image), ('rng', 'azi'))  83.7 us
    scatter-add x44, local copies, waits for them, and re-layouts, adjoint_local(): extended = extended.at[offset:offset + row_count, column_tile * TILE:colu...  81.2 us
    ppermute x8, starting transfers between devices, passed_along(): return lax.ppermute(block, axis, route)  21.5 us
    dot_general x22, matrix products, blur_local(): jnp.einsum('barc,abcj->arbj', window_rows, band_mats[offset], precision=l...  16.7 us
    ppermute x4, waiting for transfers between devices, padded(): lax.ppermute(lax.slice_in_dim(block, 0, width, axis=dim), axis, backward)  15.9 us
    ppermute x4, starting transfers between devices, padded(): lax.ppermute(lax.slice_in_dim(block, block.shape[dim] - width, None, axis...  10.9 us
    dot_general x22, matrix products, adjoint_local(): jnp.einsum('arbj,abcj->arbc', shaped, band_mats[offset], precision=lax.Pr...  9.35 us
  transfers between devices with their start and end apart: 16, of which 10 were waited for; matrix products, arithmetic and copies ran while one was open for 1% of the time, Pallas kernels for 0%

commit v1 on v0

v1 whole, which is shorter than its diff:
```python
import jax
import jax.numpy as jnp
from jax import lax
from jax.experimental import pallas as pl
from jax.experimental.pallas import tpu as pltpu
from jax.sharding import PartitionSpec as P

TILE = 128
KSIZE = 11
RADIUS = 5
TAPS = KSIZE * KSIZE
LANES = 128
HALO = 24
REACH = 20
WINDOWS = 3
ROWS = TILE + 2 * HALO
SLOTS = (KSIZE + 1) // 2
DEPTH = SLOTS * LANES
MAIN = 144
REGIONS = ((0, 1, 24), (1, 2, 64), (2, 3, 104))
VMEM = pl.BlockSpec(memory_space=pltpu.VMEM)


def call(kernel, out_shape, scratch=(), limit=4):
    single = isinstance(out_shape, jax.ShapeDtypeStruct)
    return pl.pallas_call(
        kernel,
        out_shape=out_shape,
        out_specs=VMEM if single else [VMEM] * len(out_shape),
        scratch_shapes=list(scratch),
        compiler_params=pltpu.CompilerParams(vmem_limit_bytes=limit * 2**20),
    )


def f32(*shape):
    return jax.ShapeDtypeStruct(shape, jnp.float32)


def lanes_of(shape):
    return lax.broadcasted_iota(jnp.int32, shape, len(shape) - 1)


def is_odd(axis):
    return lax.axis_index(axis) % 2 == 1


def columns_kernel(block_ref, psf_ref, near_ref, far_ref):
    lane = lanes_of((32, LANES))

    def packed(half, first):
        out = jnp.zeros((32, LANES), jnp.float32)
        for part in range(4):
            rows = block_ref[32 * part : 32 * part + 32, LANES * half : LANES * half + LANES]
            moved = pltpu.roll(rows, (32 * part - first) % LANES, 1)
            out = jnp.where((lane >= 32 * part) & (lane < 32 * part + HALO), moved, out)
        return out

    left, right = packed(0, 0), packed(1, LANES - HALO)
    odd = is_odd("azi")
    near_ref[:32] = jnp.where(odd, left, right)
    far_ref[:32] = jnp.where(odd, right, left)
    near_ref[32:] = jnp.zeros((8, LANES), jnp.float32)
    far_ref[32:] = jnp.zeros((8, LANES), jnp.float32)
    near_ref[32:33, :TAPS] = jnp.where(odd, psf_ref[0:1], psf_ref[1:2])
    far_ref[32:33, :TAPS] = jnp.where(odd, psf_ref[1:2], psf_ref[0:1])


def rows_kernel(block_ref, psf_ref, near_ref, far_ref, wide_ref, taps_ref, one_ref, two_ref, top, low):
    odd = is_odd("azi")
    lane = lanes_of((32, LANES))
    near, far = near_ref[:32], far_ref[:32]
    left = jnp.where(odd, near, far)
    right = jnp.where(odd, far, near)
    for part in range(4):
        rows = slice(32 * part, 32 * part + 32)
        first = block_ref[rows, :LANES]
        second = block_ref[rows, LANES:]
        halo_left = pltpu.roll(left, (-32 * part) % LANES, 1)
        halo_right = pltpu.roll(right, (LANES - HALO - 32 * part) % LANES, 1)
        wide_ref[rows, :LANES] = jnp.where(lane < HALO, halo_left, pltpu.roll(first, HALO, 1))
        wide_ref[rows, LANES : 2 * LANES] = jnp.where(
            lane < 64, pltpu.roll(first, 64, 1), pltpu.roll(second, 64, 1)
        )
        wide_ref[rows, 2 * LANES :] = jnp.where(
            lane < LANES - HALO, pltpu.roll(second, LANES - HALO, 1), halo_right
        )
    taps_ref[...] = jnp.zeros((8, LANES), jnp.float32)
    near_taps, far_taps = near_ref[32:33], far_ref[32:33]
    taps_ref[0:1] = jnp.where(odd, near_taps, far_taps)
    taps_ref[1:3, :TAPS] = psf_ref[...]
    taps_ref[3:4] = jnp.where(odd, far_taps, near_taps)
    top[...] = wide_ref[:HALO]
    low[...] = wide_ref[TILE - HALO :]
    top[REACH:, :LANES] = taps_ref[0:4]
    low[: HALO - REACH, :LANES] = taps_ref[0:4]
    odd_row = is_odd("rng")
    one_ref[...] = jnp.where(odd_row, top[...], low[...])
    two_ref[...] = jnp.where(odd_row, low[...], top[...])


def split(value):
    high = value.astype(jnp.bfloat16)
    return high, (value - high.astype(jnp.float32)).astype(jnp.bfloat16)


def product(parts, high, low, dims):
    rows = parts[0].shape[0]

    def dot(a, b):
        return lax.dot_general(a, b, (dims, ((), ())), preferred_element_type=jnp.float32)

    both = dot(jnp.concatenate(parts, axis=0), high)
    return both[:rows] + both[rows:] + dot(parts[0], low)


def shifted(load, offsets):
    pieces = [split(load(offset)) for offset in offsets]
    return [jnp.concatenate([piece[part] for piece in pieces], axis=1) for part in range(2)]


def adjoint_main(padded_ref, window, high_ref, low_ref, pair_ref):
    cols = pl.ds(window * LANES, LANES)
    offsets = [RADIUS - 2 * slot for slot in range(SLOTS)]
    parts = shifted(lambda o: padded_ref[pl.ds(8 + o, MAIN), cols], offsets)
    both = product(parts, high_ref[window], low_ref[window], ((1,), (0,)))
    pair_ref[8:, :] = both[:, LANES:]
    return both[:, :LANES] + pair_ref[pl.ds(7, MAIN), :]


def forward_main(field_ref, window, high_ref, low_ref, pair_ref):
    cols = pl.ds(window * LANES, LANES)
    offsets = [2 * slot - RADIUS for slot in range(SLOTS)]
    parts = shifted(lambda o: field_ref[pl.ds(HALO + o, MAIN), cols], offsets)

    def turned(ref):
        return jnp.concatenate(
            [
                jnp.concatenate(
                    [ref[window, s * LANES : (s + 1) * LANES, e * LANES : (e + 1) * LANES] for s in range(SLOTS)],
                    axis=1,
                )
                for e in range(2)
            ],
            axis=0,
        )

    both = product(parts, turned(high_ref), turned(low_ref), ((1,), (1,)))
    pair_ref[:MAIN, :] = both[:, LANES:]
    return both[:TILE, :LANES] + pair_ref[pl.ds(1, TILE), :]


def start_kernel(wide_ref, taps_ref, high_ref, low_ref, main_ref, padded, pair):
    row = lax.broadcasted_iota(jnp.int32, (LANES, LANES), 0)
    lane8 = lanes_of((8, LANES))
    taps = taps_ref[...]
    for offset in range(2 * SLOTS):
        slot, half = offset // 2, offset % 2
        place = (slice(slot * LANES, (slot + 1) * LANES), slice(half * LANES, (half + 1) * LANES))
        if offset >= KSIZE:
            for window in range(WINDOWS):
                high_ref[(window, *place)] = jnp.zeros((LANES, LANES), jnp.bfloat16)
                low_ref[(window, *place)] = jnp.zeros((LANES, LANES), jnp.bfloat16)
            continue
        line = pltpu.roll(taps, (-KSIZE * offset) % LANES, 1)
        line = pltpu.roll(jnp.where(lane8 < KSIZE, line, 0.0), LANES - RADIUS, 1)
        for window, (before, after, bound) in enumerate(REGIONS):
            base = jnp.where(
                row < bound,
                jnp.broadcast_to(line[before : before + 1], (LANES, LANES)),
                jnp.broadcast_to(line[after : after + 1], (LANES, LANES)),
            )
            band = pltpu.roll(base, 0, 1, stride=1, stride_axis=0)
            high, low = split(band)
            high_ref[(window, *place)] = high
            low_ref[(window, *place)] = low
    padded[:16] = jnp.zeros((16, WINDOWS * LANES), jnp.float32)
    padded[16 + TILE :] = jnp.zeros((16, WINDOWS * LANES), jnp.float32)
    padded[16 : 16 + TILE] = wide_ref[...]
    pair[:8] = jnp.zeros((8, LANES), jnp.float32)
    for window in range(WINDOWS):
        main_ref[:, window * LANES : (window + 1) * LANES] = adjoint_main(
            padded, window, high_ref, low_ref, pair
        )


def strip(load, table, band, window, sign):
    sums = [None] * KSIZE
    for u in range(KSIZE):
        rows = load(u)
        for v in range(KSIZE):
            term = table[band, window, pl.ds(u * KSIZE + v, 1), :] * rows
            sums[v] = term if u == 0 else sums[v] + term
    total = sums[RADIUS]
    for v in range(KSIZE):
        if v != RADIUS:
            total = total + pltpu.roll(sums[v], (sign * (v - RADIUS)) % LANES, 1)
    return total


def finish_kernel(
    wide_ref,
    high_ref,
    low_ref,
    main_ref,
    one_ref,
    two_ref,
    grad_ref,
    image_ref,
    grad2_ref,
    image2_ref,
    record_ref,
    gather_table,
    spread_table,
    edges,
    field,
    padded,
    pair,
):
    odd_row = is_odd("rng")
    one, two = one_ref[...], two_ref[...]
    above = jnp.where(odd_row, one, two)
    below = jnp.where(odd_row, two, one)
    zero = jnp.zeros((1, 1), jnp.float32)
    row24 = lax.broadcasted_iota(jnp.int32, (HALO, 1), 0)
    wide = WINDOWS * LANES
    lane = lanes_of((1, LANES))

    tap_row = lax.broadcasted_iota(jnp.int32, (LANES, LANES), 0)
    tap_lane = lanes_of((LANES, LANES))
    reach = tap_lane - (tap_row % KSIZE - RADIUS)
    for band, taps in enumerate((above[:8, :LANES], below[REACH - 4 :, :LANES])):
        columns = jnp.transpose(taps)
        skip = 0 if band == 0 else 4
        filled = [
            jnp.broadcast_to(columns[:, skip + tile : skip + tile + 1], (LANES, LANES)) for tile in range(4)
        ]
        for window, (before, after, bound) in enumerate(REGIONS):
            spread_table[band, window] = jnp.where(tap_lane < bound, filled[before], filled[after])
            gather_table[band, window] = jnp.where(reach < bound, filled[before], filled[after])

    has_left = lax.axis_index("azi") > 0
    has_right = lax.axis_index("azi") < lax.axis_size("azi") - 1
    has_above = lax.axis_index("rng") > 0
    has_below = lax.axis_index("rng") < lax.axis_size("rng") - 1
    inside = [
        (lane >= HALO) | has_left,
        lane >= 0,
        (lane < LANES - HALO) | has_right,
    ]

    edges[...] = jnp.zeros((2, 40, wide), jnp.float32)
    edges[0, :HALO] = jnp.where(row24 < HALO - REACH, 0.0, above)
    edges[1, 16:] = jnp.where(row24 >= REACH, 0.0, below)
    field[:16] = jnp.zeros((16, wide), jnp.float32)
    field[ROWS - 16 :] = jnp.zeros((16, wide), jnp.float32)
    padded[:16] = jnp.zeros((16, wide), jnp.float32)
    padded[16 + TILE :] = jnp.zeros((16, wide), jnp.float32)
    pair[:8] = jnp.zeros((8, LANES), jnp.float32)

    def cols(window):
        return pl.ds(window * LANES, LANES)

    def put_field(main, window, first, count):
        up = strip(
            lambda u: edges[0, pl.ds(first + 29 - u, count), cols(window)], spread_table, 0, window, 1
        )
        down = strip(lambda u: edges[1, pl.ds(13 - u, count), cols(window)], spread_table, 1, window, 1)
        up_main = main[:16]
        if first < -8:
            up_main = jnp.concatenate([jnp.zeros((-8 - first, LANES), jnp.float32), up_main], axis=0)
        down_main = main[128:]
        if count > 16:
            down_main = jnp.concatenate([down_main, jnp.zeros((count - 16, LANES), jnp.float32)], axis=0)
        up = up + up_main
        down = down + down_main
        keep = inside[window]
        outer = -first
        up_keep = keep & (has_above | (lax.broadcasted_iota(jnp.int32, (count, LANES), 0) >= outer))
        down_keep = keep & (has_below | (lax.broadcasted_iota(jnp.int32, (count, LANES), 0) < 8))
        field[pl.ds(HALO + first, count), cols(window)] = jnp.where(up_keep, up, 0.0)
        field[32:144, cols(window)] = jnp.where(keep, main[16:128], 0.0)
        field[pl.ds(144, count), cols(window)] = jnp.where(down_keep, down, 0.0)

    for window in range(WINDOWS):
        put_field(main_ref[:, window * LANES : (window + 1) * LANES], window, -16, 24)
    grad_ref[...] = field[HALO : HALO + TILE]

    for window in range(WINDOWS):
        image = forward_main(field, window, high_ref, low_ref, pair)
        up = strip(lambda u: field[pl.ds(3 + u, 16), cols(window)], gather_table, 0, window, -1)
        down = strip(lambda u: field[pl.ds(147 + u, 16), cols(window)], gather_table, 1, window, -1)
        padded[16 : 16 + TILE, cols(window)] = image
        edges[0, 8:24, cols(window)] = up
        edges[1, 16:32, cols(window)] = down
    edges[0, :8] = jnp.zeros((8, wide), jnp.float32)
    edges[1, 32:] = jnp.zeros((8, wide), jnp.float32)
    image_ref[...] = padded[16 : 16 + TILE]

    pair[:8] = jnp.zeros((8, LANES), jnp.float32)
    for window in range(WINDOWS):
        main = adjoint_main(padded, window, high_ref, low_ref, pair)
        put_field(main, window, -8, 16)
    grad2_ref[...] = field[HALO : HALO + TILE]

    for window in range(WINDOWS):
        image2_ref[:, window * LANES : (window + 1) * LANES] = forward_main(
            field, window, high_ref, low_ref, pair
        )

    bounds = ((24, 108), (20, 108), (20, 104))
    own = jnp.concatenate([(lane >= low) & (lane < high) for low, high in bounds], axis=1)

    def total(value):
        return jnp.sum(jnp.where(own, jnp.sum(value, axis=0, keepdims=True), 0.0), axis=1, keepdims=True)

    def best(first, second):
        size = total(second * second)
        cross = total(first * second)
        ratio = jnp.where(size > 0.0, cross / jnp.where(size > 0.0, size, 1.0), 0.0)
        rest = first - ratio * second
        return total(first * first), size, ratio, total(rest * rest)

    record = best(grad_ref[...], grad2_ref[...]) + best(image_ref[...], image2_ref[...])
    line = jnp.zeros((1, LANES), jnp.float32)
    for position, value in enumerate(record):
        line = jnp.where(lane == position, value, line)
    record_ref[...] = jnp.broadcast_to(line[None], record_ref.shape)


def combine_kernel(records_ref, block_ref, grad_ref, image_ref, grad2_ref, image2_ref, estimate_ref, residual_ref):
    records = records_ref[:, 0, :]

    def item(position):
        return records[:, position : position + 1]

    def total(value):
        return jnp.sum(value, axis=0, keepdims=True)

    gamma = total(item(0))
    delta = total(item(4))
    alpha = gamma / delta
    gamma_new = total(item(3) + (alpha - item(2)) ** 2 * item(1))
    bent = total(item(7) + (alpha - item(6)) ** 2 * item(5))
    factor = gamma_new / gamma
    delta_new = bent - factor * factor * delta
    alpha_new = gamma_new / delta_new
    first = alpha + alpha_new * (1.0 + factor)
    second = -alpha_new * alpha
    lane = lanes_of((TILE, LANES))

    def own(a_ref, b_ref):
        parts = [
            first * a_ref[:, w * LANES : (w + 1) * LANES] + second * b_ref[:, w * LANES : (w + 1) * LANES]
            for w in range(WINDOWS)
        ]
        middle = pltpu.roll(parts[1], 64, 1)
        left = jnp.where(lane < 84, pltpu.roll(parts[0], LANES - HALO, 1), middle)
        right = jnp.where(lane < 44, middle, pltpu.roll(parts[2], HALO, 1))
        return left, right

    left, right = own(grad_ref, grad2_ref)
    estimate_ref[:, :LANES] = left
    estimate_ref[:, LANES:] = right
    left, right = own(image_ref, image2_ref)
    residual_ref[:, :LANES] = block_ref[:, :LANES] - left
    residual_ref[:, LANES:] = block_ref[:, LANES:] - right


def neighbours(axis):
    count = lax.axis_size(axis)
    near = [(i, i + 1) for i in range(0, count - 1, 2)]
    far = [(i, i + 1) for i in range(1, count - 1, 2)]
    return [pairs + [(b, a) for a, b in pairs] for pairs in (near, far)]


def body(observed, psf_tiles):
    psf = psf_tiles.reshape(2, TAPS)
    devices = lax.axis_size("rng") * lax.axis_size("azi")
    wide = WINDOWS * LANES
    near, far = call(columns_kernel, [f32(40, LANES), f32(40, LANES)])(observed, psf)
    near_pairs, far_pairs = neighbours("azi")
    near = lax.ppermute(near, "azi", near_pairs)
    far = lax.ppermute(far, "azi", far_pairs)
    block, taps, one, two = call(
        rows_kernel,
        [f32(TILE, wide), f32(8, LANES), f32(HALO, wide), f32(HALO, wide)],
        [pltpu.VMEM((HALO, wide), jnp.float32)] * 2,
    )(observed, psf, near, far)
    one_pairs, two_pairs = neighbours("rng")
    one = lax.ppermute(one, "rng", one_pairs)
    two = lax.ppermute(two, "rng", two_pairs)
    matrix = jax.ShapeDtypeStruct((WINDOWS, DEPTH, 2 * LANES), jnp.bfloat16)
    high, low, main = call(
        start_kernel,
        [matrix, matrix, f32(MAIN, wide)],
        [pltpu.VMEM((160, wide), jnp.float32), pltpu.VMEM((152, LANES), jnp.float32)],
        limit=8,
    )(block, taps)
    table = pltpu.VMEM((2, WINDOWS, LANES, LANES), jnp.float32)
    grad, image, grad2, image2, record = call(
        finish_kernel,
        [f32(TILE, wide)] * 4 + [f32(devices, 1, LANES)],
        [
            table,
            table,
            pltpu.VMEM((2, 40, wide), jnp.float32),
            pltpu.VMEM((ROWS, wide), jnp.float32),
            pltpu.VMEM((160, wide), jnp.float32),
            pltpu.VMEM((152, LANES), jnp.float32),
        ],
        limit=12,
    )(block, high, low, main, one, two)
    records = lax.all_to_all(record, ("rng", "azi"), 0, 0, tiled=True)
    estimate, residual = call(combine_kernel, [f32(TILE, 2 * LANES)] * 2)(
        records, observed, grad, image, grad2, image2
    )
    return estimate, residual


def solution(mesh):
    return jax.shard_map(
        body,
        mesh=mesh,
        in_specs=(P("rng", "azi"), P("rng", "azi", None)),
        out_specs=(P("rng", "azi"), P("rng", "azi")),
        check_vma=False,
    )
```

time: 374 us -> 36.7 us (0.10); the launches traced: 370 us -> 36.5 us
  blocking collectives: 171 us -> 20.4 us
  local copies, waits for them, and re-layouts: 88.8 us -> 1.58 us
  starting transfers between devices: 37.6 us -> 4.72 us
  matrix products: 27.1 us -> 0 us
  waiting for transfers between devices: 21.8 us -> 0.19 us
  other arithmetic: 16.6 us -> 0 us
  Pallas kernels: 0 us -> 8.92 us
  between operations: 6.8 us -> 0.7 us
    psum x4 -> x0, blocking collectives: 171 us -> none  [the longest x2 87.4 us: grad_norm(): return lax.psum(jnp.sum(gradient * gradient), ('rng', 'azi'))]
    scatter-add x52 -> x0, local copies, waits for them, and re-layouts: 84.9 us -> none  [the longest x44 81.2 us: adjoint_local(): extended = extended.at[offset:offset + row_count, column_tile * TILE:colu...]
    ppermute x16 -> x4, starting transfers between devices: 37.6 us -> 4.72 us  [the longest x1 2.9 us: body(): one = lax.ppermute(one, 'rng', one_pairs)]
    dot_general x45 -> x0, matrix products: 27.1 us -> none  [the longest x22 16.7 us: blur_local(): jnp.einsum('barc,abcj->arbj', window_rows, band_mats[offset], precision=l...]
    ppermute x16 -> x4, waiting for transfers between devices: 21.8 us -> 0.19 us  [the longest x1 0.19 us: body(): near = lax.ppermute(near, 'azi', near_pairs)]
    all_to_all x0 -> x1, blocking collectives: none -> 20.4 us  [body(): records = lax.all_to_all(record, ('rng', 'azi'), 0, 0, tiled=True)]
    another operation x12 -> x0, other arithmetic: 9.12 us -> none
    pallas_call x0 -> x5, Pallas kernels: none -> 8.92 us  [the longest x1 6.25 us: body(): call(finish_kernel, [f32(TILE, wide)] * 4 + [f32(devices, 1, LANES)], [ta...]
  transfers between devices with their start and end apart: 16 -> 4, of which waited for: 10 -> 1; matrix products, arithmetic and copies ran while one was open for 1% -> 0% of each run, Pallas kernels for 0% -> 4%
where the time goes in v1:
time: 36.7 us; the launch traced here: 36.5 us
  blocking collectives  20.4 us (56%)
  Pallas kernels  8.92 us (24%)
  starting transfers between devices  4.72 us (13%)
  local copies, waits for them, and re-layouts  1.58 us (4%)
  between operations  0.7 us (2%)
    all_to_all x1, blocking collectives, body(): records = lax.all_to_all(record, ('rng', 'azi'), 0, 0, tiled=True)  20.4 us
    pallas_call x1, Pallas kernels, body(): call(finish_kernel, [f32(TILE, wide)] * 4 + [f32(devices, 1, LANES)], [ta...  6.25 us
    ppermute x1, starting transfers between devices, body(): one = lax.ppermute(one, 'rng', one_pairs)  2.9 us
    unnamed x6, local copies, waits for them, and re-layouts  1.58 us
    pallas_call x1, Pallas kernels, body(): call(start_kernel, [matrix, matrix, f32(MAIN, wide)], [pltpu.VMEM((160, w...  1.43 us
    pallas_call x1, Pallas kernels, body(): call(combine_kernel, [f32(TILE, 2 * LANES)] * 2)  0.99 us
  transfers between devices with their start and end apart: 4, of which 1 were waited for; matrix products, arithmetic and copies ran while one was open for 0% of the time, Pallas kernels for 4%

profile of v1, /device:TPU:0, one launch (start us, length us, event | category | flops | bytes accessed | tf_op | source)
XLA Modules:
  0.0 36.5 jit_solution(3563702400568156979)
XLA Ops:
  0.6 0.0 copy-start
  0.6 0.9 %copy-done = f32[128,256]{1,0:T(8,128)S(1)} copy-done((f32[128,256]{1,0:T(8,128)S(1)}, f32[128,256]{1,0:T(8,128)}, u32[]{:S(2)}) %copy-start) | copy-done | bytes 131096
  1.5 0.0 copy-start.2
  1.5 0.7 %copy-done.2 = f32[1,2,121]{2,1,0:T(2,128)S(1)} copy-done((f32[1,2,121]{2,1,0:T(2,128)S(1)}, f32[1,2,121]{2,1,0:T(2,128)}, u32[]{:S(2)}) %copy-start.2) | copy-done | bytes 992
  2.2 0.1 shard_map.41
  2.3 0.5 %collective-permute-start = (f32[40,128]{1,0:T(8,128)S(1)}, f32[40,128]{1,0:T(8,128)S(1)}, u32[]{:S(2)}, u32[]{:S(2)}) collective-permute-start(f32[40,128]{1,0:T(8,128)S(1)} %get-tuple-element.16), channel_id=1, source_target_pairs={{0,1},{2,3},{4,5},{6,7},{1,0},{3,2},{5,4},{7,6},{8,9},{10,11},{12,... | collective-permute-start | bytes 61448 | tf_op jit(solution)/shard_map/ppermute | solution.py:382
  2.8 0.7 %collective-permute-start.1 = (f32[40,128]{1,0:T(8,128)S(1)}, f32[40,128]{1,0:T(8,128)S(1)}, u32[]{:S(2)}, u32[]{:S(2)}) collective-permute-start(f32[40,128]{1,0:T(8,128)S(1)} %get-tuple-element.17), channel_id=1, source_target_pairs={{1,2},{3,4},{5,6},{2,1},{4,3},{6,5},{9,10},{11,12},{13,14},{10,9},... | collective-permute-start | bytes 61448 | tf_op jit(solution)/shard_map/ppermute | solution.py:383
  3.5 0.2 collective-permute-done.near_ref
  3.7 0.0 collective-permute-done.1.far_ref
  3.7 0.2 shard_map.42
  3.9 2.9 %collective-permute-start.2 = (f32[24,384]{1,0:T(8,128)S(1)}, f32[24,384]{1,0:T(8,128)S(1)}, u32[]{:S(2)}, u32[]{:S(2)}) collective-permute-start(f32[24,384]{1,0:T(8,128)S(1)} %get-tuple-element.23), channel_id=1, source_target_pairs={{0,8},{16,24},{8,0},{24,16},{1,9},{17,25},{9,1},{25,17},{2,10},{18... | collective-permute-start | bytes 110600 | tf_op jit(solution)/shard_map/ppermute | solution.py:390
  6.7 0.7 %collective-permute-start.3 = (f32[24,384]{1,0:T(8,128)S(1)}, f32[24,384]{1,0:T(8,128)S(1)}, u32[]{:S(2)}, u32[]{:S(2)}) collective-permute-start(f32[24,384]{1,0:T(8,128)S(1)} %get-tuple-element.24), channel_id=1, source_target_pairs={{8,16},{16,8},{9,17},{17,9},{10,18},{18,10},{11,19},{19,11},{12,20... | collective-permute-start | bytes 110600 | tf_op jit(solution)/shard_map/ppermute | solution.py:391
  7.4 1.4 %shard_map.43 = (bf16[3,768,256]{2,1,0:T(8,128)(2,1)S(1)}, bf16[3,768,256]{2,1,0:T(8,128)(2,1)S(1)}, f32[144,384]{1,0:T(8,128)S(1)}) custom-call(f32[128,384]{1,0:T(8,128)S(1)} %get-tuple-element.18.wide_ref, f32[8,128]{1,0:T(8,128)S(1)} %get-tuple-element.19.taps_ref), custom_call_target="tpu_custom_call" | custom-call | tf_op jit(solution)/shard_map/pallas_call | solution.py:393
  8.8 0.0 collective-permute-done.2.one_ref
  8.9 0.0 collective-permute-done.3.two_ref
  8.9 0.0 copy-start.1
  8.9 6.2 %shard_map.44 = (f32[128,384]{1,0:T(8,128)S(1)}, f32[128,384]{1,0:T(8,128)S(1)}, f32[128,384]{1,0:T(8,128)S(1)}, f32[128,384]{1,0:T(8,128)S(1)}, f32[32,1,128]{2,1,0:T(1,128)S(1)}) custom-call(f32[128,384]{1,0:T(8,128)S(1)} %get-tuple-element.18.wide_ref, bf16[3,768,256]{2,1,0:T(8,128)(2,1)S(1)} %get-tuple-element.20.high_ref, ...), custom_call_target="tpu_custom_call" | custom-call | tf_op jit(solution)/shard_map/pallas_call | solution.py:400
  15.1 20.4 %all_to_all.5.records_ref = f32[32,1,128]{2,1,0:T(1,128)S(1)} all-to-all(f32[32,1,128]{2,1,0:T(1,128)S(1)} %get-tuple-element.25), channel_id=1, replica_groups=mesh['rng'=4,'azi'=8] {'rng','azi'}, dimensions={0} | all-to-all | bytes 32768 | tf_op jit(solution)/shard_map/all_to_all | solution.py:413
  35.5 0.0 copy-done.1
  35.5 1.0 %shard_map.45 = (f32[128,256]{1,0:T(8,128)}, f32[128,256]{1,0:T(8,128)}) custom-call(f32[32,1,128]{2,1,0:T(1,128)S(1)} %all_to_all.5.records_ref, f32[128,256]{1,0:T(8,128)S(1)} %copy-done.1, f32[128,384]{1,0:T(8,128)S(1)} %get-tuple-element.26.grad_ref, f32[128,384]{1,0:T(8,128)S(1)} %get-tuple-element.27.image_ref, ...), custom_call_target="tpu_custom_call" | custom-call | tf_op jit(solution)/shard_map/pallas_call | solution.py:414
Async XLA Ops:
  0.6 0.9 %copy-start = (f32[128,256]{1,0:T(8,128)S(1)}, f32[128,256]{1,0:T(8,128)}, u32[]{:S(2)}) copy-start(f32[128,256]{1,0:T(8,128)} %block_ref.5) | copy-start | bytes 393220
  1.5 0.7 %copy-start.2 = (f32[1,2,121]{2,1,0:T(2,128)S(1)}, f32[1,2,121]{2,1,0:T(2,128)}, u32[]{:S(2)}) copy-start(f32[1,2,121]{2,1,0:T(2,128)} %param.3) | copy-start | bytes 2908
  2.3 1.4 %collective-permute-start = (f32[40,128]{1,0:T(8,128)S(1)}, f32[40,128]{1,0:T(8,128)S(1)}, u32[]{:S(2)}, u32[]{:S(2)}) collective-permute-start(f32[40,128]{1,0:T(8,128)S(1)} %get-tuple-element.16), channel_id=1, source_target_pairs={{0,1},{2,3},{4,5},{6,7},{1,0},{3,2},{5,4},{7,6},{8,9},{10,11},{12,... | collective-permute-start | bytes 61448 | tf_op jit(solution)/shard_map/ppermute | solution.py:382
  2.8 0.8 %collective-permute-start.1 = (f32[40,128]{1,0:T(8,128)S(1)}, f32[40,128]{1,0:T(8,128)S(1)}, u32[]{:S(2)}, u32[]{:S(2)}) collective-permute-start(f32[40,128]{1,0:T(8,128)S(1)} %get-tuple-element.17), channel_id=1, source_target_pairs={{1,2},{3,4},{5,6},{2,1},{4,3},{6,5},{9,10},{11,12},{13,14},{10,9},... | collective-permute-start | bytes 61448 | tf_op jit(solution)/shard_map/ppermute | solution.py:383
  3.9 5.0 %collective-permute-start.2 = (f32[24,384]{1,0:T(8,128)S(1)}, f32[24,384]{1,0:T(8,128)S(1)}, u32[]{:S(2)}, u32[]{:S(2)}) collective-permute-start(f32[24,384]{1,0:T(8,128)S(1)} %get-tuple-element.23), channel_id=1, source_target_pairs={{0,8},{16,24},{8,0},{24,16},{1,9},{17,25},{9,1},{25,17},{2,10},{18... | collective-permute-start | bytes 110600 | tf_op jit(solution)/shard_map/ppermute | solution.py:390
  6.7 2.1 %collective-permute-start.3 = (f32[24,384]{1,0:T(8,128)S(1)}, f32[24,384]{1,0:T(8,128)S(1)}, u32[]{:S(2)}, u32[]{:S(2)}) collective-permute-start(f32[24,384]{1,0:T(8,128)S(1)} %get-tuple-element.24), channel_id=1, source_target_pairs={{8,16},{16,8},{9,17},{17,9},{10,18},{18,10},{11,19},{19,11},{12,20... | collective-permute-start | bytes 110600 | tf_op jit(solution)/shard_map/ppermute | solution.py:391
  8.9 26.7 %copy-start.1 = (f32[128,256]{1,0:T(8,128)S(1)}, f32[128,256]{1,0:T(8,128)}, u32[]{:S(2)}) copy-start(f32[128,256]{1,0:T(8,128)} %block_ref.5) | copy-start | bytes 393220

commit v2 on v1

--- a/solution.py
+++ b/solution.py
@@ -183,18 +183,62 @@
         )
 
 
-def strip(load, table, band, window, sign):
-    sums = [None] * KSIZE
-    for u in range(KSIZE):
-        rows = load(u)
-        for v in range(KSIZE):
-            term = table[band, window, pl.ds(u * KSIZE + v, 1), :] * rows
-            sums[v] = term if u == 0 else sums[v] + term
-    total = sums[RADIUS]
-    for v in range(KSIZE):
-        if v != RADIUS:
-            total = total + pltpu.roll(sums[v], (sign * (v - RADIUS)) % LANES, 1)
-    return total
+GROUP = 32
+GROUPS = 3 * LANES // GROUP
+
+
+def strip_weights(taps, count, place, keep):
+    lane = lanes_of((8, LANES))
+    row = lax.broadcasted_iota(jnp.int32, (count, LANES), 0)
+    wide_lane = lanes_of((count, LANES))
+    pieces = [[] for _ in range(8)]
+    for part in range(3):
+        u, group = place(lane)
+        v = part * (LANES // GROUP) + group
+        index = jnp.clip(u * KSIZE + v, 0, LANES - 1)
+        base = jnp.take_along_axis(taps, index, axis=1)
+        base = jnp.where((u >= 0) & (u < KSIZE) & (v < KSIZE), base, 0.0)
+        for tile in range(8):
+            moved = pltpu.roll(
+                jnp.broadcast_to(base[tile : tile + 1], (count, LANES)), 0, 1, stride=1, stride_axis=0
+            )
+            pieces[tile].append(jnp.where(keep(wide_lane % GROUP - row), moved, 0.0))
+    return [jnp.concatenate(piece, axis=1) for piece in pieces]
+
+
+def row_product(weights, field):
+    high, low = split(field)
+    parts = split(weights)
+    return product(parts, high, low, ((1,), (0,)))
+
+
+def spread(rows, sign):
+    moved = [rows if v == RADIUS else pltpu.roll(rows, (sign * (v - RADIUS)) % LANES, 1) for v in range(KSIZE)]
+    moved.append(jnp.zeros((GROUP * (GROUPS - KSIZE), LANES), jnp.float32))
+    return jnp.concatenate(moved, axis=0)
+
+
+def forward_strips(windows, weights):
+    lane = lanes_of((16, LANES))
+    stacked = jnp.concatenate([spread(rows, -1) for rows in windows], axis=1)
+    result = row_product(jnp.concatenate(weights, axis=0), stacked)
+    out = []
+    for window, (before, after, bound) in enumerate(REGIONS):
+        cols = slice(window * LANES, (window + 1) * LANES)
+        out.append(
+            jnp.where(lane < bound, result[16 * before : 16 * before + 16, cols], result[16 * after : 16 * after + 16, cols])
+        )
+    return out
+
+
+def adjoint_strip(rows, window, weights, count):
+    before, after, bound = REGIONS[window]
+    lane = lanes_of((GROUP, LANES))
+    stacked = jnp.concatenate(
+        [spread(jnp.where(lane < bound, rows, 0.0), 1), spread(jnp.where(lane < bound, 0.0, rows), 1)], axis=0
+    )
+    both = jnp.concatenate([weights[before][:count], weights[after][:count]], axis=1)
+    return row_product(both, stacked)
 
 
 def finish_kernel(
@@ -209,8 +253,6 @@
     grad2_ref,
     image2_ref,
     record_ref,
-    gather_table,
-    spread_table,
     edges,
     field,
     padded,
@@ -220,23 +262,20 @@
     one, two = one_ref[...], two_ref[...]
     above = jnp.where(odd_row, one, two)
     below = jnp.where(odd_row, two, one)
-    zero = jnp.zeros((1, 1), jnp.float32)
     row24 = lax.broadcasted_iota(jnp.int32, (HALO, 1), 0)
     wide = WINDOWS * LANES
     lane = lanes_of((1, LANES))
 
-    tap_row = lax.broadcasted_iota(jnp.int32, (LANES, LANES), 0)
-    tap_lane = lanes_of((LANES, LANES))
-    reach = tap_lane - (tap_row % KSIZE - RADIUS)
-    for band, taps in enumerate((above[:8, :LANES], below[REACH - 4 :, :LANES])):
-        columns = jnp.transpose(taps)
-        skip = 0 if band == 0 else 4
-        filled = [
-            jnp.broadcast_to(columns[:, skip + tile : skip + tile + 1], (LANES, LANES)) for tile in range(4)
-        ]
-        for window, (before, after, bound) in enumerate(REGIONS):
-            spread_table[band, window] = jnp.where(tap_lane < bound, filled[before], filled[after])
-            gather_table[band, window] = jnp.where(reach < bound, filled[before], filled[after])
+    row8 = lax.broadcasted_iota(jnp.int32, (8, LANES), 0)
+    taps = jnp.where(row8 < 4, above[:8, :LANES], below[HALO - 8 :, :LANES])
+    forward_weights = strip_weights(taps, 16, lambda l: (l % GROUP - 3, l // GROUP), lambda d: d >= 3)
+    above_weights = strip_weights(taps, 24, lambda l: (13 - l % GROUP, l // GROUP), lambda d: d >= 3)[:4]
+    below_weights = strip_weights(
+        taps,
+        24,
+        lambda l: (10 - (l + 13) % LANES % GROUP, (l + 13) % LANES // GROUP),
+        lambda d: d <= -3,
+    )[4:]
 
     has_left = lax.axis_index("azi") > 0
     has_right = lax.axis_index("azi") < lax.axis_size("azi") - 1
@@ -248,9 +287,9 @@
         (lane < LANES - HALO) | has_right,
     ]
 
-    edges[...] = jnp.zeros((2, 40, wide), jnp.float32)
+    edges[...] = jnp.zeros((2, 48, wide), jnp.float32)
     edges[0, :HALO] = jnp.where(row24 < HALO - REACH, 0.0, above)
-    edges[1, 16:] = jnp.where(row24 >= REACH, 0.0, below)
+    edges[1, 16:40] = jnp.where(row24 >= REACH, 0.0, below)
     field[:16] = jnp.zeros((16, wide), jnp.float32)
     field[ROWS - 16 :] = jnp.zeros((16, wide), jnp.float32)
     padded[:16] = jnp.zeros((16, wide), jnp.float32)
@@ -261,10 +300,8 @@
         return pl.ds(window * LANES, LANES)
 
     def put_field(main, window, first, count):
-        up = strip(
-            lambda u: edges[0, pl.ds(first + 29 - u, count), cols(window)], spread_table, 0, window, 1
-        )
-        down = strip(lambda u: edges[1, pl.ds(13 - u, count), cols(window)], spread_table, 1, window, 1)
+        up = adjoint_strip(edges[0, pl.ds(first + 16, GROUP), cols(window)], window, above_weights, count)
+        down = adjoint_strip(edges[1, 16:48, cols(window)], window, below_weights, count)
         up_main = main[:16]
         if first < -8:
             up_main = jnp.concatenate([jnp.zeros((-8 - first, LANES), jnp.float32), up_main], axis=0)
@@ -287,13 +324,14 @@
 
     for window in range(WINDOWS):
         image = forward_main(field, window, high_ref, low_ref, pair)
-        up = strip(lambda u: field[pl.ds(3 + u, 16), cols(window)], gather_table, 0, window, -1)
-        down = strip(lambda u: field[pl.ds(147 + u, 16), cols(window)], gather_table, 1, window, -1)
         padded[16 : 16 + TILE, cols(window)] = image
-        edges[0, 8:24, cols(window)] = up
-        edges[1, 16:32, cols(window)] = down
+    ups = forward_strips([field[:GROUP, cols(w)] for w in range(WINDOWS)], forward_weights[:4])
+    downs = forward_strips([field[ROWS - GROUP :, cols(w)] for w in range(WINDOWS)], forward_weights[4:])
+    for window in range(WINDOWS):
+        edges[0, 8:24, cols(window)] = ups[window]
+        edges[1, 16:32, cols(window)] = downs[window]
     edges[0, :8] = jnp.zeros((8, wide), jnp.float32)
-    edges[1, 32:] = jnp.zeros((8, wide), jnp.float32)
+    edges[1, 32:40] = jnp.zeros((8, wide), jnp.float32)
     image_ref[...] = padded[16 : 16 + TILE]
 
     pair[:8] = jnp.zeros((8, LANES), jnp.float32)
@@ -396,14 +434,11 @@
         [pltpu.VMEM((160, wide), jnp.float32), pltpu.VMEM((152, LANES), jnp.float32)],
         limit=8,
     )(block, taps)
-    table = pltpu.VMEM((2, WINDOWS, LANES, LANES), jnp.float32)
     grad, image, grad2, image2, record = call(
         finish_kernel,
         [f32(TILE, wide)] * 4 + [f32(devices, 1, LANES)],
         [
-            table,
-            table,
-            pltpu.VMEM((2, 40, wide), jnp.float32),
+            pltpu.VMEM((2, 48, wide), jnp.float32),
             pltpu.VMEM((ROWS, wide), jnp.float32),
             pltpu.VMEM((160, wide), jnp.float32),
             pltpu.VMEM((152, LANES), jnp.float32),

time: 36.7 us -> 34.3 us (0.935)
  Pallas kernels: 8.92 us -> 6.47 us
    pallas_call x1, Pallas kernels: 6.25 us -> 3.8 us  [body(): call(finish_kernel, [f32(TILE, wide)] * 4 + [f32(devices, 1, LANES)], [pl...]
where the time goes in v2:
time: 34.3 us; the launch traced here: 34.1 us
  blocking collectives  20.4 us (59%)
  Pallas kernels  6.47 us (19%)
  starting transfers between devices  4.72 us (14%)
  local copies, waits for them, and re-layouts  1.58 us (5%)
  between operations  0.7 us (2%)
    all_to_all x1, blocking collectives, body(): records = lax.all_to_all(record, ('rng', 'azi'), 0, 0, tiled=True)  20.4 us
    pallas_call x1, Pallas kernels, body(): call(finish_kernel, [f32(TILE, wide)] * 4 + [f32(devices, 1, LANES)], [pl...  3.8 us
    ppermute x1, starting transfers between devices, body(): one = lax.ppermute(one, 'rng', one_pairs)  2.9 us
    unnamed x6, local copies, waits for them, and re-layouts  1.58 us
    pallas_call x1, Pallas kernels, body(): call(start_kernel, [matrix, matrix, f32(MAIN, wide)], [pltpu.VMEM((160, w...  1.43 us
    pallas_call x1, Pallas kernels, body(): call(combine_kernel, [f32(TILE, 2 * LANES)] * 2)  0.99 us
  transfers between devices with their start and end apart: 4, of which 1 were waited for; matrix products, arithmetic and copies ran while one was open for 0% of the time, Pallas kernels for 4%

profile of v2, /device:TPU:0, one launch (start us, length us, event | category | flops | bytes accessed | tf_op | source)
XLA Modules:
  0.0 34.1 jit_solution(10728339269497740067)
XLA Ops:
  0.6 0.0 copy-start
  0.6 0.9 %copy-done = f32[128,256]{1,0:T(8,128)S(1)} copy-done((f32[128,256]{1,0:T(8,128)S(1)}, f32[128,256]{1,0:T(8,128)}, u32[]{:S(2)}) %copy-start) | copy-done | bytes 131096
  1.5 0.0 copy-start.2
  1.5 0.7 %copy-done.2 = f32[1,2,121]{2,1,0:T(2,128)S(1)} copy-done((f32[1,2,121]{2,1,0:T(2,128)S(1)}, f32[1,2,121]{2,1,0:T(2,128)}, u32[]{:S(2)}) %copy-start.2) | copy-done | bytes 992
  2.2 0.1 shard_map.41
  2.3 0.5 %collective-permute-start = (f32[40,128]{1,0:T(8,128)S(1)}, f32[40,128]{1,0:T(8,128)S(1)}, u32[]{:S(2)}, u32[]{:S(2)}) collective-permute-start(f32[40,128]{1,0:T(8,128)S(1)} %get-tuple-element.16), channel_id=1, source_target_pairs={{0,1},{2,3},{4,5},{6,7},{1,0},{3,2},{5,4},{7,6},{8,9},{10,11},{12,... | collective-permute-start | bytes 61448 | tf_op jit(solution)/shard_map/ppermute | solution.py:420
  2.8 0.7 %collective-permute-start.1 = (f32[40,128]{1,0:T(8,128)S(1)}, f32[40,128]{1,0:T(8,128)S(1)}, u32[]{:S(2)}, u32[]{:S(2)}) collective-permute-start(f32[40,128]{1,0:T(8,128)S(1)} %get-tuple-element.17), channel_id=1, source_target_pairs={{1,2},{3,4},{5,6},{2,1},{4,3},{6,5},{9,10},{11,12},{13,14},{10,9},... | collective-permute-start | bytes 61448 | tf_op jit(solution)/shard_map/ppermute | solution.py:421
  3.5 0.2 collective-permute-done.near_ref
  3.7 0.0 collective-permute-done.1.far_ref
  3.7 0.2 shard_map.42
  3.9 2.9 %collective-permute-start.2 = (f32[24,384]{1,0:T(8,128)S(1)}, f32[24,384]{1,0:T(8,128)S(1)}, u32[]{:S(2)}, u32[]{:S(2)}) collective-permute-start(f32[24,384]{1,0:T(8,128)S(1)} %get-tuple-element.23), channel_id=1, source_target_pairs={{0,8},{16,24},{8,0},{24,16},{1,9},{17,25},{9,1},{25,17},{2,10},{18... | collective-permute-start | bytes 110600 | tf_op jit(solution)/shard_map/ppermute | solution.py:428
  6.7 0.7 %collective-permute-start.3 = (f32[24,384]{1,0:T(8,128)S(1)}, f32[24,384]{1,0:T(8,128)S(1)}, u32[]{:S(2)}, u32[]{:S(2)}) collective-permute-start(f32[24,384]{1,0:T(8,128)S(1)} %get-tuple-element.24), channel_id=1, source_target_pairs={{8,16},{16,8},{9,17},{17,9},{10,18},{18,10},{11,19},{19,11},{12,20... | collective-permute-start | bytes 110600 | tf_op jit(solution)/shard_map/ppermute | solution.py:429
  7.4 1.4 %shard_map.43 = (bf16[3,768,256]{2,1,0:T(8,128)(2,1)S(1)}, bf16[3,768,256]{2,1,0:T(8,128)(2,1)S(1)}, f32[144,384]{1,0:T(8,128)S(1)}) custom-call(f32[128,384]{1,0:T(8,128)S(1)} %get-tuple-element.18.wide_ref, f32[8,128]{1,0:T(8,128)S(1)} %get-tuple-element.19.taps_ref), custom_call_target="tpu_custom_call" | custom-call | tf_op jit(solution)/shard_map/pallas_call | solution.py:431
  8.8 0.0 collective-permute-done.2.one_ref
  8.9 0.0 collective-permute-done.3.two_ref
  8.9 0.0 copy-start.1
  8.9 3.8 %shard_map.44 = (f32[128,384]{1,0:T(8,128)S(1)}, f32[128,384]{1,0:T(8,128)S(1)}, f32[128,384]{1,0:T(8,128)S(1)}, f32[128,384]{1,0:T(8,128)S(1)}, f32[32,1,128]{2,1,0:T(1,128)S(1)}) custom-call(f32[128,384]{1,0:T(8,128)S(1)} %get-tuple-element.18.wide_ref, bf16[3,768,256]{2,1,0:T(8,128)(2,1)S(1)} %get-tuple-element.20.high_ref, ...), custom_call_target="tpu_custom_call" | custom-call | tf_op jit(solution)/shard_map/pallas_call | solution.py:437
  12.7 20.4 %all_to_all.5.records_ref = f32[32,1,128]{2,1,0:T(1,128)S(1)} all-to-all(f32[32,1,128]{2,1,0:T(1,128)S(1)} %get-tuple-element.25), channel_id=1, replica_groups=mesh['rng'=4,'azi'=8] {'rng','azi'}, dimensions={0} | all-to-all | bytes 32768 | tf_op jit(solution)/shard_map/all_to_all | solution.py:448
  33.1 0.0 copy-done.1
  33.1 1.0 %shard_map.45 = (f32[128,256]{1,0:T(8,128)}, f32[128,256]{1,0:T(8,128)}) custom-call(f32[32,1,128]{2,1,0:T(1,128)S(1)} %all_to_all.5.records_ref, f32[128,256]{1,0:T(8,128)S(1)} %copy-done.1, f32[128,384]{1,0:T(8,128)S(1)} %get-tuple-element.26.grad_ref, f32[128,384]{1,0:T(8,128)S(1)} %get-tuple-element.27.image_ref, ...), custom_call_target="tpu_custom_call" | custom-call | tf_op jit(solution)/shard_map/pallas_call | solution.py:449
Async XLA Ops:
  0.6 0.9 %copy-start = (f32[128,256]{1,0:T(8,128)S(1)}, f32[128,256]{1,0:T(8,128)}, u32[]{:S(2)}) copy-start(f32[128,256]{1,0:T(8,128)} %block_ref.5) | copy-start | bytes 393220
  1.5 0.7 %copy-start.2 = (f32[1,2,121]{2,1,0:T(2,128)S(1)}, f32[1,2,121]{2,1,0:T(2,128)}, u32[]{:S(2)}) copy-start(f32[1,2,121]{2,1,0:T(2,128)} %param.3) | copy-start | bytes 2908
  2.3 1.4 %collective-permute-start = (f32[40,128]{1,0:T(8,128)S(1)}, f32[40,128]{1,0:T(8,128)S(1)}, u32[]{:S(2)}, u32[]{:S(2)}) collective-permute-start(f32[40,128]{1,0:T(8,128)S(1)} %get-tuple-element.16), channel_id=1, source_target_pairs={{0,1},{2,3},{4,5},{6,7},{1,0},{3,2},{5,4},{7,6},{8,9},{10,11},{12,... | collective-permute-start | bytes 61448 | tf_op jit(solution)/shard_map/ppermute | solution.py:420
  2.8 0.8 %collective-permute-start.1 = (f32[40,128]{1,0:T(8,128)S(1)}, f32[40,128]{1,0:T(8,128)S(1)}, u32[]{:S(2)}, u32[]{:S(2)}) collective-permute-start(f32[40,128]{1,0:T(8,128)S(1)} %get-tuple-element.17), channel_id=1, source_target_pairs={{1,2},{3,4},{5,6},{2,1},{4,3},{6,5},{9,10},{11,12},{13,14},{10,9},... | collective-permute-start | bytes 61448 | tf_op jit(solution)/shard_map/ppermute | solution.py:421
  3.9 5.0 %collective-permute-start.2 = (f32[24,384]{1,0:T(8,128)S(1)}, f32[24,384]{1,0:T(8,128)S(1)}, u32[]{:S(2)}, u32[]{:S(2)}) collective-permute-start(f32[24,384]{1,0:T(8,128)S(1)} %get-tuple-element.23), channel_id=1, source_target_pairs={{0,8},{16,24},{8,0},{24,16},{1,9},{17,25},{9,1},{25,17},{2,10},{18... | collective-permute-start | bytes 110600 | tf_op jit(solution)/shard_map/ppermute | solution.py:428
  6.7 2.1 %collective-permute-start.3 = (f32[24,384]{1,0:T(8,128)S(1)}, f32[24,384]{1,0:T(8,128)S(1)}, u32[]{:S(2)}, u32[]{:S(2)}) collective-permute-start(f32[24,384]{1,0:T(8,128)S(1)} %get-tuple-element.24), channel_id=1, source_target_pairs={{8,16},{16,8},{9,17},{17,9},{10,18},{18,10},{11,19},{19,11},{12,20... | collective-permute-start | bytes 110600 | tf_op jit(solution)/shard_map/ppermute | solution.py:429
  8.9 24.2 %copy-start.1 = (f32[128,256]{1,0:T(8,128)S(1)}, f32[128,256]{1,0:T(8,128)}, u32[]{:S(2)}) copy-start(f32[128,256]{1,0:T(8,128)} %block_ref.5) | copy-start | bytes 393220

commit v3 on v0

v3 whole, which is shorter than its diff:
```python
import jax
import jax.numpy as jnp
from jax import lax
from jax.experimental import pallas as pl
from jax.experimental.pallas import tpu as pltpu
from jax.sharding import PartitionSpec as P

TILE = 128
KSIZE = 11
RADIUS = 5
TAPS = KSIZE * KSIZE
LANES = 128
HALO = 24
REACH = 20
WINDOWS = 3
ROWS = TILE + 2 * HALO
SLOTS = (KSIZE + 1) // 2
DEPTH = SLOTS * LANES
MAIN = 144
REGIONS = ((0, 1, 24), (1, 2, 64), (2, 3, 104))
VMEM = pl.BlockSpec(memory_space=pltpu.VMEM)


def call(kernel, out_shape, scratch=(), limit=4, inputs=None):
    given = {} if inputs is None else {"in_specs": inputs}
    return pl.pallas_call(
        kernel,
        out_shape=out_shape,
        out_specs=[VMEM] * len(out_shape),
        **given,
        scratch_shapes=list(scratch),
        compiler_params=pltpu.CompilerParams(vmem_limit_bytes=limit * 2**20),
    )


def f32(*shape):
    return jax.ShapeDtypeStruct(shape, jnp.float32)


def lanes_of(shape):
    return lax.broadcasted_iota(jnp.int32, shape, len(shape) - 1)


def is_odd(axis):
    return lax.axis_index(axis) % 2 == 1


def load_kernel(observed_ref, psf_ref, block_ref, taps_ref, far_ref, near_ref, psf, sems):
    half = TILE // 2
    loads = [
        pltpu.make_async_copy(observed_ref.at[pl.ds(half * i, half)], block_ref.at[pl.ds(half * i, half)], sems.at[i])
        for i in range(2)
    ]
    loads.append(pltpu.make_async_copy(psf_ref, psf, sems.at[2]))
    for load in loads:
        load.start()
    taps_ref[...] = jnp.zeros((8, LANES), jnp.float32)
    for load in loads:
        load.wait()
    taps_ref[1:2, :TAPS] = psf[0, 0:1, :]
    taps_ref[2:3, :TAPS] = psf[0, 1:2, :]
    columns_kernel(block_ref, taps_ref, far_ref, near_ref)


def columns_kernel(block_ref, taps_ref, far_ref, near_ref):
    lane = lanes_of((32, LANES))

    def packed(side, first):
        out = jnp.zeros((32, LANES), jnp.float32)
        for part in range(4):
            rows = block_ref[32 * part : 32 * part + 32, LANES * side : LANES * side + LANES]
            moved = pltpu.roll(rows, (32 * part - first) % LANES, 1)
            out = jnp.where((lane >= 32 * part) & (lane < 32 * part + HALO), moved, out)
        return out

    left, right = packed(0, 0), packed(1, LANES - HALO)
    odd = is_odd("azi")
    near_ref[:32] = jnp.where(odd, left, right)
    far_ref[:32] = jnp.where(odd, right, left)
    first, second = taps_ref[...], pltpu.roll(taps_ref[...], 7, 0)
    near_ref[32:] = jnp.where(odd, first, second)
    far_ref[32:] = jnp.where(odd, second, first)


def rows_kernel(block_ref, own_ref, far_ref, near_ref, _, wide_ref, taps_ref, two_ref, one_ref, top, low):
    odd = is_odd("azi")
    lane = lanes_of((32, LANES))
    near, far = near_ref[:32], far_ref[:32]
    left = jnp.where(odd, near, far)
    right = jnp.where(odd, far, near)
    for part in range(4):
        rows = slice(32 * part, 32 * part + 32)
        first = block_ref[rows, :LANES]
        second = block_ref[rows, LANES:]
        halo_left = pltpu.roll(left, (-32 * part) % LANES, 1)
        halo_right = pltpu.roll(right, (LANES - HALO - 32 * part) % LANES, 1)
        wide_ref[rows, :LANES] = jnp.where(lane < HALO, halo_left, pltpu.roll(first, HALO, 1))
        wide_ref[rows, LANES : 2 * LANES] = middle_window(first, second)
        wide_ref[rows, 2 * LANES :] = jnp.where(
            lane < LANES - HALO, pltpu.roll(second, LANES - HALO, 1), halo_right
        )
    near_taps, far_taps = near_ref[33:34], far_ref[33:34]
    taps_ref[...] = own_ref[...]
    taps_ref[0:1] = jnp.where(odd, near_taps, far_taps)
    taps_ref[3:4] = jnp.where(odd, far_taps, near_taps)
    top[...] = wide_ref[:HALO]
    low[...] = wide_ref[TILE - HALO :]
    top[REACH:, :LANES] = taps_ref[0:4]
    low[: HALO - REACH, :LANES] = taps_ref[0:4]
    odd_row = is_odd("rng")
    one_ref[...] = jnp.where(odd_row, top[...], low[...])
    two_ref[...] = jnp.where(odd_row, low[...], top[...])


def middle_window(first, second):
    lane = lanes_of(first.shape)
    return jnp.where(lane < 64, pltpu.roll(first, 64, 1), pltpu.roll(second, 64, 1))


def split(value):
    high = value.astype(jnp.bfloat16)
    return high, (value - high.astype(jnp.float32)).astype(jnp.bfloat16)


def product(parts, high, low, dims):
    rows = parts[0].shape[0]

    def dot(a, b):
        return lax.dot_general(a, b, (dims, ((), ())), preferred_element_type=jnp.float32)

    both = dot(jnp.concatenate(parts, axis=0), high)
    return both[:rows] + both[rows:] + dot(parts[0], low)


def stacked_rows(field_ref, first, count, offsets):
    pieces = [split(field_ref[pl.ds(HALO + first + offset, count), :]) for offset in offsets]
    return [jnp.concatenate([piece[part] for piece in pieces], axis=1) for part in range(2)]


def adjoint_rows(field_ref, block, pair, first, count, lead):
    offsets = [RADIUS - 2 * slot for slot in range(SLOTS)]
    parts = stacked_rows(field_ref, first - lead, count + lead, offsets)
    high, low = [jnp.concatenate([block(part, slot) for slot in range(SLOTS)], axis=0) for part in range(2)]
    both = product(parts, high, low, ((1,), (0,)))
    if lead == 0:
        pair[:8, :] = jnp.zeros((8, LANES), jnp.float32)
    pair[pl.ds(8 if lead == 0 else 0, count + lead), :] = both[:, LANES:]
    return both[lead:, :LANES] + pair[pl.ds(7 if lead == 0 else lead - 1, count), :]


def forward_rows(field_ref, block, pair):
    offsets = [2 * slot - RADIUS for slot in range(SLOTS)]
    parts = stacked_rows(field_ref, 0, MAIN, offsets)

    def turned(part):
        blocks = [block(part, slot) for slot in range(SLOTS)]
        halves = [
            jnp.concatenate([value[:, half * LANES : (half + 1) * LANES] for value in blocks], axis=1)
            for half in range(2)
        ]
        return jnp.concatenate(halves, axis=0)

    both = product(parts, turned(0), turned(1), ((1,), (1,)))
    pair[:MAIN, :] = both[:, LANES:]
    return both[:TILE, :LANES] + pair[pl.ds(1, TILE), :]


def tap_lines(taps):
    spot = (lanes_of((8, LANES)) + RADIUS) % LANES
    return [
        jnp.where(spot < KSIZE, jnp.take_along_axis(taps, jnp.minimum(KSIZE * u + spot, LANES - 1), axis=1), 0.0)
        for u in range(KSIZE)
    ]


def put_band(lines, offset, window, first, count, refs):
    slot, half = offset // 2, offset % 2
    place = (slice(slot * count, (slot + 1) * count), slice(half * LANES, (half + 1) * LANES))
    if offset >= KSIZE:
        for ref in refs:
            ref[place] = jnp.zeros((count, LANES), jnp.bfloat16)
        return
    before, after, bound = REGIONS[window]
    row = first + lax.broadcasted_iota(jnp.int32, (count, LANES), 0)
    left, right = [jnp.broadcast_to(lines[offset][tile : tile + 1], (count, LANES)) for tile in (before, after)]
    base = left if first + count <= bound else right if first >= bound else jnp.where(row < bound, left, right)
    refs[0][place], refs[1][place] = split(pltpu.roll(base, first, 1, stride=1, stride_axis=0))


def inside(window):
    lane = lanes_of((1, LANES))
    if window == 0:
        return (lane >= HALO) | (lax.axis_index("azi") > 0)
    if window == 2:
        return (lane < LANES - HALO) | (lax.axis_index("azi") < lax.axis_size("azi") - 1)
    return lane >= 0


def early_rows(rows, windows, blocks, outs, fields, pairs, between=lambda stage: None):
    own = slice(HALO, HALO + TILE)
    each = range(len(windows))
    keep = [inside(window) for window in windows]
    for i in each:
        for stage in range(4):
            fields[i, stage, :HALO] = jnp.zeros((HALO, LANES), jnp.float32)
            fields[i, stage, HALO + TILE :] = jnp.zeros((HALO, LANES), jnp.float32)
        fields[i, 0, own] = rows[i]
    for i in each:
        main = adjoint_rows(fields.at[i, 0], blocks[i], pairs.at[i, 0], -8, MAIN, 0)
        main = jnp.where(keep[i], main, 0.0)
        outs[i][0][...] = main
        fields[i, 1, HALO - 8 : HALO + TILE + 8] = main
    between(0)
    for i in each:
        image = forward_rows(fields.at[i, 1], blocks[i], pairs.at[i, 1])
        outs[i][1][...] = image
        fields[i, 2, own] = image
    between(1)
    for i in each:
        grad = adjoint_rows(fields.at[i, 2], blocks[i], pairs.at[i, 2], 0, TILE, 16)
        grad = jnp.where(keep[i], grad, 0.0)
        outs[i][2][...] = grad
        fields[i, 3, own] = grad
    between(2)
    for i in each:
        outs[i][3][...] = forward_rows(fields.at[i, 3], blocks[i], pairs.at[i, 3])
    between(3)


PATCH = 32
REST = LANES - PATCH


def middle_kernel(block_ref, taps_ref, *refs):
    outs, sides = refs[:4], (refs[4:6], refs[6:8])
    high, low, fields, pairs = refs[8:]
    lines = tap_lines(taps_ref[...])
    for offset in range(2 * SLOTS):
        put_band(lines, offset, 1, 0, LANES, (high, low))

    def between(stage):
        for offset in range(3 * stage, 3 * stage + 3):
            put_band(lines, offset, 0, PATCH, REST, sides[0])
            put_band(lines, offset, 2, 0, REST, sides[1])

    def block(part, slot):
        return (high, low)[part][slot * LANES : (slot + 1) * LANES, :]

    rows = middle_window(block_ref[:, :LANES], block_ref[:, LANES:])
    early_rows([rows], (1,), [block], [outs], fields, pairs, between)


def sides_kernel(wide_ref, taps_ref, *refs):
    rest, middle = (refs[:2], refs[2:4]), refs[4:8]
    outs, refs = (refs[8:12], refs[12:16]), refs[16:]
    plain_ref, turned_ref, inner_ref, patches, fields, pairs = refs
    taps = taps_ref[...]
    lines = tap_lines(taps)
    for offset in range(2 * SLOTS):
        put_band(lines, offset, 0, 0, PATCH, (patches.at[0, 0], patches.at[0, 1]))
        put_band(lines, offset, 2, REST, PATCH, (patches.at[1, 0], patches.at[1, 1]))

    def piece(side, part, slot):
        whole = rest[side][part][slot * REST : (slot + 1) * REST, :]
        patch = patches[side, part, slot * PATCH : (slot + 1) * PATCH, :]
        return jnp.concatenate([patch, whole] if side == 0 else [whole, patch], axis=0)

    blocks = [lambda part, slot: piece(0, part, slot), lambda part, slot: piece(1, part, slot)]

    def between(stage):
        if stage == 0:
            plain_ref[...] = jnp.concatenate(row_weights(taps, range(4), False), axis=0)
        if stage == 1:
            turned_ref[...] = jnp.concatenate(row_weights(taps, range(4), True), axis=0)

    rows = [wide_ref[:, :LANES], wide_ref[:, 2 * LANES :]]
    early_rows(rows, (0, 2), blocks, outs, fields, pairs, between)
    early = (outs[0], middle, outs[1])
    inner = [[window[0][8 + INNER.start : 8 + INNER.stop] for window in early]]
    inner += [[window[i][INNER] for window in early] for i in range(1, 4)]
    inner_ref[...] = jnp.broadcast_to(record_of(inner, 0), (8, LANES))


GROUP = 32
GROUPS = 3 * LANES // GROUP
EDGE = 4 * RADIUS
COUNT = 24


def row_weights(taps, tiles, turned):
    lane = lanes_of((8, LANES))
    pieces = [[] for _ in tiles]
    for part in range(3):
        u = lane % GROUP
        if turned:
            u = KSIZE - 1 - u
        v = part * (LANES // GROUP) + lane // GROUP
        base = jnp.take_along_axis(taps, jnp.clip(u * KSIZE + v, 0, LANES - 1), axis=1)
        base = jnp.where((u >= 0) & (u < KSIZE) & (v < KSIZE), base, 0.0)
        for piece, tile in zip(pieces, tiles):
            row = jnp.broadcast_to(base[tile : tile + 1], (COUNT, LANES))
            piece.append(pltpu.roll(row, 0, 1, stride=1, stride_axis=0))
    return [jnp.concatenate(piece, axis=1) for piece in pieces]


def spread(rows, sign):
    moved = [rows if v == RADIUS else pltpu.roll(rows, (sign * (v - RADIUS)) % LANES, 1) for v in range(KSIZE)]
    moved.append(jnp.zeros((GROUP * (GROUPS - KSIZE), LANES), rows.dtype))
    return jnp.concatenate(moved, axis=0)


def forward_edge(rows, weights):
    lane = lanes_of((COUNT, LANES))
    parts = [split(value) for value in rows]
    high, low = [jnp.concatenate([spread(part[i], -1) for part in parts], axis=1) for i in range(2)]
    result = product(split(weights), high, low, ((1,), (0,)))
    out = []
    for window, (before, after, bound) in enumerate(REGIONS):
        cols = slice(window * LANES, (window + 1) * LANES)
        left, right = [result[COUNT * tile : COUNT * tile + COUNT, cols] for tile in (before, after)]
        out.append(jnp.where(lane < bound, left, right))
    return out


def adjoint_edge(rows, window, weights):
    before, after, bound = REGIONS[window]
    lane = lanes_of((GROUP, LANES))
    high, low = [
        jnp.concatenate(
            [
                spread(jnp.where(lane < bound, part, jnp.zeros_like(part)), 1),
                spread(jnp.where(lane < bound, jnp.zeros_like(part), part), 1),
            ],
            axis=0,
        )
        for part in split(rows)
    ]
    both = [weights[COUNT * tile : COUNT * tile + COUNT] for tile in (before, after)]
    return product(split(jnp.concatenate(both, axis=1)), high, low, ((1,), (0,)))


def edge_rows(side, message, plain_ref, turned_ref, early, outs, edge, fields):
    wide = WINDOWS * LANES
    each = range(WINDOWS)
    base = 16 if side == 0 else -80
    near = slice(16, 64) if side == 0 else slice(0, 48)
    own = slice(0, 48) if side == 0 else slice(80, 128)
    out = slice(16, 40) if side == 0 else slice(24, 48)
    start = (-15, -10, -5, 0) if side == 0 else (123, 118, 113, 108)
    beyond = lax.axis_index("rng") > 0 if side == 0 else lax.axis_index("rng") < lax.axis_size("rng") - 1
    keep = [inside(window) for window in each]
    row = lax.broadcasted_iota(jnp.int32, (EDGE, LANES), 0)
    half = EDGE // 2

    def cols(window):
        return pl.ds(window * LANES, LANES)

    def spot(stage, reach=0, count=EDGE):
        return pl.ds(start[stage] - reach + base, count)

    def in_image(stage, window):
        inner = row >= -start[stage] if side == 0 else row < TILE - start[stage]
        return keep[window] & (beyond | inner)

    tiles = range(4) if side == 0 else range(4, 8)
    taps = message[:8, :LANES] if side == 0 else message[HALO - 8 :, :LANES]
    turned = jnp.concatenate(row_weights(taps, tiles, True), axis=0)
    plain = jnp.concatenate(row_weights(taps, tiles, False), axis=0)

    row24 = lax.broadcasted_iota(jnp.int32, (HALO, 1), 0)
    if side == 0:
        edge[:HALO] = jnp.where(row24 < HALO - REACH, 0.0, message)
        edge[HALO:] = jnp.zeros((16, wide), jnp.float32)
        strip = slice(4, 36)
    else:
        edge[:16] = jnp.zeros((16, wide), jnp.float32)
        edge[16:] = jnp.where(row24 >= REACH, 0.0, message)
        strip = slice(6, 38)
    for window in each:
        main = early[window][0]
        field = fields.at[0, window]
        if side == 0:
            field[:8] = jnp.zeros((8, LANES), jnp.float32)
            field[8:16] = jnp.where(beyond, main[:8], 0.0)
            field[16:64] = main[8:56]
        else:
            field[:48] = main[88:136]
            field[48:56] = jnp.where(beyond, main[136:], 0.0)
            field[56:] = jnp.zeros((16, LANES), jnp.float32)
        result = adjoint_edge(edge[strip, cols(window)], window, turned)
        field[spot(0), :] += jnp.where(in_image(0, window), result[:EDGE], 0.0)
        outs[0][:, cols(window)] = field[out]

    yield
    out_row = lax.broadcasted_iota(jnp.int32, (4 * COUNT, wide), 0) % COUNT
    mixed = (plain, plain_ref[...]) if side == 0 else (plain_ref[...], plain)
    results = forward_edge(
        [fields[0, window, spot(1, RADIUS, GROUP), :] for window in each], jnp.where(out_row < half, *mixed)
    )
    for window in each:
        field = fields.at[1, window]
        if side == 0:
            field[:16] = jnp.zeros((16, LANES), jnp.float32)
        else:
            field[48:] = jnp.zeros((24, LANES), jnp.float32)
        field[near] = early[window][1][own]
        field[spot(1), :] = results[window][:EDGE]
        outs[1][:, cols(window)] = field[out]

    yield
    in_row = lanes_of((4 * COUNT, wide)) % GROUP
    if side == 0:
        mixed = jnp.where(in_row < half, turned, turned_ref[...])
    else:
        mixed = jnp.where(in_row < EDGE, turned_ref[...], turned)
    for window in each:
        result = adjoint_edge(fields[1, window, spot(2, RADIUS, GROUP), :], window, mixed)
        field = fields.at[2, window]
        if side == 0:
            field[8:16] = jnp.zeros((8, LANES), jnp.float32)
        else:
            field[48:56] = jnp.zeros((8, LANES), jnp.float32)
        field[near] = early[window][2][own]
        field[spot(2), :] = jnp.where(in_image(2, window), result[:EDGE], 0.0)
        outs[2][:, cols(window)] = field[out]

    yield
    results = forward_edge([fields[2, window, spot(3, RADIUS, GROUP), :] for window in each], plain_ref[...])
    for window in each:
        rest = COUNT - EDGE
        if side == 0:
            outs[3][EDGE:, cols(window)] = early[window][3][EDGE:COUNT]
            outs[3][:EDGE, cols(window)] = results[window][:EDGE]
        else:
            outs[3][:rest, cols(window)] = early[window][3][TILE - COUNT : TILE - EDGE]
            outs[3][rest:, cols(window)] = results[window][:EDGE]
    yield


INNER = slice(COUNT, TILE - COUNT)


def record_of(values, position):
    lane = lanes_of((1, LANES))
    bounds = ((24, 108), (20, 108), (20, 104))

    def total(pieces):
        sums = [
            jnp.where((lane >= low) & (lane < high), jnp.sum(piece, axis=0, keepdims=True), 0.0)
            for piece, (low, high) in zip(pieces, bounds)
        ]
        return jnp.sum(sums[0] + sums[1] + sums[2], axis=1, keepdims=True)

    def best(first, second):
        size = total([b * b for b in second])
        cross = total([a * b for a, b in zip(first, second)])
        ratio = jnp.where(size > 0.0, cross / jnp.where(size > 0.0, size, 1.0), 0.0)
        rest = total([(a - ratio * b) ** 2 for a, b in zip(first, second)])
        return total([a * a for a in first]), size, ratio, rest

    grad, image, grad2, image2 = values
    line = jnp.zeros((1, LANES), jnp.float32)
    for index, value in enumerate(best(grad, grad2) + best(image, image2)):
        line = jnp.where(lane == position + index, value, line)
    return line


def edge_kernel(*refs):
    early = [refs[4 * window : 4 * window + 4] for window in (1, 0, 2)]
    two_ref, one_ref, plain_ref, turned_ref, inner_ref = refs[12:17]
    tops, lows, record_ref, edge, fields = refs[17:21], refs[21:25], *refs[25:]
    odd = is_odd("rng")
    one, two = one_ref[...], two_ref[...]
    above, below = jnp.where(odd, one, two), jnp.where(odd, two, one)
    top = edge_rows(0, above, plain_ref, turned_ref, early, tops, edge.at[0], fields.at[0])
    low = edge_rows(1, below, plain_ref, turned_ref, early, lows, edge.at[1], fields.at[1])
    for _ in zip(top, low):
        pass

    def windows(i):
        both = jnp.concatenate([tops[i][...], lows[i][...]], axis=0)
        return [both[:, w * LANES : (w + 1) * LANES] for w in range(WINDOWS)]

    line = inner_ref[:1] + record_of([windows(i) for i in range(4)], 8)
    record_ref[...] = jnp.broadcast_to(line[None], record_ref.shape)


def combine_kernel(records_ref, block_ref, *refs):
    early = [refs[4 * window : 4 * window + 4] for window in (1, 0, 2)]
    tops, lows, (estimate_ref, residual_ref) = refs[12:16], refs[16:20], refs[20:]
    records = records_ref[:, 0, :]
    lane = lanes_of((1, LANES))

    def total(value, place):
        wanted = (lane % 8 == place) & (lane < 24)
        return jnp.sum(jnp.where(wanted, jnp.sum(value, axis=0, keepdims=True), 0.0), axis=1, keepdims=True)

    gamma = total(records, 0)
    delta = total(records, 4)
    alpha = gamma / delta
    apart = records + (alpha - pltpu.roll(records, 1, 1)) ** 2 * pltpu.roll(records, 2, 1)
    gamma_new = total(apart, 3)
    bent = total(apart, 7)
    factor = gamma_new / gamma
    delta_new = bent - factor * factor * delta
    alpha_new = gamma_new / delta_new
    first = alpha + alpha_new * (1.0 + factor)
    second = -alpha_new * alpha

    def own(a, b):
        parts = [first * a[w] + second * b[w] for w in range(WINDOWS)]
        lanes = lanes_of(parts[0].shape)
        middle = pltpu.roll(parts[1], 64, 1)
        left = jnp.where(lanes < 84, pltpu.roll(parts[0], LANES - HALO, 1), middle)
        right = jnp.where(lanes < 44, middle, pltpu.roll(parts[2], HALO, 1))
        return left, right

    def windows(ref):
        return [ref[:, w * LANES : (w + 1) * LANES] for w in range(WINDOWS)]

    for rows, pieces in (
        (slice(0, COUNT), lambda i: windows(tops[i])),
        (INNER, lambda i: [early[w][i][slice(8 + COUNT, 8 + TILE - COUNT) if i == 0 else INNER] for w in range(WINDOWS)]),
        (slice(TILE - COUNT, TILE), lambda i: windows(lows[i])),
    ):
        left, right = own(pieces(0), pieces(2))
        estimate_ref[rows, :LANES] = left
        estimate_ref[rows, LANES:] = right
        left, right = own(pieces(1), pieces(3))
        residual_ref[rows, :LANES] = block_ref[rows, :LANES] - left
        residual_ref[rows, LANES:] = block_ref[rows, LANES:] - right


def neighbours(axis):
    count = lax.axis_size(axis)
    near = [(i, i + 1) for i in range(0, count - 1, 2)]
    far = [(i, i + 1) for i in range(1, count - 1, 2)]
    return [pairs + [(b, a) for a, b in pairs] for pairs in (near, far)]


def body(observed, psf_tiles):
    devices = lax.axis_size("rng") * lax.axis_size("azi")
    wide = WINDOWS * LANES
    block, own, far, near = call(
        load_kernel,
        [f32(TILE, 2 * LANES), f32(8, LANES), f32(40, LANES), f32(40, LANES)],
        [pltpu.VMEM((1, 2, TAPS), jnp.float32), pltpu.SemaphoreType.DMA((3,))],
        inputs=[pl.BlockSpec(memory_space=pltpu.HBM)] * 2,
    )(
        pltpu.with_memory_space_constraint(observed, pltpu.HBM),
        pltpu.with_memory_space_constraint(psf_tiles, pltpu.HBM),
    )
    near_pairs, far_pairs = neighbours("azi")
    far = lax.ppermute(far, "azi", far_pairs)
    near = lax.ppermute(near, "azi", near_pairs)
    early = [f32(MAIN, LANES)] + [f32(TILE, LANES)] * 3
    rest = [jax.ShapeDtypeStruct((SLOTS * REST, 2 * LANES), jnp.bfloat16)] * 4

    def scratch(windows):
        return [
            pltpu.VMEM((windows, 4, ROWS, LANES), jnp.float32),
            pltpu.VMEM((windows, 4, MAIN + 8, LANES), jnp.float32),
        ]

    *middle, high0, low0, high2, low2 = call(
        middle_kernel, early + rest, [pltpu.VMEM((DEPTH, 2 * LANES), jnp.bfloat16)] * 2 + scratch(1), limit=8
    )(block, own)
    wide_block, taps, two, one = call(
        rows_kernel,
        [f32(TILE, wide), f32(8, LANES), f32(HALO, wide), f32(HALO, wide)],
        [pltpu.VMEM((HALO, wide), jnp.float32)] * 2,
    )(block, own, far, near, middle[0])
    one_pairs, two_pairs = neighbours("rng")
    two = lax.ppermute(two, "rng", two_pairs)
    one = lax.ppermute(one, "rng", one_pairs)
    *sides, plain, turned, inner = call(
        sides_kernel,
        early * 2 + [f32(4 * COUNT, wide)] * 2 + [f32(8, LANES)],
        [pltpu.VMEM((2, 2, SLOTS * PATCH, 2 * LANES), jnp.bfloat16)] + scratch(2),
        limit=8,
    )(wide_block, taps, high0, low0, high2, low2, *middle)
    *edges, record = call(
        edge_kernel,
        [f32(COUNT, wide)] * 8 + [f32(devices, 1, LANES)],
        [pltpu.VMEM((2, 40, wide), jnp.float32), pltpu.VMEM((2, 3, WINDOWS, 72, LANES), jnp.float32)],
        limit=8,
    )(*middle, *sides, two, one, plain, turned, inner)
    records = lax.all_to_all(record, ("rng", "azi"), 0, 0, tiled=True)
    estimate, residual = call(combine_kernel, [f32(TILE, 2 * LANES)] * 2)(
        records, block, *middle, *sides, *edges
    )
    return estimate, residual


def solution(mesh):
    return jax.shard_map(
        body,
        mesh=mesh,
        in_specs=(P("rng", "azi"), P("rng", "azi", None)),
        out_specs=(P("rng", "azi"), P("rng", "azi")),
        check_vma=False,
    )
```

time: 374 us -> 31.6 us (0.08); the launches traced: 370 us -> 31.4 us
  blocking collectives: 171 us -> 10.9 us
  local copies, waits for them, and re-layouts: 88.8 us -> 0 us
  starting transfers between devices: 37.6 us -> 10.1 us
  matrix products: 27.1 us -> 0 us
  waiting for transfers between devices: 21.8 us -> 0.01 us
  other arithmetic: 16.6 us -> 0 us
  Pallas kernels: 0 us -> 9.78 us
  between operations: 6.8 us -> 0.7 us
    psum x4 -> x0, blocking collectives: 171 us -> none  [the longest x2 87.4 us: grad_norm(): return lax.psum(jnp.sum(gradient * gradient), ('rng', 'azi'))]
    scatter-add x52 -> x0, local copies, waits for them, and re-layouts: 84.9 us -> none  [the longest x44 81.2 us: adjoint_local(): extended = extended.at[offset:offset + row_count, column_tile * TILE:colu...]
    ppermute x16 -> x4, starting transfers between devices: 37.6 us -> 10.1 us  [the longest x1 4.45 us: body(): near = lax.ppermute(near, 'azi', near_pairs)]
    dot_general x45 -> x0, matrix products: 27.1 us -> none  [the longest x22 16.7 us: blur_local(): jnp.einsum('barc,abcj->arbj', window_rows, band_mats[offset], precision=l...]
    ppermute x16 -> x4, waiting for transfers between devices: 21.8 us -> 0.01 us  [the longest x1 0.01 us: body(): far = lax.ppermute(far, 'azi', far_pairs)]
    all_to_all x0 -> x1, blocking collectives: none -> 10.9 us  [body(): records = lax.all_to_all(record, ('rng', 'azi'), 0, 0, tiled=True)]
    pallas_call x0 -> x6, Pallas kernels: none -> 9.78 us  [the longest x1 2.73 us: body(): call(sides_kernel, early * 2 + [f32(4 * COUNT, wide)] * 2 + [f32(8, LANES...]
    another operation x12 -> x0, other arithmetic: 9.12 us -> none
  transfers between devices with their start and end apart: 16 -> 4, of which waited for: 10 -> 0; matrix products, arithmetic and copies ran while one was open for 1% -> 0% of each run, Pallas kernels for 0% -> 16%
where the time goes in v3:
time: 31.6 us; the launch traced here: 31.4 us
  blocking collectives  10.9 us (34%)
  starting transfers between devices  10.1 us (32%)
  Pallas kernels  9.78 us (31%)
  between operations  0.7 us (2%)
    all_to_all x1, blocking collectives, body(): records = lax.all_to_all(record, ('rng', 'azi'), 0, 0, tiled=True)  10.9 us
    ppermute x1, starting transfers between devices, body(): near = lax.ppermute(near, 'azi', near_pairs)  4.45 us
    ppermute x1, starting transfers between devices, body(): one = lax.ppermute(one, 'rng', one_pairs)  4.29 us
    pallas_call x1, Pallas kernels, body(): call(sides_kernel, early * 2 + [f32(4 * COUNT, wide)] * 2 + [f32(8, LANES...  2.73 us
    pallas_call x1, Pallas kernels, body(): call(edge_kernel, [f32(COUNT, wide)] * 8 + [f32(devices, 1, LANES)], [plt...  2.51 us
    pallas_call x1, Pallas kernels, body(): call(middle_kernel, early + rest, [pltpu.VMEM((DEPTH, 2 * LANES), jnp.bfl...  2.31 us
    pallas_call x1, Pallas kernels, body(): call(combine_kernel, [f32(TILE, 2 * LANES)] * 2)  1.08 us
    pallas_call x1, Pallas kernels, body(): call(load_kernel, [f32(TILE, 2 * LANES), f32(8, LANES), f32(40, LANES), f...  1 us
  transfers between devices with their start and end apart: 4, of which 0 were waited for; matrix products, arithmetic and copies ran while one was open for 0% of the time, Pallas kernels for 16%

profile of v3, /device:TPU:0, one launch (start us, length us, event | category | flops | bytes accessed | tf_op | source)
XLA Modules:
  0.0 31.4 jit_solution(2050811206420150307)
XLA Ops:
  0.6 1.0 %shard_map.41 = (f32[128,256]{1,0:T(8,128)S(1)}, f32[8,128]{1,0:T(8,128)S(1)}, f32[40,128]{1,0:T(8,128)S(1)}, f32[40,128]{1,0:T(8,128)S(1)}) custom-call(f32[128,256]{1,0:T(8,128)} %observed_ref.1, f32[1,2,121]{2,1,0:T(2,128)} %psf_ref.1), custom_call_target="tpu_custom_call" | custom-call | tf_op jit(solution)/shard_map/pallas_call | solution.py:544
  1.6 0.7 %collective-permute-start = (f32[40,128]{1,0:T(8,128)S(1)}, f32[40,128]{1,0:T(8,128)S(1)}, u32[]{:S(2)}, u32[]{:S(2)}) collective-permute-start(f32[40,128]{1,0:T(8,128)S(1)} %get-tuple-element.44), channel_id=1, source_target_pairs={{1,2},{3,4},{5,6},{2,1},{4,3},{6,5},{9,10},{11,12},{13,14},{10,9},... | collective-permute-start | bytes 61448 | tf_op jit(solution)/shard_map/ppermute | solution.py:554
  2.3 4.5 %collective-permute-start.1 = (f32[40,128]{1,0:T(8,128)S(1)}, f32[40,128]{1,0:T(8,128)S(1)}, u32[]{:S(2)}, u32[]{:S(2)}) collective-permute-start(f32[40,128]{1,0:T(8,128)S(1)} %get-tuple-element.45), channel_id=1, source_target_pairs={{0,1},{2,3},{4,5},{6,7},{1,0},{3,2},{5,4},{7,6},{8,9},{10,11},{12,... | collective-permute-start | bytes 61448 | tf_op jit(solution)/shard_map/ppermute | solution.py:555
  6.8 2.3 %shard_map.42 = (f32[144,128]{1,0:T(8,128)S(1)}, f32[128,128]{1,0:T(8,128)S(1)}, f32[128,128]{1,0:T(8,128)S(1)}, f32[128,128]{1,0:T(8,128)S(1)}, bf16[576,256]{1...) custom-call(f32[128,256]{1,0:T(8,128)S(1)} %get-tuple-element.38.bloc, ...), custom_call_target="tpu_custom_call" | custom-call | tf_op jit(solution)/shard_map/pallas_call | solution.py:565
  9.1 0.0 collective-permute-done.far_ref
  9.1 0.0 collective-permute-done.1.near_ref
  9.1 0.2 shard_map.43
  9.3 0.7 %collective-permute-start.2 = (f32[24,384]{1,0:T(8,128)S(1)}, f32[24,384]{1,0:T(8,128)S(1)}, u32[]{:S(2)}, u32[]{:S(2)}) collective-permute-start(f32[24,384]{1,0:T(8,128)S(1)} %get-tuple-element.60), channel_id=1, source_target_pairs={{8,16},{16,8},{9,17},{17,9},{10,18},{18,10},{11,19},{19,11},{12,20... | collective-permute-start | bytes 110600 | tf_op jit(solution)/shard_map/ppermute | solution.py:574
  9.9 4.3 %collective-permute-start.3 = (f32[24,384]{1,0:T(8,128)S(1)}, f32[24,384]{1,0:T(8,128)S(1)}, u32[]{:S(2)}, u32[]{:S(2)}) collective-permute-start(f32[24,384]{1,0:T(8,128)S(1)} %get-tuple-element.61), channel_id=1, source_target_pairs={{0,8},{16,24},{8,0},{24,16},{1,9},{17,25},{9,1},{25,17},{2,10},{18... | collective-permute-start | bytes 110600 | tf_op jit(solution)/shard_map/ppermute | solution.py:575
  14.2 2.7 %shard_map.44 = (f32[144,128]{1,0:T(8,128)S(1)}, f32[128,128]{1,0:T(8,128)S(1)}, f32[128,128]{1,0:T(8,128)S(1)}, f32[128,128]{1,0:T(8,128)S(1)}, f32[144,128]{1,...) custom-call(f32[128,384]{1,0:T(8,128)S(1)} %get-tuple-element.46.wid, ...), custom_call_target="tpu_custom_call" | custom-call | tf_op jit(solution)/shard_map/pallas_call | solution.py:576
  17.0 0.0 collective-permute-done.2.refs_12_
  17.0 0.0 collective-permute-done.3.refs_13_
  17.0 2.5 %shard_map.45 = (f32[24,384]{1,0:T(8,128)S(1)}, f32[24,384]{1,0:T(8,128)S(1)}, f32[24,384]{1,0:T(8,128)S(1)}, f32[24,384]{1,0:T(8,128)S(1)}, f32[24,384]{1,0:T(8...) custom-call(f32[144,128]{1,0:T(8,128)S(1)} %get-tuple-element.40._.r, ...), custom_call_target="tpu_custom_call" | custom-call | tf_op jit(solution)/shard_map/pallas_call | solution.py:582
  19.5 10.9 %all_to_all.5.records_ref = f32[32,1,128]{2,1,0:T(1,128)S(1)} all-to-all(f32[32,1,128]{2,1,0:T(1,128)S(1)} %get-tuple-element.65), channel_id=1, replica_groups=mesh['rng'=4,'azi'=8] {'rng','azi'}, dimensions={0} | all-to-all | bytes 32768 | tf_op jit(solution)/shard_map/all_to_all | solution.py:588
  30.4 1.1 %shard_map.46 = (f32[128,256]{1,0:T(8,128)}, f32[128,256]{1,0:T(8,128)}) custom-call(f32[32,1,128]{2,1,0:T(1,128)S(1)} %all_to_all.5.records_ref, f32[128,256]{1,0:T(8,128)S(1)} %get-tuple-element.38.block_ref, f32[144,128]{1,0:T(8,128)S(1)} %get-tuple-element.40._.refs_4_.refs_0_, f32[128,128]{1,0:T(8,128)S(1)} %get-tuple-element.41.refs_5_.refs_1_, ...), custom_call_target="tpu_custom_call" | custom-call | tf_op jit(solution)/shard_map/pallas_call | solution.py:589
Async XLA Ops:
  1.6 7.4 %collective-permute-start = (f32[40,128]{1,0:T(8,128)S(1)}, f32[40,128]{1,0:T(8,128)S(1)}, u32[]{:S(2)}, u32[]{:S(2)}) collective-permute-start(f32[40,128]{1,0:T(8,128)S(1)} %get-tuple-element.44), channel_id=1, source_target_pairs={{1,2},{3,4},{5,6},{2,1},{4,3},{6,5},{9,10},{11,12},{13,14},{10,9},... | collective-permute-start | bytes 61448 | tf_op jit(solution)/shard_map/ppermute | solution.py:554
  2.3 6.8 %collective-permute-start.1 = (f32[40,128]{1,0:T(8,128)S(1)}, f32[40,128]{1,0:T(8,128)S(1)}, u32[]{:S(2)}, u32[]{:S(2)}) collective-permute-start(f32[40,128]{1,0:T(8,128)S(1)} %get-tuple-element.45), channel_id=1, source_target_pairs={{0,1},{2,3},{4,5},{6,7},{1,0},{3,2},{5,4},{7,6},{8,9},{10,11},{12,... | collective-permute-start | bytes 61448 | tf_op jit(solution)/shard_map/ppermute | solution.py:555
  9.3 7.7 %collective-permute-start.2 = (f32[24,384]{1,0:T(8,128)S(1)}, f32[24,384]{1,0:T(8,128)S(1)}, u32[]{:S(2)}, u32[]{:S(2)}) collective-permute-start(f32[24,384]{1,0:T(8,128)S(1)} %get-tuple-element.60), channel_id=1, source_target_pairs={{8,16},{16,8},{9,17},{17,9},{10,18},{18,10},{11,19},{19,11},{12,20... | collective-permute-start | bytes 110600 | tf_op jit(solution)/shard_map/ppermute | solution.py:574
  9.9 7.0 %collective-permute-start.3 = (f32[24,384]{1,0:T(8,128)S(1)}, f32[24,384]{1,0:T(8,128)S(1)}, u32[]{:S(2)}, u32[]{:S(2)}) collective-permute-start(f32[24,384]{1,0:T(8,128)S(1)} %get-tuple-element.61), channel_id=1, source_target_pairs={{0,8},{16,24},{8,0},{24,16},{1,9},{17,25},{9,1},{25,17},{2,10},{18... | collective-permute-start | bytes 110600 | tf_op jit(solution)/shard_map/ppermute | solution.py:575

commit v4 on v3

--- a/solution.py
+++ b/solution.py
@@ -86,8 +86,10 @@
     odd = is_odd("azi")
     lane = lanes_of((32, LANES))
     near, far = near_ref[:32], far_ref[:32]
-    left = jnp.where(odd, near, far)
-    right = jnp.where(odd, far, near)
+    has_left = lax.axis_index("azi") > 0
+    has_right = lax.axis_index("azi") < lax.axis_size("azi") - 1
+    left = jnp.where(has_left, jnp.where(odd, near, far), 0.0)
+    right = jnp.where(has_right, jnp.where(odd, far, near), 0.0)
     for part in range(4):
         rows = slice(32 * part, 32 * part + 32)
         first = block_ref[rows, :LANES]
@@ -101,8 +103,8 @@
         )
     near_taps, far_taps = near_ref[33:34], far_ref[33:34]
     taps_ref[...] = own_ref[...]
-    taps_ref[0:1] = jnp.where(odd, near_taps, far_taps)
-    taps_ref[3:4] = jnp.where(odd, far_taps, near_taps)
+    taps_ref[0:1] = jnp.where(has_left, jnp.where(odd, near_taps, far_taps), 0.0)
+    taps_ref[3:4] = jnp.where(has_right, jnp.where(odd, far_taps, near_taps), 0.0)
     top[...] = wide_ref[:HALO]
     low[...] = wide_ref[TILE - HALO :]
     top[REACH:, :LANES] = taps_ref[0:4]
@@ -471,7 +473,10 @@
     tops, lows, record_ref, edge, fields = refs[17:21], refs[21:25], *refs[25:]
     odd = is_odd("rng")
     one, two = one_ref[...], two_ref[...]
-    above, below = jnp.where(odd, one, two), jnp.where(odd, two, one)
+    has_above = lax.axis_index("rng") > 0
+    has_below = lax.axis_index("rng") < lax.axis_size("rng") - 1
+    above = jnp.where(has_above, jnp.where(odd, one, two), 0.0)
+    below = jnp.where(has_below, jnp.where(odd, two, one), 0.0)
     top = edge_rows(0, above, plain_ref, turned_ref, early, tops, edge.at[0], fields.at[0])
     low = edge_rows(1, below, plain_ref, turned_ref, early, lows, edge.at[1], fields.at[1])
     for _ in zip(top, low):
@@ -531,11 +536,22 @@
         residual_ref[rows, LANES:] = block_ref[rows, LANES:] - right
 
 
-def neighbours(axis):
-    count = lax.axis_size(axis)
-    near = [(i, i + 1) for i in range(0, count - 1, 2)]
-    far = [(i, i + 1) for i in range(1, count - 1, 2)]
-    return [pairs + [(b, a) for a, b in pairs] for pairs in (near, far)]
+def partners(axis, other):
+    count, across = lax.axis_size(axis), lax.axis_size(other)
+
+    def number(i, j):
+        return i * across + j if axis == "rng" else j * count + i
+
+    near, far = [], []
+    for i in range(count):
+        for j in range(across):
+            near.append((number(i, j), number(i ^ 1, j)))
+            beside = i + 1 if i % 2 else i - 1
+            far.append((number(i, j), number(beside, j) if 0 <= beside < count else number(i, j ^ 1)))
+    return near, far
+
+
+BOTH = ("rng", "azi")
 
 
 def body(observed, psf_tiles):
@@ -550,9 +566,9 @@
         pltpu.with_memory_space_constraint(observed, pltpu.HBM),
         pltpu.with_memory_space_constraint(psf_tiles, pltpu.HBM),
     )
-    near_pairs, far_pairs = neighbours("azi")
-    far = lax.ppermute(far, "azi", far_pairs)
-    near = lax.ppermute(near, "azi", near_pairs)
+    near_pairs, far_pairs = partners("azi", "rng")
+    far = lax.ppermute(far, BOTH, far_pairs)
+    near = lax.ppermute(near, BOTH, near_pairs)
     early = [f32(MAIN, LANES)] + [f32(TILE, LANES)] * 3
     rest = [jax.ShapeDtypeStruct((SLOTS * REST, 2 * LANES), jnp.bfloat16)] * 4
 
@@ -570,9 +586,9 @@
         [f32(TILE, wide), f32(8, LANES), f32(HALO, wide), f32(HALO, wide)],
         [pltpu.VMEM((HALO, wide), jnp.float32)] * 2,
     )(block, own, far, near, middle[0])
-    one_pairs, two_pairs = neighbours("rng")
-    two = lax.ppermute(two, "rng", two_pairs)
-    one = lax.ppermute(one, "rng", one_pairs)
+    one_pairs, two_pairs = partners("rng", "azi")
+    two = lax.ppermute(two, BOTH, two_pairs)
+    one = lax.ppermute(one, BOTH, one_pairs)
     *sides, plain, turned, inner = call(
         sides_kernel,
         early * 2 + [f32(4 * COUNT, wide)] * 2 + [f32(8, LANES)],
@@ -585,7 +601,7 @@
         [pltpu.VMEM((2, 40, wide), jnp.float32), pltpu.VMEM((2, 3, WINDOWS, 72, LANES), jnp.float32)],
         limit=8,
     )(*middle, *sides, two, one, plain, turned, inner)
-    records = lax.all_to_all(record, ("rng", "azi"), 0, 0, tiled=True)
+    records = lax.all_to_all(record, BOTH, 0, 0, tiled=True)
     estimate, residual = call(combine_kernel, [f32(TILE, 2 * LANES)] * 2)(
         records, block, *middle, *sides, *edges
     )

time: 31.6 us -> 27.9 us (0.88)
  starting transfers between devices: 10.1 us -> 6.25 us
    ppermute x4, starting transfers between devices: 10.1 us -> 6.25 us  [the longest x1 3 us: body(): far = lax.ppermute(far, BOTH, far_pairs)]
  transfers between devices with their start and end apart: 4 -> 4, of which waited for: 0 -> 0; matrix products, arithmetic and copies ran while one was open for 0% -> 0% of each run, Pallas kernels for 16% -> 18%
where the time goes in v4:
time: 27.9 us; the launch traced here: 27.7 us
  blocking collectives  11 us (39%)
  Pallas kernels  9.77 us (35%)
  starting transfers between devices  6.25 us (22%)
  between operations  0.68 us (2%)
    all_to_all x1, blocking collectives, body(): records = lax.all_to_all(record, BOTH, 0, 0, tiled=True)  11 us
    ppermute x1, starting transfers between devices, body(): far = lax.ppermute(far, BOTH, far_pairs)  3 us
    pallas_call x1, Pallas kernels, body(): call(sides_kernel, early * 2 + [f32(4 * COUNT, wide)] * 2 + [f32(8, LANES...  2.72 us
    ppermute x1, starting transfers between devices, body(): one = lax.ppermute(one, BOTH, one_pairs)  2.67 us
    pallas_call x1, Pallas kernels, body(): call(edge_kernel, [f32(COUNT, wide)] * 8 + [f32(devices, 1, LANES)], [plt...  2.5 us
    pallas_call x1, Pallas kernels, body(): call(middle_kernel, early + rest, [pltpu.VMEM((DEPTH, 2 * LANES), jnp.bfl...  2.3 us
    pallas_call x1, Pallas kernels, body(): call(combine_kernel, [f32(TILE, 2 * LANES)] * 2)  1.08 us
    pallas_call x1, Pallas kernels, body(): call(load_kernel, [f32(TILE, 2 * LANES), f32(8, LANES), f32(40, LANES), f...  1 us
  transfers between devices with their start and end apart: 4, of which 0 were waited for; matrix products, arithmetic and copies ran while one was open for 0% of the time, Pallas kernels for 18%

profile of v4, /device:TPU:0, one launch (start us, length us, event | category | flops | bytes accessed | tf_op | source)
XLA Modules:
  0.0 27.7 jit_solution(4045061632073506368)
XLA Ops:
  0.6 1.0 %shard_map.41 = (f32[128,256]{1,0:T(8,128)S(1)}, f32[8,128]{1,0:T(8,128)S(1)}, f32[40,128]{1,0:T(8,128)S(1)}, f32[40,128]{1,0:T(8,128)S(1)}) custom-call(f32[128,256]{1,0:T(8,128)} %observed_ref.1, f32[1,2,121]{2,1,0:T(2,128)} %psf_ref.1), custom_call_target="tpu_custom_call" | custom-call | tf_op jit(solution)/shard_map/pallas_call | solution.py:560
  1.6 3.0 %collective-permute-start = (f32[40,128]{1,0:T(8,128)S(1)}, f32[40,128]{1,0:T(8,128)S(1)}, u32[]{:S(2)}, u32[]{:S(2)}) collective-permute-start(f32[40,128]{1,0:T(8,128)S(1)} %get-tuple-element.44), channel_id=1, source_target_pairs={{0,8},{8,0},{16,24},{24,16},{1,2},{9,10},{17,18},{25,26},{2,1},{10... | collective-permute-start | bytes 61448 | tf_op jit(solution)/shard_map/ppermute | solution.py:570
  4.6 0.2 collective-permute-start.1
  4.8 2.3 %shard_map.42 = (f32[144,128]{1,0:T(8,128)S(1)}, f32[128,128]{1,0:T(8,128)S(1)}, f32[128,128]{1,0:T(8,128)S(1)}, f32[128,128]{1,0:T(8,128)S(1)}, bf16[576,256]{1...) custom-call(f32[128,256]{1,0:T(8,128)S(1)} %get-tuple-element.38.bloc, ...), custom_call_target="tpu_custom_call" | custom-call | tf_op jit(solution)/shard_map/pallas_call | solution.py:581
  7.2 0.0 collective-permute-done.far_ref
  7.2 0.0 collective-permute-done.1.near_ref
  7.2 0.2 shard_map.43
  7.3 0.4 %collective-permute-start.2 = (f32[24,384]{1,0:T(8,128)S(1)}, f32[24,384]{1,0:T(8,128)S(1)}, u32[]{:S(2)}, u32[]{:S(2)}) collective-permute-start(f32[24,384]{1,0:T(8,128)S(1)} %get-tuple-element.60), channel_id=1, source_target_pairs={{0,1},{1,0},{2,3},{3,2},{4,5},{5,4},{6,7},{7,6},{8,16},{9,17},{10,... | collective-permute-start | bytes 110600 | tf_op jit(solution)/shard_map/ppermute | solution.py:590
  7.7 2.7 %collective-permute-start.3 = (f32[24,384]{1,0:T(8,128)S(1)}, f32[24,384]{1,0:T(8,128)S(1)}, u32[]{:S(2)}, u32[]{:S(2)}) collective-permute-start(f32[24,384]{1,0:T(8,128)S(1)} %get-tuple-element.61), channel_id=1, source_target_pairs={{0,8},{1,9},{2,10},{3,11},{4,12},{5,13},{6,14},{7,15},{8,0},{9,1},... | collective-permute-start | bytes 110600 | tf_op jit(solution)/shard_map/ppermute | solution.py:591
  10.4 2.7 %shard_map.44 = (f32[144,128]{1,0:T(8,128)S(1)}, f32[128,128]{1,0:T(8,128)S(1)}, f32[128,128]{1,0:T(8,128)S(1)}, f32[128,128]{1,0:T(8,128)S(1)}, f32[144,128]{1,...) custom-call(f32[128,384]{1,0:T(8,128)S(1)} %get-tuple-element.46.wid, ...), custom_call_target="tpu_custom_call" | custom-call | tf_op jit(solution)/shard_map/pallas_call | solution.py:592
  13.1 0.0 collective-permute-done.2.refs_12_
  13.1 0.0 collective-permute-done.3.refs_13_
  13.1 2.5 %shard_map.45 = (f32[24,384]{1,0:T(8,128)S(1)}, f32[24,384]{1,0:T(8,128)S(1)}, f32[24,384]{1,0:T(8,128)S(1)}, f32[24,384]{1,0:T(8,128)S(1)}, f32[24,384]{1,0:T(8...) custom-call(f32[144,128]{1,0:T(8,128)S(1)} %get-tuple-element.40._.r, ...), custom_call_target="tpu_custom_call" | custom-call | tf_op jit(solution)/shard_map/pallas_call | solution.py:598
  15.6 11.0 %all_to_all.5.records_ref = f32[32,1,128]{2,1,0:T(1,128)S(1)} all-to-all(f32[32,1,128]{2,1,0:T(1,128)S(1)} %get-tuple-element.65), channel_id=1, replica_groups=mesh['rng'=4,'azi'=8] {'rng','azi'}, dimensions={0} | all-to-all | bytes 32768 | tf_op jit(solution)/shard_map/all_to_all | solution.py:604
  26.6 1.1 %shard_map.46 = (f32[128,256]{1,0:T(8,128)}, f32[128,256]{1,0:T(8,128)}) custom-call(f32[32,1,128]{2,1,0:T(1,128)S(1)} %all_to_all.5.records_ref, f32[128,256]{1,0:T(8,128)S(1)} %get-tuple-element.38.block_ref, f32[144,128]{1,0:T(8,128)S(1)} %get-tuple-element.40._.refs_4_.refs_0_, f32[128,128]{1,0:T(8,128)S(1)} %get-tuple-element.41.refs_5_.refs_1_, ...), custom_call_target="tpu_custom_call" | custom-call | tf_op jit(solution)/shard_map/pallas_call | solution.py:605
Async XLA Ops:
  1.6 5.5 %collective-permute-start = (f32[40,128]{1,0:T(8,128)S(1)}, f32[40,128]{1,0:T(8,128)S(1)}, u32[]{:S(2)}, u32[]{:S(2)}) collective-permute-start(f32[40,128]{1,0:T(8,128)S(1)} %get-tuple-element.44), channel_id=1, source_target_pairs={{0,8},{8,0},{16,24},{24,16},{1,2},{9,10},{17,18},{25,26},{2,1},{10... | collective-permute-start | bytes 61448 | tf_op jit(solution)/shard_map/ppermute | solution.py:570
  4.6 2.5 %collective-permute-start.1 = (f32[40,128]{1,0:T(8,128)S(1)}, f32[40,128]{1,0:T(8,128)S(1)}, u32[]{:S(2)}, u32[]{:S(2)}) collective-permute-start(f32[40,128]{1,0:T(8,128)S(1)} %get-tuple-element.45), channel_id=1, source_target_pairs={{0,1},{8,9},{16,17},{24,25},{1,0},{9,8},{17,16},{25,24},{2,3},{10,... | collective-permute-start | bytes 61448 | tf_op jit(solution)/shard_map/ppermute | solution.py:571
  7.3 5.8 %collective-permute-start.2 = (f32[24,384]{1,0:T(8,128)S(1)}, f32[24,384]{1,0:T(8,128)S(1)}, u32[]{:S(2)}, u32[]{:S(2)}) collective-permute-start(f32[24,384]{1,0:T(8,128)S(1)} %get-tuple-element.60), channel_id=1, source_target_pairs={{0,1},{1,0},{2,3},{3,2},{4,5},{5,4},{6,7},{7,6},{8,16},{9,17},{10,... | collective-permute-start | bytes 110600 | tf_op jit(solution)/shard_map/ppermute | solution.py:590
  7.7 5.4 %collective-permute-start.3 = (f32[24,384]{1,0:T(8,128)S(1)}, f32[24,384]{1,0:T(8,128)S(1)}, u32[]{:S(2)}, u32[]{:S(2)}) collective-permute-start(f32[24,384]{1,0:T(8,128)S(1)} %get-tuple-element.61), channel_id=1, source_target_pairs={{0,8},{1,9},{2,10},{3,11},{4,12},{5,13},{6,14},{7,15},{8,0},{9,1},... | collective-permute-start | bytes 110600 | tf_op jit(solution)/shard_map/ppermute | solution.py:591

commit v5 on v4

--- a/solution.py
+++ b/solution.py
@@ -45,13 +45,16 @@
     return lax.axis_index(axis) % 2 == 1
 
 
+CHUNKS = 4
+
+
 def load_kernel(observed_ref, psf_ref, block_ref, taps_ref, far_ref, near_ref, psf, sems):
-    half = TILE // 2
+    part = TILE // CHUNKS
     loads = [
-        pltpu.make_async_copy(observed_ref.at[pl.ds(half * i, half)], block_ref.at[pl.ds(half * i, half)], sems.at[i])
-        for i in range(2)
+        pltpu.make_async_copy(observed_ref.at[pl.ds(part * i, part)], block_ref.at[pl.ds(part * i, part)], sems.at[i])
+        for i in range(CHUNKS)
     ]
-    loads.append(pltpu.make_async_copy(psf_ref, psf, sems.at[2]))
+    loads.append(pltpu.make_async_copy(psf_ref, psf, sems.at[CHUNKS]))
     for load in loads:
         load.start()
     taps_ref[...] = jnp.zeros((8, LANES), jnp.float32)
@@ -327,21 +330,24 @@
 def adjoint_edge(rows, window, weights):
     before, after, bound = REGIONS[window]
     lane = lanes_of((GROUP, LANES))
+    whole = [spread(part, 1) for part in split(rows)]
     high, low = [
         jnp.concatenate(
-            [
-                spread(jnp.where(lane < bound, part, jnp.zeros_like(part)), 1),
-                spread(jnp.where(lane < bound, jnp.zeros_like(part), part), 1),
-            ],
+            [part]
+            + [
+                jnp.where(lane < bound + v - RADIUS, moved, jnp.zeros_like(moved))
+                for v, moved in enumerate(part[GROUP * v : GROUP * v + GROUP] for v in range(KSIZE))
+            ]
+            + [part[GROUP * KSIZE :]],
             axis=0,
         )
-        for part in split(rows)
+        for part in whole
     ]
-    both = [weights[COUNT * tile : COUNT * tile + COUNT] for tile in (before, after)]
-    return product(split(jnp.concatenate(both, axis=1)), high, low, ((1,), (0,)))
-
-
-def edge_rows(side, message, plain_ref, turned_ref, early, outs, edge, fields):
+    left, right = [weights[COUNT * tile : COUNT * tile + COUNT] for tile in (before, after)]
+    return product(split(jnp.concatenate([right, left - right], axis=1)), high, low, ((1,), (0,)))
+
+
+def edge_rows(side, message, plain, turned, plain_ref, turned_ref, early, outs, edge, fields):
     wide = WINDOWS * LANES
     each = range(WINDOWS)
     base = 16 if side == 0 else -80
@@ -363,11 +369,6 @@
     def in_image(stage, window):
         inner = row >= -start[stage] if side == 0 else row < TILE - start[stage]
         return keep[window] & (beyond | inner)
-
-    tiles = range(4) if side == 0 else range(4, 8)
-    taps = message[:8, :LANES] if side == 0 else message[HALO - 8 :, :LANES]
-    turned = jnp.concatenate(row_weights(taps, tiles, True), axis=0)
-    plain = jnp.concatenate(row_weights(taps, tiles, False), axis=0)
 
     row24 = lax.broadcasted_iota(jnp.int32, (HALO, 1), 0)
     if side == 0:
@@ -477,8 +478,14 @@
     has_below = lax.axis_index("rng") < lax.axis_size("rng") - 1
     above = jnp.where(has_above, jnp.where(odd, one, two), 0.0)
     below = jnp.where(has_below, jnp.where(odd, two, one), 0.0)
-    top = edge_rows(0, above, plain_ref, turned_ref, early, tops, edge.at[0], fields.at[0])
-    low = edge_rows(1, below, plain_ref, turned_ref, early, lows, edge.at[1], fields.at[1])
+    row = lax.broadcasted_iota(jnp.int32, (8, LANES), 0)
+    taps = jnp.where(row < 4, above[:8, :LANES], below[HALO - 8 :, :LANES])
+    turned, plain = row_weights(taps, range(8), True), row_weights(taps, range(8), False)
+    (turned, turned_low), (plain, plain_low) = [
+        [jnp.concatenate(weights[side : side + 4], axis=0) for side in (0, 4)] for weights in (turned, plain)
+    ]
+    top = edge_rows(0, above, plain, turned, plain_ref, turned_ref, early, tops, edge.at[0], fields.at[0])
+    low = edge_rows(1, below, plain_low, turned_low, plain_ref, turned_ref, early, lows, edge.at[1], fields.at[1])
     for _ in zip(top, low):
         pass
 
@@ -560,7 +567,7 @@
     block, own, far, near = call(
         load_kernel,
         [f32(TILE, 2 * LANES), f32(8, LANES), f32(40, LANES), f32(40, LANES)],
-        [pltpu.VMEM((1, 2, TAPS), jnp.float32), pltpu.SemaphoreType.DMA((3,))],
+        [pltpu.VMEM((1, 2, TAPS), jnp.float32), pltpu.SemaphoreType.DMA((CHUNKS + 1,))],
         inputs=[pl.BlockSpec(memory_space=pltpu.HBM)] * 2,
     )(
         pltpu.with_memory_space_constraint(observed, pltpu.HBM),

time: 27.9 us -> 27.4 us (0.982)
  Pallas kernels: 9.77 us -> 9.31 us
    pallas_call x1, Pallas kernels: 2.5 us -> 2.09 us  [body(): call(edge_kernel, [f32(COUNT, wide)] * 8 + [f32(devices, 1, LANES)], [plt...]
  transfers between devices with their start and end apart: 4 -> 4, of which waited for: 0 -> 0; matrix products, arithmetic and copies ran while one was open for 0% -> 0% of each run, Pallas kernels for 18% -> 19%
where the time goes in v5:
time: 27.4 us; the launch traced here: 27.2 us
  blocking collectives  11 us (40%)
  Pallas kernels  9.31 us (34%)
  starting transfers between devices  6.25 us (23%)
  between operations  0.68 us (2%)
    all_to_all x1, blocking collectives, body(): records = lax.all_to_all(record, BOTH, 0, 0, tiled=True)  11 us
    ppermute x1, starting transfers between devices, body(): far = lax.ppermute(far, BOTH, far_pairs)  3 us
    pallas_call x1, Pallas kernels, body(): call(sides_kernel, early * 2 + [f32(4 * COUNT, wide)] * 2 + [f32(8, LANES...  2.73 us
    ppermute x1, starting transfers between devices, body(): one = lax.ppermute(one, BOTH, one_pairs)  2.67 us
    pallas_call x1, Pallas kernels, body(): call(middle_kernel, early + rest, [pltpu.VMEM((DEPTH, 2 * LANES), jnp.bfl...  2.31 us
    pallas_call x1, Pallas kernels, body(): call(edge_kernel, [f32(COUNT, wide)] * 8 + [f32(devices, 1, LANES)], [plt...  2.09 us
    pallas_call x1, Pallas kernels, body(): call(combine_kernel, [f32(TILE, 2 * LANES)] * 2)  1.08 us
    pallas_call x1, Pallas kernels, body(): call(load_kernel, [f32(TILE, 2 * LANES), f32(8, LANES), f32(40, LANES), f...  0.95 us
  transfers between devices with their start and end apart: 4, of which 0 were waited for; matrix products, arithmetic and copies ran while one was open for 0% of the time, Pallas kernels for 19%

profile of v5, /device:TPU:0, one launch (start us, length us, event | category | flops | bytes accessed | tf_op | source)
XLA Modules:
  0.0 27.2 jit_solution(4508488076257763446)
XLA Ops:
  0.6 1.0 %shard_map.41 = (f32[128,256]{1,0:T(8,128)S(1)}, f32[8,128]{1,0:T(8,128)S(1)}, f32[40,128]{1,0:T(8,128)S(1)}, f32[40,128]{1,0:T(8,128)S(1)}) custom-call(f32[128,256]{1,0:T(8,128)} %observed_ref.1, f32[1,2,121]{2,1,0:T(2,128)} %psf_ref.1), custom_call_target="tpu_custom_call" | custom-call | tf_op jit(solution)/shard_map/pallas_call | solution.py:567
  1.6 3.0 %collective-permute-start = (f32[40,128]{1,0:T(8,128)S(1)}, f32[40,128]{1,0:T(8,128)S(1)}, u32[]{:S(2)}, u32[]{:S(2)}) collective-permute-start(f32[40,128]{1,0:T(8,128)S(1)} %get-tuple-element.44), channel_id=1, source_target_pairs={{0,8},{8,0},{16,24},{24,16},{1,2},{9,10},{17,18},{25,26},{2,1},{10... | collective-permute-start | bytes 61448 | tf_op jit(solution)/shard_map/ppermute | solution.py:577
  4.6 0.2 collective-permute-start.1
  4.8 2.3 %shard_map.42 = (f32[144,128]{1,0:T(8,128)S(1)}, f32[128,128]{1,0:T(8,128)S(1)}, f32[128,128]{1,0:T(8,128)S(1)}, f32[128,128]{1,0:T(8,128)S(1)}, bf16[576,256]{1...) custom-call(f32[128,256]{1,0:T(8,128)S(1)} %get-tuple-element.38.bloc, ...), custom_call_target="tpu_custom_call" | custom-call | tf_op jit(solution)/shard_map/pallas_call | solution.py:588
  7.1 0.0 collective-permute-done.far_ref
  7.1 0.0 collective-permute-done.1.near_ref
  7.1 0.2 shard_map.43
  7.3 0.4 %collective-permute-start.2 = (f32[24,384]{1,0:T(8,128)S(1)}, f32[24,384]{1,0:T(8,128)S(1)}, u32[]{:S(2)}, u32[]{:S(2)}) collective-permute-start(f32[24,384]{1,0:T(8,128)S(1)} %get-tuple-element.60), channel_id=1, source_target_pairs={{0,1},{1,0},{2,3},{3,2},{4,5},{5,4},{6,7},{7,6},{8,16},{9,17},{10,... | collective-permute-start | bytes 110600 | tf_op jit(solution)/shard_map/ppermute | solution.py:597
  7.7 2.7 %collective-permute-start.3 = (f32[24,384]{1,0:T(8,128)S(1)}, f32[24,384]{1,0:T(8,128)S(1)}, u32[]{:S(2)}, u32[]{:S(2)}) collective-permute-start(f32[24,384]{1,0:T(8,128)S(1)} %get-tuple-element.61), channel_id=1, source_target_pairs={{0,8},{1,9},{2,10},{3,11},{4,12},{5,13},{6,14},{7,15},{8,0},{9,1},... | collective-permute-start | bytes 110600 | tf_op jit(solution)/shard_map/ppermute | solution.py:598
  10.3 2.7 %shard_map.44 = (f32[144,128]{1,0:T(8,128)S(1)}, f32[128,128]{1,0:T(8,128)S(1)}, f32[128,128]{1,0:T(8,128)S(1)}, f32[128,128]{1,0:T(8,128)S(1)}, f32[144,128]{1,...) custom-call(f32[128,384]{1,0:T(8,128)S(1)} %get-tuple-element.46.wid, ...), custom_call_target="tpu_custom_call" | custom-call | tf_op jit(solution)/shard_map/pallas_call | solution.py:599
  13.1 0.0 collective-permute-done.2.refs_12_
  13.1 0.0 collective-permute-done.3.refs_13_
  13.1 2.1 %shard_map.45 = (f32[24,384]{1,0:T(8,128)S(1)}, f32[24,384]{1,0:T(8,128)S(1)}, f32[24,384]{1,0:T(8,128)S(1)}, f32[24,384]{1,0:T(8,128)S(1)}, f32[24,384]{1,0:T(8...) custom-call(f32[144,128]{1,0:T(8,128)S(1)} %get-tuple-element.40._.r, ...), custom_call_target="tpu_custom_call" | custom-call | tf_op jit(solution)/shard_map/pallas_call | solution.py:605
  15.2 11.0 %all_to_all.5.records_ref = f32[32,1,128]{2,1,0:T(1,128)S(1)} all-to-all(f32[32,1,128]{2,1,0:T(1,128)S(1)} %get-tuple-element.65), channel_id=1, replica_groups=mesh['rng'=4,'azi'=8] {'rng','azi'}, dimensions={0} | all-to-all | bytes 32768 | tf_op jit(solution)/shard_map/all_to_all | solution.py:611
  26.1 1.1 %shard_map.46 = (f32[128,256]{1,0:T(8,128)}, f32[128,256]{1,0:T(8,128)}) custom-call(f32[32,1,128]{2,1,0:T(1,128)S(1)} %all_to_all.5.records_ref, f32[128,256]{1,0:T(8,128)S(1)} %get-tuple-element.38.block_ref, f32[144,128]{1,0:T(8,128)S(1)} %get-tuple-element.40._.refs_4_.refs_0_, f32[128,128]{1,0:T(8,128)S(1)} %get-tuple-element.41.refs_5_.refs_1_, ...), custom_call_target="tpu_custom_call" | custom-call | tf_op jit(solution)/shard_map/pallas_call | solution.py:612
Async XLA Ops:
  1.6 5.5 %collective-permute-start = (f32[40,128]{1,0:T(8,128)S(1)}, f32[40,128]{1,0:T(8,128)S(1)}, u32[]{:S(2)}, u32[]{:S(2)}) collective-permute-start(f32[40,128]{1,0:T(8,128)S(1)} %get-tuple-element.44), channel_id=1, source_target_pairs={{0,8},{8,0},{16,24},{24,16},{1,2},{9,10},{17,18},{25,26},{2,1},{10... | collective-permute-start | bytes 61448 | tf_op jit(solution)/shard_map/ppermute | solution.py:577
  4.6 2.5 %collective-permute-start.1 = (f32[40,128]{1,0:T(8,128)S(1)}, f32[40,128]{1,0:T(8,128)S(1)}, u32[]{:S(2)}, u32[]{:S(2)}) collective-permute-start(f32[40,128]{1,0:T(8,128)S(1)} %get-tuple-element.45), channel_id=1, source_target_pairs={{0,1},{8,9},{16,17},{24,25},{1,0},{9,8},{17,16},{25,24},{2,3},{10,... | collective-permute-start | bytes 61448 | tf_op jit(solution)/shard_map/ppermute | solution.py:578
  7.3 5.8 %collective-permute-start.2 = (f32[24,384]{1,0:T(8,128)S(1)}, f32[24,384]{1,0:T(8,128)S(1)}, u32[]{:S(2)}, u32[]{:S(2)}) collective-permute-start(f32[24,384]{1,0:T(8,128)S(1)} %get-tuple-element.60), channel_id=1, source_target_pairs={{0,1},{1,0},{2,3},{3,2},{4,5},{5,4},{6,7},{7,6},{8,16},{9,17},{10,... | collective-permute-start | bytes 110600 | tf_op jit(solution)/shard_map/ppermute | solution.py:597
  7.7 5.4 %collective-permute-start.3 = (f32[24,384]{1,0:T(8,128)S(1)}, f32[24,384]{1,0:T(8,128)S(1)}, u32[]{:S(2)}, u32[]{:S(2)}) collective-permute-start(f32[24,384]{1,0:T(8,128)S(1)} %get-tuple-element.61), channel_id=1, source_target_pairs={{0,8},{1,9},{2,10},{3,11},{4,12},{5,13},{6,14},{7,15},{8,0},{9,1},... | collective-permute-start | bytes 110600 | tf_op jit(solution)/shard_map/ppermute | solution.py:598

commit v6 on v5

--- a/solution.py
+++ b/solution.py
@@ -153,9 +153,9 @@
     return both[lead:, :LANES] + pair[pl.ds(7 if lead == 0 else lead - 1, count), :]
 
 
-def forward_rows(field_ref, block, pair):
+def forward_rows(field_ref, block, pair, first, count):
     offsets = [2 * slot - RADIUS for slot in range(SLOTS)]
-    parts = stacked_rows(field_ref, 0, MAIN, offsets)
+    parts = stacked_rows(field_ref, first, count + 16, offsets)
 
     def turned(part):
         blocks = [block(part, slot) for slot in range(SLOTS)]
@@ -166,8 +166,8 @@
         return jnp.concatenate(halves, axis=0)
 
     both = product(parts, turned(0), turned(1), ((1,), (1,)))
-    pair[:MAIN, :] = both[:, LANES:]
-    return both[:TILE, :LANES] + pair[pl.ds(1, TILE), :]
+    pair[: count + 16, :] = both[:, LANES:]
+    return both[:count, :LANES] + pair[pl.ds(1, count), :]
 
 
 def tap_lines(taps):
@@ -203,12 +203,13 @@
 
 def early_rows(rows, windows, blocks, outs, fields, pairs, between=lambda stage: None):
     own = slice(HALO, HALO + TILE)
+    most, fewer = slice(8, TILE - 8), slice(16, TILE - 16)
     each = range(len(windows))
     keep = [inside(window) for window in windows]
     for i in each:
         for stage in range(4):
-            fields[i, stage, :HALO] = jnp.zeros((HALO, LANES), jnp.float32)
-            fields[i, stage, HALO + TILE :] = jnp.zeros((HALO, LANES), jnp.float32)
+            fields[i, stage, : HALO + 8] = jnp.zeros((HALO + 8, LANES), jnp.float32)
+            fields[i, stage, HALO + TILE - 8 :] = jnp.zeros((HALO + 8, LANES), jnp.float32)
         fields[i, 0, own] = rows[i]
     for i in each:
         main = adjoint_rows(fields.at[i, 0], blocks[i], pairs.at[i, 0], -8, MAIN, 0)
@@ -217,18 +218,18 @@
         fields[i, 1, HALO - 8 : HALO + TILE + 8] = main
     between(0)
     for i in each:
-        image = forward_rows(fields.at[i, 1], blocks[i], pairs.at[i, 1])
-        outs[i][1][...] = image
-        fields[i, 2, own] = image
+        image = forward_rows(fields.at[i, 1], blocks[i], pairs.at[i, 1], most.start, TILE - 16)
+        outs[i][1][most] = image
+        fields[i, 2, HALO + most.start : HALO + most.stop] = image
     between(1)
     for i in each:
-        grad = adjoint_rows(fields.at[i, 2], blocks[i], pairs.at[i, 2], 0, TILE, 16)
+        grad = adjoint_rows(fields.at[i, 2], blocks[i], pairs.at[i, 2], most.start, TILE - 16, 16)
         grad = jnp.where(keep[i], grad, 0.0)
-        outs[i][2][...] = grad
-        fields[i, 3, own] = grad
+        outs[i][2][most] = grad
+        fields[i, 3, HALO + most.start : HALO + most.stop] = grad
     between(2)
     for i in each:
-        outs[i][3][...] = forward_rows(fields.at[i, 3], blocks[i], pairs.at[i, 3])
+        outs[i][3][fewer] = forward_rows(fields.at[i, 3], blocks[i], pairs.at[i, 3], fewer.start, TILE - 32)
     between(3)
 
 
@@ -314,17 +315,12 @@
     return jnp.concatenate(moved, axis=0)
 
 
-def forward_edge(rows, weights):
-    lane = lanes_of((COUNT, LANES))
-    parts = [split(value) for value in rows]
-    high, low = [jnp.concatenate([spread(part[i], -1) for part in parts], axis=1) for i in range(2)]
-    result = product(split(weights), high, low, ((1,), (0,)))
-    out = []
-    for window, (before, after, bound) in enumerate(REGIONS):
-        cols = slice(window * LANES, (window + 1) * LANES)
-        left, right = [result[COUNT * tile : COUNT * tile + COUNT, cols] for tile in (before, after)]
-        out.append(jnp.where(lane < bound, left, right))
-    return out
+def forward_edge(rows, window, weights):
+    before, after, bound = REGIONS[window]
+    high, low = [spread(part, -1) for part in split(rows)]
+    both = [weights[COUNT * tile : COUNT * tile + COUNT] for tile in (before, after)]
+    result = product(split(jnp.concatenate(both, axis=0)), high, low, ((1,), (0,)))
+    return jnp.where(lanes_of((COUNT, LANES)) < bound, result[:COUNT], result[COUNT:])
 
 
 def adjoint_edge(rows, window, weights):
@@ -351,8 +347,8 @@
     wide = WINDOWS * LANES
     each = range(WINDOWS)
     base = 16 if side == 0 else -80
-    near = slice(16, 64) if side == 0 else slice(0, 48)
-    own = slice(0, 48) if side == 0 else slice(80, 128)
+    near = slice(24, 64) if side == 0 else slice(0, 40)
+    own = slice(8, 48) if side == 0 else slice(80, 120)
     out = slice(16, 40) if side == 0 else slice(24, 48)
     start = (-15, -10, -5, 0) if side == 0 else (123, 118, 113, 108)
     beyond = lax.axis_index("rng") > 0 if side == 0 else lax.axis_index("rng") < lax.axis_size("rng") - 1
@@ -397,15 +393,14 @@
     yield
     out_row = lax.broadcasted_iota(jnp.int32, (4 * COUNT, wide), 0) % COUNT
     mixed = (plain, plain_ref[...]) if side == 0 else (plain_ref[...], plain)
-    results = forward_edge(
-        [fields[0, window, spot(1, RADIUS, GROUP), :] for window in each], jnp.where(out_row < half, *mixed)
-    )
+    mixed = jnp.where(out_row < half, *mixed)
+    results = [forward_edge(fields[0, window, spot(1, RADIUS, GROUP), :], window, mixed) for window in each]
     for window in each:
         field = fields.at[1, window]
         if side == 0:
-            field[:16] = jnp.zeros((16, LANES), jnp.float32)
+            field[:24] = jnp.zeros((24, LANES), jnp.float32)
         else:
-            field[48:] = jnp.zeros((24, LANES), jnp.float32)
+            field[40:] = jnp.zeros((32, LANES), jnp.float32)
         field[near] = early[window][1][own]
         field[spot(1), :] = results[window][:EDGE]
         outs[1][:, cols(window)] = field[out]
@@ -420,15 +415,15 @@
         result = adjoint_edge(fields[1, window, spot(2, RADIUS, GROUP), :], window, mixed)
         field = fields.at[2, window]
         if side == 0:
-            field[8:16] = jnp.zeros((8, LANES), jnp.float32)
+            field[8:24] = jnp.zeros((16, LANES), jnp.float32)
         else:
-            field[48:56] = jnp.zeros((8, LANES), jnp.float32)
+            field[40:56] = jnp.zeros((16, LANES), jnp.float32)
         field[near] = early[window][2][own]
         field[spot(2), :] = jnp.where(in_image(2, window), result[:EDGE], 0.0)
         outs[2][:, cols(window)] = field[out]
 
     yield
-    results = forward_edge([fields[2, window, spot(3, RADIUS, GROUP), :] for window in each], plain_ref[...])
+    results = [forward_edge(fields[2, window, spot(3, RADIUS, GROUP), :], window, plain_ref[...]) for window in each]
     for window in each:
         rest = COUNT - EDGE
         if side == 0:

time: 27.4 us -> 27.1 us (0.989)
  Pallas kernels: 9.31 us -> 8.87 us
  transfers between devices with their start and end apart: 4 -> 4, of which waited for: 0 -> 0; matrix products, arithmetic and copies ran while one was open for 0% -> 0% of each run, Pallas kernels for 19% -> 18%
where the time goes in v6:
time: 27.1 us; the launch traced here: 26.9 us
  blocking collectives  11.1 us (41%)
  Pallas kernels  8.87 us (33%)
  starting transfers between devices  6.25 us (23%)
  between operations  0.68 us (3%)
    all_to_all x1, blocking collectives, body(): records = lax.all_to_all(record, BOTH, 0, 0, tiled=True)  11.1 us
    ppermute x1, starting transfers between devices, body(): far = lax.ppermute(far, BOTH, far_pairs)  3 us
    ppermute x1, starting transfers between devices, body(): one = lax.ppermute(one, BOTH, one_pairs)  2.67 us
    pallas_call x1, Pallas kernels, body(): call(sides_kernel, early * 2 + [f32(4 * COUNT, wide)] * 2 + [f32(8, LANES...  2.58 us
    pallas_call x1, Pallas kernels, body(): call(middle_kernel, early + rest, [pltpu.VMEM((DEPTH, 2 * LANES), jnp.bfl...  2.19 us
    pallas_call x1, Pallas kernels, body(): call(edge_kernel, [f32(COUNT, wide)] * 8 + [f32(devices, 1, LANES)], [plt...  1.91 us
    pallas_call x1, Pallas kernels, body(): call(combine_kernel, [f32(TILE, 2 * LANES)] * 2)  1.08 us
    pallas_call x1, Pallas kernels, body(): call(load_kernel, [f32(TILE, 2 * LANES), f32(8, LANES), f32(40, LANES), f...  0.95 us
  transfers between devices with their start and end apart: 4, of which 0 were waited for; matrix products, arithmetic and copies ran while one was open for 0% of the time, Pallas kernels for 18%

profile of v6, /device:TPU:0, one launch (start us, length us, event | category | flops | bytes accessed | tf_op | source)
XLA Modules:
  0.0 26.9 jit_solution(1549283364147918013)
XLA Ops:
  0.6 1.0 %shard_map.41 = (f32[128,256]{1,0:T(8,128)S(1)}, f32[8,128]{1,0:T(8,128)S(1)}, f32[40,128]{1,0:T(8,128)S(1)}, f32[40,128]{1,0:T(8,128)S(1)}) custom-call(f32[128,256]{1,0:T(8,128)} %observed_ref.1, f32[1,2,121]{2,1,0:T(2,128)} %psf_ref.1), custom_call_target="tpu_custom_call" | custom-call | tf_op jit(solution)/shard_map/pallas_call | solution.py:562
  1.6 3.0 %collective-permute-start = (f32[40,128]{1,0:T(8,128)S(1)}, f32[40,128]{1,0:T(8,128)S(1)}, u32[]{:S(2)}, u32[]{:S(2)}) collective-permute-start(f32[40,128]{1,0:T(8,128)S(1)} %get-tuple-element.44), channel_id=1, source_target_pairs={{0,8},{8,0},{16,24},{24,16},{1,2},{9,10},{17,18},{25,26},{2,1},{10... | collective-permute-start | bytes 61448 | tf_op jit(solution)/shard_map/ppermute | solution.py:572
  4.6 0.2 collective-permute-start.1
  4.8 2.2 %shard_map.42 = (f32[144,128]{1,0:T(8,128)S(1)}, f32[128,128]{1,0:T(8,128)S(1)}, f32[128,128]{1,0:T(8,128)S(1)}, f32[128,128]{1,0:T(8,128)S(1)}, bf16[576,256]{1...) custom-call(f32[128,256]{1,0:T(8,128)S(1)} %get-tuple-element.38.bloc, ...), custom_call_target="tpu_custom_call" | custom-call | tf_op jit(solution)/shard_map/pallas_call | solution.py:583
  7.0 0.0 collective-permute-done.far_ref
  7.0 0.0 collective-permute-done.1.near_ref
  7.0 0.2 shard_map.43
  7.2 0.4 %collective-permute-start.2 = (f32[24,384]{1,0:T(8,128)S(1)}, f32[24,384]{1,0:T(8,128)S(1)}, u32[]{:S(2)}, u32[]{:S(2)}) collective-permute-start(f32[24,384]{1,0:T(8,128)S(1)} %get-tuple-element.60), channel_id=1, source_target_pairs={{0,1},{1,0},{2,3},{3,2},{4,5},{5,4},{6,7},{7,6},{8,16},{9,17},{10,... | collective-permute-start | bytes 110600 | tf_op jit(solution)/shard_map/ppermute | solution.py:592
  7.6 2.7 %collective-permute-start.3 = (f32[24,384]{1,0:T(8,128)S(1)}, f32[24,384]{1,0:T(8,128)S(1)}, u32[]{:S(2)}, u32[]{:S(2)}) collective-permute-start(f32[24,384]{1,0:T(8,128)S(1)} %get-tuple-element.61), channel_id=1, source_target_pairs={{0,8},{1,9},{2,10},{3,11},{4,12},{5,13},{6,14},{7,15},{8,0},{9,1},... | collective-permute-start | bytes 110600 | tf_op jit(solution)/shard_map/ppermute | solution.py:593
  10.2 2.6 %shard_map.44 = (f32[144,128]{1,0:T(8,128)S(1)}, f32[128,128]{1,0:T(8,128)S(1)}, f32[128,128]{1,0:T(8,128)S(1)}, f32[128,128]{1,0:T(8,128)S(1)}, f32[144,128]{1,...) custom-call(f32[128,384]{1,0:T(8,128)S(1)} %get-tuple-element.46.wid, ...), custom_call_target="tpu_custom_call" | custom-call | tf_op jit(solution)/shard_map/pallas_call | solution.py:594
  12.8 0.0 collective-permute-done.2.refs_12_
  12.8 0.0 collective-permute-done.3.refs_13_
  12.8 1.9 %shard_map.45 = (f32[24,384]{1,0:T(8,128)S(1)}, f32[24,384]{1,0:T(8,128)S(1)}, f32[24,384]{1,0:T(8,128)S(1)}, f32[24,384]{1,0:T(8,128)S(1)}, f32[24,384]{1,0:T(8...) custom-call(f32[144,128]{1,0:T(8,128)S(1)} %get-tuple-element.40._.r, ...), custom_call_target="tpu_custom_call" | custom-call | tf_op jit(solution)/shard_map/pallas_call | solution.py:600
  14.7 11.1 %all_to_all.5.records_ref = f32[32,1,128]{2,1,0:T(1,128)S(1)} all-to-all(f32[32,1,128]{2,1,0:T(1,128)S(1)} %get-tuple-element.65), channel_id=1, replica_groups=mesh['rng'=4,'azi'=8] {'rng','azi'}, dimensions={0} | all-to-all | bytes 32768 | tf_op jit(solution)/shard_map/all_to_all | solution.py:606
  25.8 1.1 %shard_map.46 = (f32[128,256]{1,0:T(8,128)}, f32[128,256]{1,0:T(8,128)}) custom-call(f32[32,1,128]{2,1,0:T(1,128)S(1)} %all_to_all.5.records_ref, f32[128,256]{1,0:T(8,128)S(1)} %get-tuple-element.38.block_ref, f32[144,128]{1,0:T(8,128)S(1)} %get-tuple-element.40._.refs_4_.refs_0_, f32[128,128]{1,0:T(8,128)S(1)} %get-tuple-element.41.refs_5_.refs_1_, ...), custom_call_target="tpu_custom_call" | custom-call | tf_op jit(solution)/shard_map/pallas_call | solution.py:607
Async XLA Ops:
  1.6 5.4 %collective-permute-start = (f32[40,128]{1,0:T(8,128)S(1)}, f32[40,128]{1,0:T(8,128)S(1)}, u32[]{:S(2)}, u32[]{:S(2)}) collective-permute-start(f32[40,128]{1,0:T(8,128)S(1)} %get-tuple-element.44), channel_id=1, source_target_pairs={{0,8},{8,0},{16,24},{24,16},{1,2},{9,10},{17,18},{25,26},{2,1},{10... | collective-permute-start | bytes 61448 | tf_op jit(solution)/shard_map/ppermute | solution.py:572
  4.6 2.4 %collective-permute-start.1 = (f32[40,128]{1,0:T(8,128)S(1)}, f32[40,128]{1,0:T(8,128)S(1)}, u32[]{:S(2)}, u32[]{:S(2)}) collective-permute-start(f32[40,128]{1,0:T(8,128)S(1)} %get-tuple-element.45), channel_id=1, source_target_pairs={{0,1},{8,9},{16,17},{24,25},{1,0},{9,8},{17,16},{25,24},{2,3},{10,... | collective-permute-start | bytes 61448 | tf_op jit(solution)/shard_map/ppermute | solution.py:573
  7.2 5.6 %collective-permute-start.2 = (f32[24,384]{1,0:T(8,128)S(1)}, f32[24,384]{1,0:T(8,128)S(1)}, u32[]{:S(2)}, u32[]{:S(2)}) collective-permute-start(f32[24,384]{1,0:T(8,128)S(1)} %get-tuple-element.60), channel_id=1, source_target_pairs={{0,1},{1,0},{2,3},{3,2},{4,5},{5,4},{6,7},{7,6},{8,16},{9,17},{10,... | collective-permute-start | bytes 110600 | tf_op jit(solution)/shard_map/ppermute | solution.py:592
  7.6 5.3 %collective-permute-start.3 = (f32[24,384]{1,0:T(8,128)S(1)}, f32[24,384]{1,0:T(8,128)S(1)}, u32[]{:S(2)}, u32[]{:S(2)}) collective-permute-start(f32[24,384]{1,0:T(8,128)S(1)} %get-tuple-element.61), channel_id=1, source_target_pairs={{0,8},{1,9},{2,10},{3,11},{4,12},{5,13},{6,14},{7,15},{8,0},{9,1},... | collective-permute-start | bytes 110600 | tf_op jit(solution)/shard_map/ppermute | solution.py:593

commit v7 on v6

--- a/solution.py
+++ b/solution.py
@@ -85,31 +85,39 @@
     far_ref[32:] = jnp.where(odd, second, first)
 
 
-def rows_kernel(block_ref, own_ref, far_ref, near_ref, _, wide_ref, taps_ref, two_ref, one_ref, top, low):
+def side_halos(near_ref, far_ref):
     odd = is_odd("azi")
-    lane = lanes_of((32, LANES))
     near, far = near_ref[:32], far_ref[:32]
     has_left = lax.axis_index("azi") > 0
     has_right = lax.axis_index("azi") < lax.axis_size("azi") - 1
-    left = jnp.where(has_left, jnp.where(odd, near, far), 0.0)
-    right = jnp.where(has_right, jnp.where(odd, far, near), 0.0)
-    for part in range(4):
-        rows = slice(32 * part, 32 * part + 32)
-        first = block_ref[rows, :LANES]
-        second = block_ref[rows, LANES:]
-        halo_left = pltpu.roll(left, (-32 * part) % LANES, 1)
-        halo_right = pltpu.roll(right, (LANES - HALO - 32 * part) % LANES, 1)
-        wide_ref[rows, :LANES] = jnp.where(lane < HALO, halo_left, pltpu.roll(first, HALO, 1))
-        wide_ref[rows, LANES : 2 * LANES] = middle_window(first, second)
-        wide_ref[rows, 2 * LANES :] = jnp.where(
-            lane < LANES - HALO, pltpu.roll(second, LANES - HALO, 1), halo_right
-        )
+    return jnp.where(has_left, jnp.where(odd, near, far), 0.0), jnp.where(has_right, jnp.where(odd, far, near), 0.0)
+
+
+def side_windows(block_ref, halos, part):
+    rows = slice(32 * part, 32 * part + 32)
+    lane = lanes_of((32, LANES))
+    left = pltpu.roll(halos[0], (-32 * part) % LANES, 1)
+    right = pltpu.roll(halos[1], (LANES - HALO - 32 * part) % LANES, 1)
+    first = jnp.where(lane < HALO, left, pltpu.roll(block_ref[rows, :LANES], HALO, 1))
+    second = jnp.where(lane < LANES - HALO, pltpu.roll(block_ref[rows, LANES:], LANES - HALO, 1), right)
+    return first, second
+
+
+def rows_kernel(block_ref, own_ref, far_ref, near_ref, _, taps_ref, two_ref, one_ref, top, low):
+    halos = side_halos(near_ref, far_ref)
+    odd = is_odd("azi")
+    has_left = lax.axis_index("azi") > 0
+    has_right = lax.axis_index("azi") < lax.axis_size("azi") - 1
     near_taps, far_taps = near_ref[33:34], far_ref[33:34]
     taps_ref[...] = own_ref[...]
     taps_ref[0:1] = jnp.where(has_left, jnp.where(odd, near_taps, far_taps), 0.0)
     taps_ref[3:4] = jnp.where(has_right, jnp.where(odd, far_taps, near_taps), 0.0)
-    top[...] = wide_ref[:HALO]
-    low[...] = wide_ref[TILE - HALO :]
+    for ref, part, rows in ((top, 0, slice(0, HALO)), (low, 3, slice(TILE - HALO, TILE))):
+        inner = slice(0, HALO) if part == 0 else slice(8, 32)
+        first, second = side_windows(block_ref, halos, part)
+        ref[:, :LANES] = first[inner]
+        ref[:, LANES : 2 * LANES] = middle_window(block_ref[rows, :LANES], block_ref[rows, LANES:])
+        ref[:, 2 * LANES :] = second[inner]
     top[REACH:, :LANES] = taps_ref[0:4]
     low[: HALO - REACH, :LANES] = taps_ref[0:4]
     odd_row = is_odd("rng")
@@ -137,9 +145,20 @@
     return both[:rows] + both[rows:] + dot(parts[0], low)
 
 
+def put_parts(field_ref, rows, value):
+    high = value.astype(jnp.bfloat16).astype(jnp.float32)
+    field_ref[0, rows] = high
+    field_ref[1, rows] = value - high
+
+
 def stacked_rows(field_ref, first, count, offsets):
-    pieces = [split(field_ref[pl.ds(HALO + first + offset, count), :]) for offset in offsets]
-    return [jnp.concatenate([piece[part] for piece in pieces], axis=1) for part in range(2)]
+    return [
+        jnp.concatenate(
+            [field_ref[part, pl.ds(HALO + first + offset, count), :].astype(jnp.bfloat16) for offset in offsets],
+            axis=1,
+        )
+        for part in range(2)
+    ]
 
 
 def adjoint_rows(field_ref, block, pair, first, count, lead):
@@ -208,25 +227,26 @@
     keep = [inside(window) for window in windows]
     for i in each:
         for stage in range(4):
-            fields[i, stage, : HALO + 8] = jnp.zeros((HALO + 8, LANES), jnp.float32)
-            fields[i, stage, HALO + TILE - 8 :] = jnp.zeros((HALO + 8, LANES), jnp.float32)
-        fields[i, 0, own] = rows[i]
+            for part in range(2):
+                fields[i, stage, part, : HALO + 8] = jnp.zeros((HALO + 8, LANES), jnp.float32)
+                fields[i, stage, part, HALO + TILE - 8 :] = jnp.zeros((HALO + 8, LANES), jnp.float32)
+        put_parts(fields.at[i, 0], own, rows[i])
     for i in each:
         main = adjoint_rows(fields.at[i, 0], blocks[i], pairs.at[i, 0], -8, MAIN, 0)
         main = jnp.where(keep[i], main, 0.0)
         outs[i][0][...] = main
-        fields[i, 1, HALO - 8 : HALO + TILE + 8] = main
+        put_parts(fields.at[i, 1], slice(HALO - 8, HALO + TILE + 8), main)
     between(0)
     for i in each:
         image = forward_rows(fields.at[i, 1], blocks[i], pairs.at[i, 1], most.start, TILE - 16)
         outs[i][1][most] = image
-        fields[i, 2, HALO + most.start : HALO + most.stop] = image
+        put_parts(fields.at[i, 2], slice(HALO + most.start, HALO + most.stop), image)
     between(1)
     for i in each:
         grad = adjoint_rows(fields.at[i, 2], blocks[i], pairs.at[i, 2], most.start, TILE - 16, 16)
         grad = jnp.where(keep[i], grad, 0.0)
         outs[i][2][most] = grad
-        fields[i, 3, HALO + most.start : HALO + most.stop] = grad
+        put_parts(fields.at[i, 3], slice(HALO + most.start, HALO + most.stop), grad)
     between(2)
     for i in each:
         outs[i][3][fewer] = forward_rows(fields.at[i, 3], blocks[i], pairs.at[i, 3], fewer.start, TILE - 32)
@@ -256,7 +276,7 @@
     early_rows([rows], (1,), [block], [outs], fields, pairs, between)
 
 
-def sides_kernel(wide_ref, taps_ref, *refs):
+def sides_kernel(block_ref, far_ref, near_ref, taps_ref, *refs):
     rest, middle = (refs[:2], refs[2:4]), refs[4:8]
     outs, refs = (refs[8:12], refs[12:16]), refs[16:]
     plain_ref, turned_ref, inner_ref, patches, fields, pairs = refs
@@ -279,7 +299,9 @@
         if stage == 1:
             turned_ref[...] = jnp.concatenate(row_weights(taps, range(4), True), axis=0)
 
-    rows = [wide_ref[:, :LANES], wide_ref[:, 2 * LANES :]]
+    halos = side_halos(near_ref, far_ref)
+    parts = [side_windows(block_ref, halos, part) for part in range(4)]
+    rows = [jnp.concatenate([part[side] for part in parts], axis=0) for side in range(2)]
     early_rows(rows, (0, 2), blocks, outs, fields, pairs, between)
     early = (outs[0], middle, outs[1])
     inner = [[window[0][8 + INNER.start : 8 + INNER.stop] for window in early]]
@@ -576,16 +598,16 @@
 
     def scratch(windows):
         return [
-            pltpu.VMEM((windows, 4, ROWS, LANES), jnp.float32),
+            pltpu.VMEM((windows, 4, 2, ROWS, LANES), jnp.float32),
             pltpu.VMEM((windows, 4, MAIN + 8, LANES), jnp.float32),
         ]
 
     *middle, high0, low0, high2, low2 = call(
         middle_kernel, early + rest, [pltpu.VMEM((DEPTH, 2 * LANES), jnp.bfloat16)] * 2 + scratch(1), limit=8
     )(block, own)
-    wide_block, taps, two, one = call(
+    taps, two, one = call(
         rows_kernel,
-        [f32(TILE, wide), f32(8, LANES), f32(HALO, wide), f32(HALO, wide)],
+        [f32(8, LANES), f32(HALO, wide), f32(HALO, wide)],
         [pltpu.VMEM((HALO, wide), jnp.float32)] * 2,
     )(block, own, far, near, middle[0])
     one_pairs, two_pairs = partners("rng", "azi")
@@ -596,7 +618,7 @@
         early * 2 + [f32(4 * COUNT, wide)] * 2 + [f32(8, LANES)],
         [pltpu.VMEM((2, 2, SLOTS * PATCH, 2 * LANES), jnp.bfloat16)] + scratch(2),
         limit=8,
-    )(wide_block, taps, high0, low0, high2, low2, *middle)
+    )(block, far, near, taps, high0, low0, high2, low2, *middle)
     *edges, record = call(
         edge_kernel,
         [f32(COUNT, wide)] * 8 + [f32(devices, 1, LANES)],

time: 27.1 us -> 27.1 us (level)
  no operation moved by 1% of the time
where the time goes in v7:
time: 27.1 us; the launch traced here: 26.9 us
  blocking collectives  11.1 us (41%)
  Pallas kernels  8.84 us (33%)
  starting transfers between devices  6.25 us (23%)
  between operations  0.68 us (3%)
    all_to_all x1, blocking collectives, body(): records = lax.all_to_all(record, BOTH, 0, 0, tiled=True)  11.1 us
    ppermute x1, starting transfers between devices, body(): far = lax.ppermute(far, BOTH, far_pairs)  3 us
    ppermute x1, starting transfers between devices, body(): one = lax.ppermute(one, BOTH, one_pairs)  2.67 us
    pallas_call x1, Pallas kernels, body(): call(sides_kernel, early * 2 + [f32(4 * COUNT, wide)] * 2 + [f32(8, LANES...  2.59 us
    pallas_call x1, Pallas kernels, body(): call(middle_kernel, early + rest, [pltpu.VMEM((DEPTH, 2 * LANES), jnp.bfl...  2.21 us
    pallas_call x1, Pallas kernels, body(): call(edge_kernel, [f32(COUNT, wide)] * 8 + [f32(devices, 1, LANES)], [plt...  1.9 us
    pallas_call x1, Pallas kernels, body(): call(combine_kernel, [f32(TILE, 2 * LANES)] * 2)  1.08 us
    pallas_call x1, Pallas kernels, body(): call(load_kernel, [f32(TILE, 2 * LANES), f32(8, LANES), f32(40, LANES), f...  0.95 us
  transfers between devices with their start and end apart: 4, of which 0 were waited for; matrix products, arithmetic and copies ran while one was open for 0% of the time, Pallas kernels for 18%

profile of v7, /device:TPU:0, one launch (start us, length us, event | category | flops | bytes accessed | tf_op | source)
XLA Modules:
  0.0 26.9 jit_solution(18065627159025462598)
XLA Ops:
  0.6 1.0 %shard_map.41 = (f32[128,256]{1,0:T(8,128)S(1)}, f32[8,128]{1,0:T(8,128)S(1)}, f32[40,128]{1,0:T(8,128)S(1)}, f32[40,128]{1,0:T(8,128)S(1)}) custom-call(f32[128,256]{1,0:T(8,128)} %observed_ref.1, f32[1,2,121]{2,1,0:T(2,128)} %psf_ref.1), custom_call_target="tpu_custom_call" | custom-call | tf_op jit(solution)/shard_map/pallas_call | solution.py:584
  1.6 3.0 %collective-permute-start = (f32[40,128]{1,0:T(8,128)S(1)}, f32[40,128]{1,0:T(8,128)S(1)}, u32[]{:S(2)}, u32[]{:S(2)}) collective-permute-start(f32[40,128]{1,0:T(8,128)S(1)} %get-tuple-element.43), channel_id=1, source_target_pairs={{0,8},{8,0},{16,24},{24,16},{1,2},{9,10},{17,18},{25,26},{2,1},{10... | collective-permute-start | bytes 61448 | tf_op jit(solution)/shard_map/ppermute | solution.py:594
  4.6 0.2 collective-permute-start.1
  4.8 2.2 %shard_map.42 = (f32[144,128]{1,0:T(8,128)S(1)}, f32[128,128]{1,0:T(8,128)S(1)}, f32[128,128]{1,0:T(8,128)S(1)}, f32[128,128]{1,0:T(8,128)S(1)}, bf16[576,256]{1...) custom-call(f32[128,256]{1,0:T(8,128)S(1)} %get-tuple-element.37.bloc, ...), custom_call_target="tpu_custom_call" | custom-call | tf_op jit(solution)/shard_map/pallas_call | solution.py:605
  7.0 0.0 collective-permute-done.far_ref
  7.0 0.0 collective-permute-done.1.near_ref
  7.0 0.1 shard_map.43
  7.1 0.4 %collective-permute-start.2 = (f32[24,384]{1,0:T(8,128)S(1)}, f32[24,384]{1,0:T(8,128)S(1)}, u32[]{:S(2)}, u32[]{:S(2)}) collective-permute-start(f32[24,384]{1,0:T(8,128)S(1)} %get-tuple-element.58), channel_id=1, source_target_pairs={{0,1},{1,0},{2,3},{3,2},{4,5},{5,4},{6,7},{7,6},{8,16},{9,17},{10,... | collective-permute-start | bytes 110600 | tf_op jit(solution)/shard_map/ppermute | solution.py:614
  7.5 2.7 %collective-permute-start.3 = (f32[24,384]{1,0:T(8,128)S(1)}, f32[24,384]{1,0:T(8,128)S(1)}, u32[]{:S(2)}, u32[]{:S(2)}) collective-permute-start(f32[24,384]{1,0:T(8,128)S(1)} %get-tuple-element.59), channel_id=1, source_target_pairs={{0,8},{1,9},{2,10},{3,11},{4,12},{5,13},{6,14},{7,15},{8,0},{9,1},... | collective-permute-start | bytes 110600 | tf_op jit(solution)/shard_map/ppermute | solution.py:615
  10.2 2.6 %shard_map.44 = (f32[144,128]{1,0:T(8,128)S(1)}, f32[128,128]{1,0:T(8,128)S(1)}, f32[128,128]{1,0:T(8,128)S(1)}, f32[128,128]{1,0:T(8,128)S(1)}, f32[144,128]{1,...) custom-call(f32[128,256]{1,0:T(8,128)S(1)} %get-tuple-element.37.blo, ...), custom_call_target="tpu_custom_call" | custom-call | tf_op jit(solution)/shard_map/pallas_call | solution.py:616
  12.8 0.0 collective-permute-done.2.refs_12_
  12.8 0.0 collective-permute-done.3.refs_13_
  12.8 1.9 %shard_map.45 = (f32[24,384]{1,0:T(8,128)S(1)}, f32[24,384]{1,0:T(8,128)S(1)}, f32[24,384]{1,0:T(8,128)S(1)}, f32[24,384]{1,0:T(8,128)S(1)}, f32[24,384]{1,0:T(8...) custom-call(f32[144,128]{1,0:T(8,128)S(1)} %get-tuple-element.39._.r, ...), custom_call_target="tpu_custom_call" | custom-call | tf_op jit(solution)/shard_map/pallas_call | solution.py:622
  14.7 11.1 %all_to_all.5.records_ref = f32[32,1,128]{2,1,0:T(1,128)S(1)} all-to-all(f32[32,1,128]{2,1,0:T(1,128)S(1)} %get-tuple-element.63), channel_id=1, replica_groups=mesh['rng'=4,'azi'=8] {'rng','azi'}, dimensions={0} | all-to-all | bytes 32768 | tf_op jit(solution)/shard_map/all_to_all | solution.py:628
  25.8 1.1 %shard_map.46 = (f32[128,256]{1,0:T(8,128)}, f32[128,256]{1,0:T(8,128)}) custom-call(f32[32,1,128]{2,1,0:T(1,128)S(1)} %all_to_all.5.records_ref, f32[128,256]{1,0:T(8,128)S(1)} %get-tuple-element.37.block_ref, f32[144,128]{1,0:T(8,128)S(1)} %get-tuple-element.39._.refs_4_.refs_0_, f32[128,128]{1,0:T(8,128)S(1)} %get-tuple-element.40.refs_5_.refs_1_, ...), custom_call_target="tpu_custom_call" | custom-call | tf_op jit(solution)/shard_map/pallas_call | solution.py:629
Async XLA Ops:
  1.6 5.4 %collective-permute-start = (f32[40,128]{1,0:T(8,128)S(1)}, f32[40,128]{1,0:T(8,128)S(1)}, u32[]{:S(2)}, u32[]{:S(2)}) collective-permute-start(f32[40,128]{1,0:T(8,128)S(1)} %get-tuple-element.43), channel_id=1, source_target_pairs={{0,8},{8,0},{16,24},{24,16},{1,2},{9,10},{17,18},{25,26},{2,1},{10... | collective-permute-start | bytes 61448 | tf_op jit(solution)/shard_map/ppermute | solution.py:594
  4.6 2.4 %collective-permute-start.1 = (f32[40,128]{1,0:T(8,128)S(1)}, f32[40,128]{1,0:T(8,128)S(1)}, u32[]{:S(2)}, u32[]{:S(2)}) collective-permute-start(f32[40,128]{1,0:T(8,128)S(1)} %get-tuple-element.44), channel_id=1, source_target_pairs={{0,1},{8,9},{16,17},{24,25},{1,0},{9,8},{17,16},{25,24},{2,3},{10,... | collective-permute-start | bytes 61448 | tf_op jit(solution)/shard_map/ppermute | solution.py:595
  7.1 5.6 %collective-permute-start.2 = (f32[24,384]{1,0:T(8,128)S(1)}, f32[24,384]{1,0:T(8,128)S(1)}, u32[]{:S(2)}, u32[]{:S(2)}) collective-permute-start(f32[24,384]{1,0:T(8,128)S(1)} %get-tuple-element.58), channel_id=1, source_target_pairs={{0,1},{1,0},{2,3},{3,2},{4,5},{5,4},{6,7},{7,6},{8,16},{9,17},{10,... | collective-permute-start | bytes 110600 | tf_op jit(solution)/shard_map/ppermute | solution.py:614
  7.5 5.3 %collective-permute-start.3 = (f32[24,384]{1,0:T(8,128)S(1)}, f32[24,384]{1,0:T(8,128)S(1)}, u32[]{:S(2)}, u32[]{:S(2)}) collective-permute-start(f32[24,384]{1,0:T(8,128)S(1)} %get-tuple-element.59), channel_id=1, source_target_pairs={{0,8},{1,9},{2,10},{3,11},{4,12},{5,13},{6,14},{7,15},{8,0},{9,1},... | collective-permute-start | bytes 110600 | tf_op jit(solution)/shard_map/ppermute | solution.py:615

commit v8 on v7

--- a/solution.py
+++ b/solution.py
@@ -339,9 +339,9 @@
 
 def forward_edge(rows, window, weights):
     before, after, bound = REGIONS[window]
-    high, low = [spread(part, -1) for part in split(rows)]
+    high, low = [spread(part, -1)[: GROUP * KSIZE] for part in split(rows)]
     both = [weights[COUNT * tile : COUNT * tile + COUNT] for tile in (before, after)]
-    result = product(split(jnp.concatenate(both, axis=0)), high, low, ((1,), (0,)))
+    result = product(split(jnp.concatenate(both, axis=0)[:, : GROUP * KSIZE]), high, low, ((1,), (0,)))
     return jnp.where(lanes_of((COUNT, LANES)) < bound, result[:COUNT], result[COUNT:])
 
 

time: 27.1 us -> 27.1 us (level)
  no operation moved by 1% of the time
where the time goes in v8:
time: 27.1 us; the launch traced here: 26.9 us
  blocking collectives  11.1 us (41%)
  Pallas kernels  8.84 us (33%)
  starting transfers between devices  6.25 us (23%)
  between operations  0.68 us (3%)
    all_to_all x1, blocking collectives, body(): records = lax.all_to_all(record, BOTH, 0, 0, tiled=True)  11.1 us
    ppermute x1, starting transfers between devices, body(): far = lax.ppermute(far, BOTH, far_pairs)  3 us
    ppermute x1, starting transfers between devices, body(): one = lax.ppermute(one, BOTH, one_pairs)  2.67 us
    pallas_call x1, Pallas kernels, body(): call(sides_kernel, early * 2 + [f32(4 * COUNT, wide)] * 2 + [f32(8, LANES...  2.59 us
    pallas_call x1, Pallas kernels, body(): call(middle_kernel, early + rest, [pltpu.VMEM((DEPTH, 2 * LANES), jnp.bfl...  2.21 us
    pallas_call x1, Pallas kernels, body(): call(edge_kernel, [f32(COUNT, wide)] * 8 + [f32(devices, 1, LANES)], [plt...  1.9 us
    pallas_call x1, Pallas kernels, body(): call(combine_kernel, [f32(TILE, 2 * LANES)] * 2)  1.08 us
    pallas_call x1, Pallas kernels, body(): call(load_kernel, [f32(TILE, 2 * LANES), f32(8, LANES), f32(40, LANES), f...  0.95 us
  transfers between devices with their start and end apart: 4, of which 0 were waited for; matrix products, arithmetic and copies ran while one was open for 0% of the time, Pallas kernels for 18%

profile of v8, /device:TPU:0, one launch (start us, length us, event | category | flops | bytes accessed | tf_op | source)
XLA Modules:
  0.0 26.9 jit_solution(8039036291797758586)
XLA Ops:
  0.6 1.0 %shard_map.41 = (f32[128,256]{1,0:T(8,128)S(1)}, f32[8,128]{1,0:T(8,128)S(1)}, f32[40,128]{1,0:T(8,128)S(1)}, f32[40,128]{1,0:T(8,128)S(1)}) custom-call(f32[128,256]{1,0:T(8,128)} %observed_ref.1, f32[1,2,121]{2,1,0:T(2,128)} %psf_ref.1), custom_call_target="tpu_custom_call" | custom-call | tf_op jit(solution)/shard_map/pallas_call | solution.py:584
  1.6 3.0 %collective-permute-start = (f32[40,128]{1,0:T(8,128)S(1)}, f32[40,128]{1,0:T(8,128)S(1)}, u32[]{:S(2)}, u32[]{:S(2)}) collective-permute-start(f32[40,128]{1,0:T(8,128)S(1)} %get-tuple-element.43), channel_id=1, source_target_pairs={{0,8},{8,0},{16,24},{24,16},{1,2},{9,10},{17,18},{25,26},{2,1},{10... | collective-permute-start | bytes 61448 | tf_op jit(solution)/shard_map/ppermute | solution.py:594
  4.6 0.2 collective-permute-start.1
  4.8 2.2 %shard_map.42 = (f32[144,128]{1,0:T(8,128)S(1)}, f32[128,128]{1,0:T(8,128)S(1)}, f32[128,128]{1,0:T(8,128)S(1)}, f32[128,128]{1,0:T(8,128)S(1)}, bf16[576,256]{1...) custom-call(f32[128,256]{1,0:T(8,128)S(1)} %get-tuple-element.37.bloc, ...), custom_call_target="tpu_custom_call" | custom-call | tf_op jit(solution)/shard_map/pallas_call | solution.py:605
  7.0 0.0 collective-permute-done.far_ref
  7.0 0.0 collective-permute-done.1.near_ref
  7.0 0.1 shard_map.43
  7.1 0.4 %collective-permute-start.2 = (f32[24,384]{1,0:T(8,128)S(1)}, f32[24,384]{1,0:T(8,128)S(1)}, u32[]{:S(2)}, u32[]{:S(2)}) collective-permute-start(f32[24,384]{1,0:T(8,128)S(1)} %get-tuple-element.58), channel_id=1, source_target_pairs={{0,1},{1,0},{2,3},{3,2},{4,5},{5,4},{6,7},{7,6},{8,16},{9,17},{10,... | collective-permute-start | bytes 110600 | tf_op jit(solution)/shard_map/ppermute | solution.py:614
  7.5 2.7 %collective-permute-start.3 = (f32[24,384]{1,0:T(8,128)S(1)}, f32[24,384]{1,0:T(8,128)S(1)}, u32[]{:S(2)}, u32[]{:S(2)}) collective-permute-start(f32[24,384]{1,0:T(8,128)S(1)} %get-tuple-element.59), channel_id=1, source_target_pairs={{0,8},{1,9},{2,10},{3,11},{4,12},{5,13},{6,14},{7,15},{8,0},{9,1},... | collective-permute-start | bytes 110600 | tf_op jit(solution)/shard_map/ppermute | solution.py:615
  10.2 2.6 %shard_map.44 = (f32[144,128]{1,0:T(8,128)S(1)}, f32[128,128]{1,0:T(8,128)S(1)}, f32[128,128]{1,0:T(8,128)S(1)}, f32[128,128]{1,0:T(8,128)S(1)}, f32[144,128]{1,...) custom-call(f32[128,256]{1,0:T(8,128)S(1)} %get-tuple-element.37.blo, ...), custom_call_target="tpu_custom_call" | custom-call | tf_op jit(solution)/shard_map/pallas_call | solution.py:616
  12.8 0.0 collective-permute-done.2.refs_12_
  12.8 0.0 collective-permute-done.3.refs_13_
  12.8 1.9 %shard_map.45 = (f32[24,384]{1,0:T(8,128)S(1)}, f32[24,384]{1,0:T(8,128)S(1)}, f32[24,384]{1,0:T(8,128)S(1)}, f32[24,384]{1,0:T(8,128)S(1)}, f32[24,384]{1,0:T(8...) custom-call(f32[144,128]{1,0:T(8,128)S(1)} %get-tuple-element.39._.r, ...), custom_call_target="tpu_custom_call" | custom-call | tf_op jit(solution)/shard_map/pallas_call | solution.py:622
  14.7 11.1 %all_to_all.5.records_ref = f32[32,1,128]{2,1,0:T(1,128)S(1)} all-to-all(f32[32,1,128]{2,1,0:T(1,128)S(1)} %get-tuple-element.63), channel_id=1, replica_groups=mesh['rng'=4,'azi'=8] {'rng','azi'}, dimensions={0} | all-to-all | bytes 32768 | tf_op jit(solution)/shard_map/all_to_all | solution.py:628
  25.8 1.1 %shard_map.46 = (f32[128,256]{1,0:T(8,128)}, f32[128,256]{1,0:T(8,128)}) custom-call(f32[32,1,128]{2,1,0:T(1,128)S(1)} %all_to_all.5.records_ref, f32[128,256]{1,0:T(8,128)S(1)} %get-tuple-element.37.block_ref, f32[144,128]{1,0:T(8,128)S(1)} %get-tuple-element.39._.refs_4_.refs_0_, f32[128,128]{1,0:T(8,128)S(1)} %get-tuple-element.40.refs_5_.refs_1_, ...), custom_call_target="tpu_custom_call" | custom-call | tf_op jit(solution)/shard_map/pallas_call | solution.py:629
Async XLA Ops:
  1.6 5.4 %collective-permute-start = (f32[40,128]{1,0:T(8,128)S(1)}, f32[40,128]{1,0:T(8,128)S(1)}, u32[]{:S(2)}, u32[]{:S(2)}) collective-permute-start(f32[40,128]{1,0:T(8,128)S(1)} %get-tuple-element.43), channel_id=1, source_target_pairs={{0,8},{8,0},{16,24},{24,16},{1,2},{9,10},{17,18},{25,26},{2,1},{10... | collective-permute-start | bytes 61448 | tf_op jit(solution)/shard_map/ppermute | solution.py:594
  4.6 2.4 %collective-permute-start.1 = (f32[40,128]{1,0:T(8,128)S(1)}, f32[40,128]{1,0:T(8,128)S(1)}, u32[]{:S(2)}, u32[]{:S(2)}) collective-permute-start(f32[40,128]{1,0:T(8,128)S(1)} %get-tuple-element.44), channel_id=1, source_target_pairs={{0,1},{8,9},{16,17},{24,25},{1,0},{9,8},{17,16},{25,24},{2,3},{10,... | collective-permute-start | bytes 61448 | tf_op jit(solution)/shard_map/ppermute | solution.py:595
  7.1 5.6 %collective-permute-start.2 = (f32[24,384]{1,0:T(8,128)S(1)}, f32[24,384]{1,0:T(8,128)S(1)}, u32[]{:S(2)}, u32[]{:S(2)}) collective-permute-start(f32[24,384]{1,0:T(8,128)S(1)} %get-tuple-element.58), channel_id=1, source_target_pairs={{0,1},{1,0},{2,3},{3,2},{4,5},{5,4},{6,7},{7,6},{8,16},{9,17},{10,... | collective-permute-start | bytes 110600 | tf_op jit(solution)/shard_map/ppermute | solution.py:614
  7.5 5.3 %collective-permute-start.3 = (f32[24,384]{1,0:T(8,128)S(1)}, f32[24,384]{1,0:T(8,128)S(1)}, u32[]{:S(2)}, u32[]{:S(2)}) collective-permute-start(f32[24,384]{1,0:T(8,128)S(1)} %get-tuple-element.59), channel_id=1, source_target_pairs={{0,8},{1,9},{2,10},{3,11},{4,12},{5,13},{6,14},{7,15},{8,0},{9,1},... | collective-permute-start | bytes 110600 | tf_op jit(solution)/shard_map/ppermute | solution.py:615

commit v9 on v8

--- a/solution.py
+++ b/solution.py
@@ -103,7 +103,7 @@
     return first, second
 
 
-def rows_kernel(block_ref, own_ref, far_ref, near_ref, _, taps_ref, two_ref, one_ref, top, low):
+def rows_kernel(own_ref, far_ref, near_ref, ends_ref, taps_ref, two_ref, one_ref, top, low):
     halos = side_halos(near_ref, far_ref)
     odd = is_odd("azi")
     has_left = lax.axis_index("azi") > 0
@@ -112,12 +112,13 @@
     taps_ref[...] = own_ref[...]
     taps_ref[0:1] = jnp.where(has_left, jnp.where(odd, near_taps, far_taps), 0.0)
     taps_ref[3:4] = jnp.where(has_right, jnp.where(odd, far_taps, near_taps), 0.0)
-    for ref, part, rows in ((top, 0, slice(0, HALO)), (low, 3, slice(TILE - HALO, TILE))):
-        inner = slice(0, HALO) if part == 0 else slice(8, 32)
-        first, second = side_windows(block_ref, halos, part)
-        ref[:, :LANES] = first[inner]
-        ref[:, LANES : 2 * LANES] = middle_window(block_ref[rows, :LANES], block_ref[rows, LANES:])
-        ref[:, 2 * LANES :] = second[inner]
+    lane = lanes_of((HALO, LANES))
+    for ref, part, inner, ends in ((top, 0, slice(0, HALO), slice(0, HALO)), (low, 3, slice(8, 32), slice(HALO, 2 * HALO))):
+        left = pltpu.roll(halos[0][inner], (-32 * part) % LANES, 1)
+        right = pltpu.roll(halos[1][inner], (LANES - HALO - 32 * part) % LANES, 1)
+        ref[:, :LANES] = jnp.where(lane < HALO, left, ends_ref[ends, :LANES])
+        ref[:, LANES : 2 * LANES] = ends_ref[ends, LANES : 2 * LANES]
+        ref[:, 2 * LANES :] = jnp.where(lane < LANES - HALO, ends_ref[ends, 2 * LANES :], right)
     top[REACH:, :LANES] = taps_ref[0:4]
     low[: HALO - REACH, :LANES] = taps_ref[0:4]
     odd_row = is_odd("rng")
@@ -258,8 +259,14 @@
 
 
 def middle_kernel(block_ref, taps_ref, *refs):
-    outs, sides = refs[:4], (refs[4:6], refs[6:8])
-    high, low, fields, pairs = refs[8:]
+    outs, sides, ends_ref = refs[:4], (refs[4:6], refs[6:8]), refs[8]
+    high, low, fields, pairs = refs[9:]
+    for side, ends in enumerate((slice(0, HALO), slice(TILE - HALO, TILE))):
+        first, second = block_ref[ends, :LANES], block_ref[ends, LANES:]
+        place = slice(HALO * side, HALO * side + HALO)
+        ends_ref[place, :LANES] = pltpu.roll(first, HALO, 1)
+        ends_ref[place, LANES : 2 * LANES] = middle_window(first, second)
+        ends_ref[place, 2 * LANES :] = pltpu.roll(second, LANES - HALO, 1)
     lines = tap_lines(taps_ref[...])
     for offset in range(2 * SLOTS):
         put_band(lines, offset, 1, 0, LANES, (high, low))
@@ -469,7 +476,7 @@
             jnp.where((lane >= low) & (lane < high), jnp.sum(piece, axis=0, keepdims=True), 0.0)
             for piece, (low, high) in zip(pieces, bounds)
         ]
-        return jnp.sum(sums[0] + sums[1] + sums[2], axis=1, keepdims=True)
+        return jnp.broadcast_to(jnp.sum(sums[0] + sums[1] + sums[2], axis=1, keepdims=True), (1, LANES))
 
     def best(first, second):
         size = total([b * b for b in second])
@@ -522,7 +529,8 @@
 
     def total(value, place):
         wanted = (lane % 8 == place) & (lane < 24)
-        return jnp.sum(jnp.where(wanted, jnp.sum(value, axis=0, keepdims=True), 0.0), axis=1, keepdims=True)
+        one = jnp.sum(jnp.where(wanted, jnp.sum(value, axis=0, keepdims=True), 0.0), axis=1, keepdims=True)
+        return jnp.broadcast_to(one, (1, LANES))
 
     gamma = total(records, 0)
     delta = total(records, 4)
@@ -571,7 +579,7 @@
         for j in range(across):
             near.append((number(i, j), number(i ^ 1, j)))
             beside = i + 1 if i % 2 else i - 1
-            far.append((number(i, j), number(beside, j) if 0 <= beside < count else number(i, j ^ 1)))
+            far.append((number(i, j), number(beside, j) if 0 <= beside < count else number(i, j ^ (1 if axis == "rng" else 2))))
     return near, far
 
 
@@ -602,14 +610,14 @@
             pltpu.VMEM((windows, 4, MAIN + 8, LANES), jnp.float32),
         ]
 
-    *middle, high0, low0, high2, low2 = call(
-        middle_kernel, early + rest, [pltpu.VMEM((DEPTH, 2 * LANES), jnp.bfloat16)] * 2 + scratch(1), limit=8
+    *middle, high0, low0, high2, low2, ends = call(
+        middle_kernel, early + rest + [f32(2 * HALO, wide)], [pltpu.VMEM((DEPTH, 2 * LANES), jnp.bfloat16)] * 2 + scratch(1), limit=8
     )(block, own)
     taps, two, one = call(
         rows_kernel,
         [f32(8, LANES), f32(HALO, wide), f32(HALO, wide)],
         [pltpu.VMEM((HALO, wide), jnp.float32)] * 2,
-    )(block, own, far, near, middle[0])
+    )(own, far, near, ends)
     one_pairs, two_pairs = partners("rng", "azi")
     two = lax.ppermute(two, BOTH, two_pairs)
     one = lax.ppermute(one, BOTH, one_pairs)

time: 27.1 us -> 27.1 us (level)
  no operation moved by 1% of the time
where the time goes in v9:
time: 27.1 us; the launch traced here: 26.9 us
  blocking collectives  11.2 us (41%)
  Pallas kernels  8.84 us (33%)
  starting transfers between devices  6.25 us (23%)
  between operations  0.67 us (2%)
    all_to_all x1, blocking collectives, body(): records = lax.all_to_all(record, BOTH, 0, 0, tiled=True)  11.2 us
    ppermute x1, starting transfers between devices, body(): far = lax.ppermute(far, BOTH, far_pairs)  3.03 us
    ppermute x1, starting transfers between devices, body(): one = lax.ppermute(one, BOTH, one_pairs)  2.65 us
    pallas_call x1, Pallas kernels, body(): call(sides_kernel, early * 2 + [f32(4 * COUNT, wide)] * 2 + [f32(8, LANES...  2.59 us
    pallas_call x1, Pallas kernels, body(): call(middle_kernel, early + rest + [f32(2 * HALO, wide)], [pltpu.VMEM((DE...  2.21 us
    pallas_call x1, Pallas kernels, body(): call(edge_kernel, [f32(COUNT, wide)] * 8 + [f32(devices, 1, LANES)], [plt...  1.9 us
    pallas_call x1, Pallas kernels, body(): call(combine_kernel, [f32(TILE, 2 * LANES)] * 2)  1.08 us
    pallas_call x1, Pallas kernels, body(): call(load_kernel, [f32(TILE, 2 * LANES), f32(8, LANES), f32(40, LANES), f...  0.95 us
  transfers between devices with their start and end apart: 4, of which 0 were waited for; matrix products, arithmetic and copies ran while one was open for 0% of the time, Pallas kernels for 18%

profile of v9, /device:TPU:0, one launch (start us, length us, event | category | flops | bytes accessed | tf_op | source)
XLA Modules:
  0.0 26.9 jit_solution(11539986536283424950)
XLA Ops:
  0.6 1.0 %shard_map.41 = (f32[128,256]{1,0:T(8,128)S(1)}, f32[8,128]{1,0:T(8,128)S(1)}, f32[40,128]{1,0:T(8,128)S(1)}, f32[40,128]{1,0:T(8,128)S(1)}) custom-call(f32[128,256]{1,0:T(8,128)} %observed_ref.1, f32[1,2,121]{2,1,0:T(2,128)} %psf_ref.1), custom_call_target="tpu_custom_call" | custom-call | tf_op jit(solution)/shard_map/pallas_call | solution.py:592
  1.6 3.0 %collective-permute-start = (f32[40,128]{1,0:T(8,128)S(1)}, f32[40,128]{1,0:T(8,128)S(1)}, u32[]{:S(2)}, u32[]{:S(2)}) collective-permute-start(f32[40,128]{1,0:T(8,128)S(1)} %get-tuple-element.44), channel_id=1, source_target_pairs={{0,16},{8,24},{16,0},{24,8},{1,2},{9,10},{17,18},{25,26},{2,1},{10... | collective-permute-start | bytes 61448 | tf_op jit(solution)/shard_map/ppermute | solution.py:602
  4.6 0.2 collective-permute-start.1
  4.8 2.2 %shard_map.42 = (f32[144,128]{1,0:T(8,128)S(1)}, f32[128,128]{1,0:T(8,128)S(1)}, f32[128,128]{1,0:T(8,128)S(1)}, f32[128,128]{1,0:T(8,128)S(1)}, bf16[576,256]{1...) custom-call(f32[128,256]{1,0:T(8,128)S(1)} %get-tuple-element.38.blo, ...), custom_call_target="tpu_custom_call" | custom-call | tf_op jit(solution)/shard_map/pallas_call | solution.py:613
  7.0 0.0 collective-permute-done.far_ref
  7.0 0.0 collective-permute-done.1.near_ref
  7.0 0.1 shard_map.43
  7.1 0.4 %collective-permute-start.2 = (f32[24,384]{1,0:T(8,128)S(1)}, f32[24,384]{1,0:T(8,128)S(1)}, u32[]{:S(2)}, u32[]{:S(2)}) collective-permute-start(f32[24,384]{1,0:T(8,128)S(1)} %get-tuple-element.60), channel_id=1, source_target_pairs={{0,1},{1,0},{2,3},{3,2},{4,5},{5,4},{6,7},{7,6},{8,16},{9,17},{10,... | collective-permute-start | bytes 110600 | tf_op jit(solution)/shard_map/ppermute | solution.py:622
  7.5 2.6 %collective-permute-start.3 = (f32[24,384]{1,0:T(8,128)S(1)}, f32[24,384]{1,0:T(8,128)S(1)}, u32[]{:S(2)}, u32[]{:S(2)}) collective-permute-start(f32[24,384]{1,0:T(8,128)S(1)} %get-tuple-element.61), channel_id=1, source_target_pairs={{0,8},{1,9},{2,10},{3,11},{4,12},{5,13},{6,14},{7,15},{8,0},{9,1},... | collective-permute-start | bytes 110600 | tf_op jit(solution)/shard_map/ppermute | solution.py:623
  10.2 2.6 %shard_map.44 = (f32[144,128]{1,0:T(8,128)S(1)}, f32[128,128]{1,0:T(8,128)S(1)}, f32[128,128]{1,0:T(8,128)S(1)}, f32[128,128]{1,0:T(8,128)S(1)}, f32[144,128]{1,...) custom-call(f32[128,256]{1,0:T(8,128)S(1)} %get-tuple-element.38.blo, ...), custom_call_target="tpu_custom_call" | custom-call | tf_op jit(solution)/shard_map/pallas_call | solution.py:624
  12.8 0.0 collective-permute-done.2.refs_12_
  12.8 0.0 collective-permute-done.3.refs_13_
  12.8 1.9 %shard_map.45 = (f32[24,384]{1,0:T(8,128)S(1)}, f32[24,384]{1,0:T(8,128)S(1)}, f32[24,384]{1,0:T(8,128)S(1)}, f32[24,384]{1,0:T(8,128)S(1)}, f32[24,384]{1,0:T(8...) custom-call(f32[144,128]{1,0:T(8,128)S(1)} %get-tuple-element.40.ref, ...), custom_call_target="tpu_custom_call" | custom-call | tf_op jit(solution)/shard_map/pallas_call | solution.py:630
  14.7 11.2 %all_to_all.5.records_ref = f32[32,1,128]{2,1,0:T(1,128)S(1)} all-to-all(f32[32,1,128]{2,1,0:T(1,128)S(1)} %get-tuple-element.65), channel_id=1, replica_groups=mesh['rng'=4,'azi'=8] {'rng','azi'}, dimensions={0} | all-to-all | bytes 32768 | tf_op jit(solution)/shard_map/all_to_all | solution.py:636
  25.9 1.1 %shard_map.46 = (f32[128,256]{1,0:T(8,128)}, f32[128,256]{1,0:T(8,128)}) custom-call(f32[32,1,128]{2,1,0:T(1,128)S(1)} %all_to_all.5.records_ref, f32[128,256]{1,0:T(8,128)S(1)} %get-tuple-element.38.block_ref, f32[144,128]{1,0:T(8,128)S(1)} %get-tuple-element.40.refs_4_.refs_0_, f32[128,128]{1,0:T(8,128)S(1)} %get-tuple-element.41.refs_5_.refs_1_, ...), custom_call_target="tpu_custom_call" | custom-call | tf_op jit(solution)/shard_map/pallas_call | solution.py:637
Async XLA Ops:
  1.6 5.4 %collective-permute-start = (f32[40,128]{1,0:T(8,128)S(1)}, f32[40,128]{1,0:T(8,128)S(1)}, u32[]{:S(2)}, u32[]{:S(2)}) collective-permute-start(f32[40,128]{1,0:T(8,128)S(1)} %get-tuple-element.44), channel_id=1, source_target_pairs={{0,16},{8,24},{16,0},{24,8},{1,2},{9,10},{17,18},{25,26},{2,1},{10... | collective-permute-start | bytes 61448 | tf_op jit(solution)/shard_map/ppermute | solution.py:602
  4.6 2.4 %collective-permute-start.1 = (f32[40,128]{1,0:T(8,128)S(1)}, f32[40,128]{1,0:T(8,128)S(1)}, u32[]{:S(2)}, u32[]{:S(2)}) collective-permute-start(f32[40,128]{1,0:T(8,128)S(1)} %get-tuple-element.45), channel_id=1, source_target_pairs={{0,1},{8,9},{16,17},{24,25},{1,0},{9,8},{17,16},{25,24},{2,3},{10,... | collective-permute-start | bytes 61448 | tf_op jit(solution)/shard_map/ppermute | solution.py:603
  7.1 5.6 %collective-permute-start.2 = (f32[24,384]{1,0:T(8,128)S(1)}, f32[24,384]{1,0:T(8,128)S(1)}, u32[]{:S(2)}, u32[]{:S(2)}) collective-permute-start(f32[24,384]{1,0:T(8,128)S(1)} %get-tuple-element.60), channel_id=1, source_target_pairs={{0,1},{1,0},{2,3},{3,2},{4,5},{5,4},{6,7},{7,6},{8,16},{9,17},{10,... | collective-permute-start | bytes 110600 | tf_op jit(solution)/shard_map/ppermute | solution.py:622
  7.5 5.2 %collective-permute-start.3 = (f32[24,384]{1,0:T(8,128)S(1)}, f32[24,384]{1,0:T(8,128)S(1)}, u32[]{:S(2)}, u32[]{:S(2)}) collective-permute-start(f32[24,384]{1,0:T(8,128)S(1)} %get-tuple-element.61), channel_id=1, source_target_pairs={{0,8},{1,9},{2,10},{3,11},{4,12},{5,13},{6,14},{7,15},{8,0},{9,1},... | collective-permute-start | bytes 110600 | tf_op jit(solution)/shard_map/ppermute | solution.py:623

commit v10 on v8

--- a/solution.py
+++ b/solution.py
@@ -411,12 +411,15 @@
         result = adjoint_edge(edge[strip, cols(window)], window, turned)
         field[spot(0), :] += jnp.where(in_image(0, window), result[:EDGE], 0.0)
         outs[0][:, cols(window)] = field[out]
-
-    yield
+        yield
+
     out_row = lax.broadcasted_iota(jnp.int32, (4 * COUNT, wide), 0) % COUNT
     mixed = (plain, plain_ref[...]) if side == 0 else (plain_ref[...], plain)
     mixed = jnp.where(out_row < half, *mixed)
-    results = [forward_edge(fields[0, window, spot(1, RADIUS, GROUP), :], window, mixed) for window in each]
+    results = []
+    for window in each:
+        results.append(forward_edge(fields[0, window, spot(1, RADIUS, GROUP), :], window, mixed))
+        yield
     for window in each:
         field = fields.at[1, window]
         if side == 0:
@@ -427,7 +430,6 @@
         field[spot(1), :] = results[window][:EDGE]
         outs[1][:, cols(window)] = field[out]
 
-    yield
     in_row = lanes_of((4 * COUNT, wide)) % GROUP
     if side == 0:
         mixed = jnp.where(in_row < half, turned, turned_ref[...])
@@ -443,9 +445,12 @@
         field[near] = early[window][2][own]
         field[spot(2), :] = jnp.where(in_image(2, window), result[:EDGE], 0.0)
         outs[2][:, cols(window)] = field[out]
-
-    yield
-    results = [forward_edge(fields[2, window, spot(3, RADIUS, GROUP), :], window, plain_ref[...]) for window in each]
+        yield
+
+    results = []
+    for window in each:
+        results.append(forward_edge(fields[2, window, spot(3, RADIUS, GROUP), :], window, plain_ref[...]))
+        yield
     for window in each:
         rest = COUNT - EDGE
         if side == 0:

time: 27.1 us -> 27 us (level)
  no operation moved by 1% of the time
where the time goes in v10:
time: 27 us; the launch traced here: 26.8 us
  blocking collectives  11.1 us (41%)
  Pallas kernels  8.83 us (33%)
  starting transfers between devices  6.25 us (23%)
  between operations  0.68 us (3%)
    all_to_all x1, blocking collectives, body(): records = lax.all_to_all(record, BOTH, 0, 0, tiled=True)  11.1 us
    ppermute x1, starting transfers between devices, body(): far = lax.ppermute(far, BOTH, far_pairs)  3 us
    ppermute x1, starting transfers between devices, body(): one = lax.ppermute(one, BOTH, one_pairs)  2.67 us
    pallas_call x1, Pallas kernels, body(): call(sides_kernel, early * 2 + [f32(4 * COUNT, wide)] * 2 + [f32(8, LANES...  2.59 us
    pallas_call x1, Pallas kernels, body(): call(middle_kernel, early + rest, [pltpu.VMEM((DEPTH, 2 * LANES), jnp.bfl...  2.21 us
    pallas_call x1, Pallas kernels, body(): call(edge_kernel, [f32(COUNT, wide)] * 8 + [f32(devices, 1, LANES)], [plt...  1.89 us
    pallas_call x1, Pallas kernels, body(): call(combine_kernel, [f32(TILE, 2 * LANES)] * 2)  1.08 us
    pallas_call x1, Pallas kernels, body(): call(load_kernel, [f32(TILE, 2 * LANES), f32(8, LANES), f32(40, LANES), f...  0.95 us
  transfers between devices with their start and end apart: 4, of which 0 were waited for; matrix products, arithmetic and copies ran while one was open for 0% of the time, Pallas kernels for 18%

profile of v10, /device:TPU:0, one launch (start us, length us, event | category | flops | bytes accessed | tf_op | source)
XLA Modules:
  0.0 26.8 jit_solution(6985570593877793286)
XLA Ops:
  0.6 1.0 %shard_map.41 = (f32[128,256]{1,0:T(8,128)S(1)}, f32[8,128]{1,0:T(8,128)S(1)}, f32[40,128]{1,0:T(8,128)S(1)}, f32[40,128]{1,0:T(8,128)S(1)}) custom-call(f32[128,256]{1,0:T(8,128)} %observed_ref.1, f32[1,2,121]{2,1,0:T(2,128)} %psf_ref.1), custom_call_target="tpu_custom_call" | custom-call | tf_op jit(solution)/shard_map/pallas_call | solution.py:589
  1.6 3.0 %collective-permute-start = (f32[40,128]{1,0:T(8,128)S(1)}, f32[40,128]{1,0:T(8,128)S(1)}, u32[]{:S(2)}, u32[]{:S(2)}) collective-permute-start(f32[40,128]{1,0:T(8,128)S(1)} %get-tuple-element.43), channel_id=1, source_target_pairs={{0,8},{8,0},{16,24},{24,16},{1,2},{9,10},{17,18},{25,26},{2,1},{10... | collective-permute-start | bytes 61448 | tf_op jit(solution)/shard_map/ppermute | solution.py:599
  4.6 0.2 collective-permute-start.1
  4.8 2.2 %shard_map.42 = (f32[144,128]{1,0:T(8,128)S(1)}, f32[128,128]{1,0:T(8,128)S(1)}, f32[128,128]{1,0:T(8,128)S(1)}, f32[128,128]{1,0:T(8,128)S(1)}, bf16[576,256]{1...) custom-call(f32[128,256]{1,0:T(8,128)S(1)} %get-tuple-element.37.bloc, ...), custom_call_target="tpu_custom_call" | custom-call | tf_op jit(solution)/shard_map/pallas_call | solution.py:610
  7.0 0.0 collective-permute-done.far_ref
  7.0 0.0 collective-permute-done.1.near_ref
  7.0 0.1 shard_map.43
  7.1 0.4 %collective-permute-start.2 = (f32[24,384]{1,0:T(8,128)S(1)}, f32[24,384]{1,0:T(8,128)S(1)}, u32[]{:S(2)}, u32[]{:S(2)}) collective-permute-start(f32[24,384]{1,0:T(8,128)S(1)} %get-tuple-element.58), channel_id=1, source_target_pairs={{0,1},{1,0},{2,3},{3,2},{4,5},{5,4},{6,7},{7,6},{8,16},{9,17},{10,... | collective-permute-start | bytes 110600 | tf_op jit(solution)/shard_map/ppermute | solution.py:619
  7.5 2.7 %collective-permute-start.3 = (f32[24,384]{1,0:T(8,128)S(1)}, f32[24,384]{1,0:T(8,128)S(1)}, u32[]{:S(2)}, u32[]{:S(2)}) collective-permute-start(f32[24,384]{1,0:T(8,128)S(1)} %get-tuple-element.59), channel_id=1, source_target_pairs={{0,8},{1,9},{2,10},{3,11},{4,12},{5,13},{6,14},{7,15},{8,0},{9,1},... | collective-permute-start | bytes 110600 | tf_op jit(solution)/shard_map/ppermute | solution.py:620
  10.2 2.6 %shard_map.44 = (f32[144,128]{1,0:T(8,128)S(1)}, f32[128,128]{1,0:T(8,128)S(1)}, f32[128,128]{1,0:T(8,128)S(1)}, f32[128,128]{1,0:T(8,128)S(1)}, f32[144,128]{1,...) custom-call(f32[128,256]{1,0:T(8,128)S(1)} %get-tuple-element.37.blo, ...), custom_call_target="tpu_custom_call" | custom-call | tf_op jit(solution)/shard_map/pallas_call | solution.py:621
  12.8 0.0 collective-permute-done.2.refs_12_
  12.8 0.0 collective-permute-done.3.refs_13_
  12.8 1.9 %shard_map.45 = (f32[24,384]{1,0:T(8,128)S(1)}, f32[24,384]{1,0:T(8,128)S(1)}, f32[24,384]{1,0:T(8,128)S(1)}, f32[24,384]{1,0:T(8,128)S(1)}, f32[24,384]{1,0:T(8...) custom-call(f32[144,128]{1,0:T(8,128)S(1)} %get-tuple-element.39._.r, ...), custom_call_target="tpu_custom_call" | custom-call | tf_op jit(solution)/shard_map/pallas_call | solution.py:627
  14.7 11.1 %all_to_all.5.records_ref = f32[32,1,128]{2,1,0:T(1,128)S(1)} all-to-all(f32[32,1,128]{2,1,0:T(1,128)S(1)} %get-tuple-element.63), channel_id=1, replica_groups=mesh['rng'=4,'azi'=8] {'rng','azi'}, dimensions={0} | all-to-all | bytes 32768 | tf_op jit(solution)/shard_map/all_to_all | solution.py:633
  25.8 1.1 %shard_map.46 = (f32[128,256]{1,0:T(8,128)}, f32[128,256]{1,0:T(8,128)}) custom-call(f32[32,1,128]{2,1,0:T(1,128)S(1)} %all_to_all.5.records_ref, f32[128,256]{1,0:T(8,128)S(1)} %get-tuple-element.37.block_ref, f32[144,128]{1,0:T(8,128)S(1)} %get-tuple-element.39._.refs_4_.refs_0_, f32[128,128]{1,0:T(8,128)S(1)} %get-tuple-element.40.refs_5_.refs_1_, ...), custom_call_target="tpu_custom_call" | custom-call | tf_op jit(solution)/shard_map/pallas_call | solution.py:634
Async XLA Ops:
  1.6 5.4 %collective-permute-start = (f32[40,128]{1,0:T(8,128)S(1)}, f32[40,128]{1,0:T(8,128)S(1)}, u32[]{:S(2)}, u32[]{:S(2)}) collective-permute-start(f32[40,128]{1,0:T(8,128)S(1)} %get-tuple-element.43), channel_id=1, source_target_pairs={{0,8},{8,0},{16,24},{24,16},{1,2},{9,10},{17,18},{25,26},{2,1},{10... | collective-permute-start | bytes 61448 | tf_op jit(solution)/shard_map/ppermute | solution.py:599
  4.6 2.4 %collective-permute-start.1 = (f32[40,128]{1,0:T(8,128)S(1)}, f32[40,128]{1,0:T(8,128)S(1)}, u32[]{:S(2)}, u32[]{:S(2)}) collective-permute-start(f32[40,128]{1,0:T(8,128)S(1)} %get-tuple-element.44), channel_id=1, source_target_pairs={{0,1},{8,9},{16,17},{24,25},{1,0},{9,8},{17,16},{25,24},{2,3},{10,... | collective-permute-start | bytes 61448 | tf_op jit(solution)/shard_map/ppermute | solution.py:600
  7.1 5.6 %collective-permute-start.2 = (f32[24,384]{1,0:T(8,128)S(1)}, f32[24,384]{1,0:T(8,128)S(1)}, u32[]{:S(2)}, u32[]{:S(2)}) collective-permute-start(f32[24,384]{1,0:T(8,128)S(1)} %get-tuple-element.58), channel_id=1, source_target_pairs={{0,1},{1,0},{2,3},{3,2},{4,5},{5,4},{6,7},{7,6},{8,16},{9,17},{10,... | collective-permute-start | bytes 110600 | tf_op jit(solution)/shard_map/ppermute | solution.py:619
  7.5 5.3 %collective-permute-start.3 = (f32[24,384]{1,0:T(8,128)S(1)}, f32[24,384]{1,0:T(8,128)S(1)}, u32[]{:S(2)}, u32[]{:S(2)}) collective-permute-start(f32[24,384]{1,0:T(8,128)S(1)} %get-tuple-element.59), channel_id=1, source_target_pairs={{0,8},{1,9},{2,10},{3,11},{4,12},{5,13},{6,14},{7,15},{8,0},{9,1},... | collective-permute-start | bytes 110600 | tf_op jit(solution)/shard_map/ppermute | solution.py:620
